TPU v7x, 256 devices: a whole 4x4x8 slice. The times are simulated.
256 devices in a mesh: row: 8 (over x, core), col: 32 (over y, z).
Axes of the slice: x: 4, y: 4, z: 8, core: 2. Of those that a mesh axis runs over, the one named last changes fastest.
Arguments:
- src_points: bfloat16 [64, 32768], P(None, ('row', 'col')), may hold values from -6 to 6
- tgt_points: bfloat16 [64, 32768], P(None, ('col', 'row')), may hold values from -6 to 6
- src_dual: float32 [32768], P('row'), may hold values from 0.8 to 1.2
- tgt_dual: float32 [32768], P('col'), may hold values from 0.8 to 1.2
- src_cot: float32 [32768], P('row'), may hold values from -2.5 to 6.5
- tgt_cot: float32 [32768], P('col'), may hold values from -2.5 to 6.5
Outputs:
- src_grad: float32 [64, 32768], P(None, ('row', 'col'))
- tgt_grad: float32 [64, 32768], P(None, ('col', 'row'))
All inputs are finite; a program needn't handle non-finite values.
Results may differ from a plain program's by a relative error of at most 0.00045.
Values may be sent and summed in bfloat16 or wider, within the bound.
No kernel may reach another device: no remote copies, remote signals or barrier semaphores. Data moves between devices by JAX's collectives and lax.ppermute only.
A program may use at most 64 MiB of HBM per device.

v0:
```python
import jax
import jax.numpy as jnp
from jax import lax
from jax.sharding import PartitionSpec as P

blur_scale = 0.25
ridge_shift = 0.5


def reduce_rows(term):
    return lax.psum(term, "col")


def reduce_cols(term):
    return lax.psum(term, "row")


def body(src_points, tgt_points, src_dual, tgt_dual, src_cot, tgt_cot):
    col_count = lax.axis_size("col")
    row_count = lax.axis_size("row")
    src_block = lax.all_gather(src_points, "col", axis=1, tiled=True)
    tgt_block = lax.all_gather(tgt_points, "row", axis=1, tiled=True)
    width = src_block.shape[0]
    src_rows = src_block.shape[1]
    tgt_cols = tgt_block.shape[1]
    total = tgt_cols * col_count
    src_wide = src_block.astype(jnp.float32)
    tgt_wide = tgt_block.astype(jnp.float32)
    src_norm = jnp.sum(src_wide * src_wide, axis=0)
    tgt_norm = jnp.sum(tgt_wide * tgt_wide, axis=0)
    step_rows = min(512, src_rows)
    blocks = src_rows // step_rows
    src_tiles = src_block.reshape(width, blocks, step_rows).transpose(1, 0, 2)
    wide_tiles = src_wide.reshape(width, blocks, step_rows).transpose(1, 0, 2)
    norm_tiles = src_norm.reshape(blocks, step_rows)
    dual_tiles = src_dual.reshape(blocks, step_rows)
    row_share = src_rows // col_count
    col_share = tgt_cols // row_count

    def plan_tile(piece, norms, duals):
        dots = lax.dot_general(
            piece, tgt_block, (((0,), (0,)), ((), ())), preferred_element_type=jnp.float32
        )
        cost = (norms[:, None] + tgt_norm[None, :] - 2.0 * dots) / width
        return jnp.exp((duals[:, None] + tgt_dual[None, :] - cost) / blur_scale) / total

    def sweep(row_vec, col_vec, with_mass):
        vec_tiles = row_vec.reshape(blocks, step_rows)

        def visit(carry, inputs):
            piece, norms, duals, weights = inputs
            plan = plan_tile(piece, norms, duals)
            pushed = jnp.sum(plan * col_vec[None, :], axis=1)
            pulled = carry[1] + jnp.sum(plan * weights[:, None], axis=0)
            if with_mass:
                return (
                    (carry[0] + jnp.sum(plan, axis=0), pulled),
                    jnp.stack([jnp.sum(plan, axis=1), pushed]),
                )
            return ((carry[0], pulled), pushed[None, :])

        zero = jnp.zeros((tgt_cols,), jnp.float32)
        (mass_c, pulled), row_out = lax.scan(
            visit, (zero, zero), (src_tiles, norm_tiles, dual_tiles, vec_tiles)
        )
        row_terms = row_out.transpose(1, 0, 2).reshape(row_out.shape[1], src_rows)
        if with_mass:
            col_terms = jnp.stack([mass_c, pulled])
        else:
            col_terms = pulled[None, :]
        return (row_terms, col_terms)

    row_weight = 1.0 / col_count
    col_weight = 1.0 / row_count

    def inner(pairs):
        local = jnp.stack(
            [
                jnp.sum(first * second) * row_weight + jnp.sum(third * fourth) * col_weight
                for first, second, third, fourth in pairs
            ]
        )
        return lax.psum(local, ("row", "col"))

    start_norm = inner([(src_cot, src_cot, tgt_cot, tgt_cot)])[0]
    row_terms, col_terms = sweep(src_cot, tgt_cot, True)
    row_terms = reduce_rows(row_terms)
    col_terms = reduce_cols(col_terms)
    row_mass = row_terms[0] + ridge_shift
    col_mass = col_terms[0] + ridge_shift
    row_image = row_mass * src_cot + row_terms[1]
    col_image = col_mass * tgt_cot + col_terms[1]
    curve = inner([(src_cot, row_image, tgt_cot, col_image)])[0]
    alpha = start_norm / curve
    row_sol = alpha * src_cot
    col_sol = alpha * tgt_cot
    row_res = src_cot - alpha * row_image
    col_res = tgt_cot - alpha * col_image
    next_norm = inner([(row_res, row_res, col_res, col_res)])[0]
    ratio = next_norm / start_norm
    row_dir = row_res + ratio * src_cot
    col_dir = col_res + ratio * tgt_cot
    row_terms, col_terms = sweep(row_dir, col_dir, False)
    row_image = row_mass * row_dir + reduce_rows(row_terms)[0]
    col_image = col_mass * col_dir + reduce_cols(col_terms)[0]
    alpha = next_norm / inner([(row_dir, row_image, col_dir, col_image)])[0]
    row_sol = row_sol + alpha * row_dir
    col_sol = col_sol + alpha * col_dir
    full_col = col_sol
    sol_tiles = row_sol.reshape(blocks, step_rows)
    scale = 2.0 / (blur_scale * width)

    def visit_grad(carry, inputs):
        piece, wide, norms, duals, weights = inputs
        plan = plan_tile(piece, norms, duals)
        mixed = plan * (weights[:, None] + full_col[None, :])
        toward = lax.dot_general(
            tgt_wide, mixed, (((1,), (1,)), ((), ())), precision=lax.Precision.HIGHEST
        )
        row_grad = wide * jnp.sum(mixed, axis=1)[None, :] - toward
        back = jnp.dot(wide, mixed, precision=lax.Precision.HIGHEST)
        col_grad = tgt_wide * jnp.sum(mixed, axis=0)[None, :] - back
        return (carry + scale * col_grad, scale * row_grad)

    col_total, row_out = lax.scan(
        visit_grad,
        jnp.zeros((width, tgt_cols), jnp.float32),
        (src_tiles, wide_tiles, norm_tiles, dual_tiles, sol_tiles),
    )
    row_term = row_out.transpose(1, 0, 2).reshape(width, src_rows)
    src_grad = reduce_rows(row_term)
    tgt_grad = reduce_cols(col_total)
    src_grad = lax.dynamic_slice_in_dim(src_grad, lax.axis_index("col") * row_share, row_share, 1)
    tgt_grad = lax.dynamic_slice_in_dim(tgt_grad, lax.axis_index("row") * col_share, col_share, 1)
    return (src_grad, tgt_grad)


def solution(mesh):
    in_specs = (
        P(None, ("row", "col")),
        P(None, ("col", "row")),
        P("row"),
        P("col"),
        P("row"),
        P("col"),
    )
    out_specs = (P(None, ("row", "col")), P(None, ("col", "row")))
    return jax.shard_map(body, mesh=mesh, in_specs=in_specs, out_specs=out_specs, check_vma=False)
```

profile of v0, /device:TPU:1, one launch (start us, length us, event | category | flops | bytes accessed | tf_op | source)
XLA Modules:
  0.0 916.4 jit_solution(12477700825398217710)
XLA Ops:
  8.0 43.0 %all_gather.6 = bf16[64,4096]{1,0:T(8,128)(2,1)S(1)} all-gather(bf16[64,128]{1,0:T(8,128)(2,1)} %param.12), channel_id=1, replica_groups=mesh['row'=8,'col'=32] {'col'}, dimensions={1}, use_global_device_ids=true | all-gather | bytes 540672 | tf_op jit(solution)/shard_map/all_gather | solution.py:21
  51.1 24.2 %all_gather.7 = bf16[64,1024]{1,0:T(8,128)(2,1)S(1)} all-gather(bf16[64,128]{1,0:T(8,128)(2,1)} %param.13), channel_id=1, replica_groups=mesh['row'=8,'col'=32] {'row'}, dimensions={1}, use_global_device_ids=true | all-gather | bytes 147456 | tf_op jit(solution)/shard_map/all_gather | solution.py:22
  75.8 12.3 %while.41 = (s32[]{:T(128)}, f32[1024]{0:T(1024)S(1)}, f32[1024]{0:T(1024)S(1)}, f32[8,2,512]{2,1,0:T(2,128)S(1)}, f32[8,512]{1,0:T(8,128)S(1)}, /*index=5*/f32[...) while((s32[]{:T(128)}, f32[1024]{0:T(1024)S(1)}, ...), condition=%wide.region_10.11_spmd.clone, body=%wide.region_5.10_spmd.clone.sunk | while | flops 74452480 | bytes 280747 | solution.py:63
  75.8 1.4 multiply_reduce_fusion.18
  77.4 1.4 multiply_reduce_fusion.18
  78.9 1.4 multiply_reduce_fusion.18
  80.4 1.4 multiply_reduce_fusion.18
  82.0 1.4 multiply_reduce_fusion.18
  83.5 1.4 multiply_reduce_fusion.18
  85.0 1.4 multiply_reduce_fusion.18
  86.6 1.4 multiply_reduce_fusion.18
  88.0 112.8 %psum.71 = f32[2,4096]{1,0:T(2,128)S(1)} all-reduce(f32[2,4096]{1,0:T(2,128)S(1)} %bitcast.171), channel_id=1, replica_groups=mesh['row'=8,'col'=32] {'col'}, use_global_device_ids=true, to_apply=%region_11.12 | all-reduce | flops 8192 | bytes 65536 | tf_op jit(solution)/shard_map/psum | solution.py:11
  200.9 39.7 %psum.72 = f32[2,1024]{1,0:T(2,128)S(1)} all-reduce(f32[2,1024]{1,0:T(2,128)S(1)} %pad_maximum_fusion), channel_id=1, replica_groups=mesh['row'=8,'col'=32] {'row'}, use_global_device_ids=true, to_apply=%region_13.14 | all-reduce | flops 2048 | bytes 16384 | tf_op jit(solution)/shard_map/psum | solution.py:15
  244.7 73.7 %all-reduce = (f32[1]{0:T(128)}, f32[1]{0:T(128)}) all-reduce(f32[1]{0:T(128)} %bitcast.1, f32[1]{0:T(128)} %bitcast.10), channel_id=1, replica_groups=mesh['row'=8,'col'=32] {'row','col'}, use_global_device_ids=true, to_apply=%region_3.0 | all-reduce | flops 2 | bytes 16 | tf_op jit(solution)/shard_map/psum | solution.py:83
  322.1 74.0 %psum.74 = f32[1]{0:T(128)} all-reduce(f32[1]{0:T(128)} %bitcast.12), channel_id=1, replica_groups=mesh['row'=8,'col'=32] {'row','col'}, use_global_device_ids=true, to_apply=%region_18.19 | all-reduce | flops 1 | bytes 8 | tf_op jit(solution)/shard_map/psum | solution.py:83
  397.4 10.1 %while.42 = (s32[]{:T(128)}, f32[1024]{0:T(1024)S(1)}, f32[8,1,512]{2,1,0:T(1,128)S(1)}, f32[8,512]{1,0:T(8,128)S(1)}, f32[1024]{0:T(1024)S(1)}, /*index=5*/f32[...) while((s32[]{:T(128)}, f32[1024]{0:T(1024)S(1)}, ...), condition=%wide.region_22.23_spmd.clone, body=%wide.region_19.22_spmd.clone.sunk | while | flops 72878080 | bytes 258207 | solution.py:63
  397.5 1.2 multiply_reduce_fusion.19
  398.8 1.2 multiply_reduce_fusion.19
  400.0 1.2 multiply_reduce_fusion.19
  401.3 1.2 multiply_reduce_fusion.19
  402.6 1.2 multiply_reduce_fusion.19
  405.1 1.2 multiply_reduce_fusion.19
  407.6 112.5 %psum.75 = f32[4096]{0:T(1024)S(1)} all-reduce(f32[4096]{0:T(1024)S(1)} %bitcast.172), channel_id=1, replica_groups=mesh['row'=8,'col'=32] {'col'}, use_global_device_ids=true, to_apply=%region_23.24 | all-reduce | flops 4096 | bytes 32768 | tf_op jit(solution)/shard_map/psum | solution.py:11
  521.3 40.3 %psum.76 = f32[1024]{0:T(1024)S(1)} all-reduce(f32[1024]{0:T(1024)S(1)} %get-tuple-element.196), channel_id=1, replica_groups=mesh['row'=8,'col'=32] {'row'}, use_global_device_ids=true, to_apply=%region_25.26 | all-reduce | flops 1024 | bytes 8192 | tf_op jit(solution)/shard_map/psum | solution.py:15
  562.8 73.3 %psum.77 = f32[1]{0:T(128)} all-reduce(f32[1]{0:T(128)} %bitcast.15), channel_id=1, replica_groups=mesh['row'=8,'col'=32] {'row','col'}, use_global_device_ids=true, to_apply=%region_27.28 | all-reduce | flops 1 | bytes 8 | tf_op jit(solution)/shard_map/psum | solution.py:83
  637.5 1.2 copy.17
  638.8 61.6 %while.43 = (s32[]{:T(128)}, f32[64,1024]{1,0:T(8,128)S(1)}, f32[8,64,512]{2,1,0:T(8,128)}, f32[8,512]{1,0:T(8,128)S(1)}, f32[1024]{0:T(1024)S(1)}, /*index=5*/f...) while((s32[]{:T(128)}, f32[64,1024]{1,0:T(8,128)S(1)}, ...), condition=%wide.region_31.32_spmd.clone, body=%wide.region_28.31_spmd.clone.sunk | while | flops 879131136 | bytes 8235187 | solution.py:125
  638.8 2.1 fusion.40
  640.9 1.3 constant_dynamic-slice_fusion.21
  642.2 1.4 fusion.41
  643.6 2.8 fusion.42
  646.5 2.1 fusion.40
  648.6 1.3 constant_dynamic-slice_fusion.21
  649.9 1.4 fusion.41
  651.3 2.8 fusion.42
  654.2 2.1 fusion.40
  656.3 1.3 constant_dynamic-slice_fusion.21
  657.6 1.4 fusion.41
  659.0 2.8 fusion.42
  661.9 2.1 fusion.40
  664.0 1.3 constant_dynamic-slice_fusion.21
  665.3 1.4 fusion.41
  666.7 2.8 fusion.42
  669.6 2.1 fusion.40
  671.7 1.3 constant_dynamic-slice_fusion.21
  673.0 1.4 fusion.41
  674.4 2.8 fusion.42
  677.3 2.1 fusion.40
  679.4 1.3 constant_dynamic-slice_fusion.21
  680.7 1.4 fusion.41
  682.1 2.8 fusion.42
  684.9 2.1 fusion.40
  687.1 1.3 constant_dynamic-slice_fusion.21
  688.4 1.4 fusion.41
  689.8 2.8 fusion.42
  692.6 2.1 fusion.40
  694.8 1.3 constant_dynamic-slice_fusion.21
  696.1 1.4 fusion.41
  697.5 2.8 fusion.42
  701.1 2.4 copy.15
  703.5 54.7 %all-reduce.6.cloned.1.call-done = f32[64,1024]{1,0:T(8,128)} async-done(((f32[64,1024]{1,0:T(8,128)}), f32[64,1024]{1,0:T(8,128)}) %all-reduce.6.cloned.1.call-update) | async-done | bytes 262160 | tf_op jit(solution)/shard_map/psum | solution.py:15
  758.2 1.4 constant_dynamic-slice_fusion.8
  759.6 148.6 %all-reduce.4.cloned.1.call-done = f32[64,4096]{1,0:T(8,128)} async-done(((f32[64,4096]{1,0:T(8,128)}), f32[64,4096]{1,0:T(8,128)}) %all-reduce.4.cloned.1.call-update) | async-done | bytes 1048592 | tf_op jit(solution)/shard_map/psum | solution.py:11
  908.2 1.4 constant_dynamic-slice_fusion.9
  (150 shorter events, 9.4 us)
Async XLA Ops:
  7.2 68.6 %copy-start.2 = (f32[4096]{0:T(1024)S(1)}, f32[4096]{0:T(1024)}, u32[]{:S(2)}) copy-start(f32[4096]{0:T(1024)} %param.16) | copy-start | bytes 49156
  7.2 68.6 %copy-start.4 = (f32[1024]{0:T(1024)S(1)}, f32[1024]{0:T(1024)}, u32[]{:S(2)}) copy-start(f32[1024]{0:T(1024)} %param.15) | copy-start | bytes 12292
  7.2 68.6 %copy-start.3 = (f32[1024]{0:T(1024)S(1)}, f32[1024]{0:T(1024)}, u32[]{:S(2)}) copy-start(f32[1024]{0:T(1024)} %param.17) | copy-start | bytes 12292
  7.2 751.0 %all-reduce.6.cloned.1.call-start = ((), (), s32[]{:S(2)}) async-start(), calls=%async_computation.1 | async-start | bytes 524288 | tf_op jit(solution)/shard_map/psum | solution.py:15
  407.6 229.9 %copy-start.1 = (bf16[8,64,512]{2,1,0:T(8,128)(2,1)}, bf16[8,64,512]{2,1,0:T(8,128)(2,1)S(1)}, u32[]{:S(2)}) copy-start(bf16[8,64,512]{2,1,0:T(8,128)(2,1)S(1)} %get-tuple-element.833) | copy-start | bytes 1572868
  700.3 0.7 copy-start
  701.0 207.1 %all-reduce.4.cloned.1.call-start = ((), (), s32[]{:S(2)}) async-start(), calls=%async_computation | async-start | bytes 2097152 | tf_op jit(solution)/shard_map/psum | solution.py:11
Sparse Core Ops, SparseCore 0:
  701.2 56.9 all-reduce.5
  762.0 146.0 all-reduce.3
where the time goes:
time: 922 us; the launch traced here: 916 us
  blocking collectives  593 us (64%)
  waiting for transfers between devices  203 us (22%)
  matrix products  71.2 us (8%)
  between operations  23.4 us (3%)
  local copies, waits for them, and re-layouts  19.3 us (2%)
    psum x2, blocking collectives, reduce_rows(): return lax.psum(term, 'col')  225 us
    psum x3, blocking collectives, inner(): return lax.psum(local, ('row', 'col'))  221 us
    psum x1, waiting for transfers between devices, reduce_rows(): return lax.psum(term, 'col')  149 us
    psum x2, blocking collectives, reduce_cols(): return lax.psum(term, 'row')  80 us
    psum x1, waiting for transfers between devices, reduce_cols(): return lax.psum(term, 'row')  54.7 us
    all_gather x1, blocking collectives, body(): src_block = lax.all_gather(src_points, 'col', axis=1, tiled=True)  43 us
    dot_general x24, matrix products, plan_tile(): lax.dot_general(piece, tgt_block, (((0,), (0,)), ((), ())), preferred_ele...  37.6 us
    all_gather x1, blocking collectives, body(): tgt_block = lax.all_gather(tgt_points, 'row', axis=1, tiled=True)  24.2 us
  transfers between devices with their start and end apart: 2, of which 2 were waited for; matrix products, arithmetic and copies ran while one was open for 0% of the time, Pallas kernels for 0%

commit v1 on v0

v1 whole, which is shorter than its diff:
```python
import jax
import jax.numpy as jnp
import numpy as np
from jax import lax
from jax.experimental import pallas as pl
from jax.experimental.pallas import tpu as pltpu
from jax.sharding import Mesh, PartitionSpec as P

blur_scale = 0.25
ridge_shift = 0.5
D = 64
L = 128
KP = 80
SA = ("x", "y")
TA = ("c", "z")
NA = 16
NB = 16
ROWS = NA * L
COLS = NB * L
STEP = 4
BLK = STEP * L
MA = 208
PR = 144
LOG2E = 1.4426950408889634
GAIN = 2.0 * LOG2E / (blur_scale * D)
SHIFT = 15.0 / GAIN
f32 = jnp.float32
bf16 = jnp.bfloat16
HI = lax.Precision.HIGHEST
VMEM = 56 * 1024 * 1024


def split3(v):
    hi = v.astype(bf16)
    rest = v - hi.astype(f32)
    mid = rest.astype(bf16)
    low = (rest - mid.astype(f32)).astype(bf16)
    return hi, mid, low


def join3(block, at):
    return (
        block[at : at + 1].astype(f32)
        + block[at + 1 : at + 2].astype(f32)
        + block[at + 2 : at + 3].astype(f32)
    )


def call(kernel, out_shape, **kw):
    return pl.pallas_call(
        kernel,
        out_shape=out_shape,
        compiler_params=pltpu.CompilerParams(vmem_limit_bytes=VMEM),
        **kw,
    )


def sds(shape, dtype):
    return jax.ShapeDtypeStruct(shape, dtype)


def pack_kernel(src_ref, tgt_ref, sd_ref, td_ref, sc_ref, tc_ref, out_s, out_t):
    si = lax.axis_index("y") * 8 + lax.axis_index("z")
    ti = lax.axis_index("x") * 2 + lax.axis_index("c")
    one = jnp.ones((3, L), bf16)

    def fill(points, dual, cot, first, shift, out):
        wide = points.astype(f32)
        norm = jnp.sum(wide * wide, axis=0, keepdims=True)
        bias = (D / 2.0) * dual - 0.5 * norm - shift
        biases = jnp.concatenate(split3(bias), axis=0)
        cots = jnp.concatenate(split3(cot), axis=0)
        none = jnp.zeros((3, L), bf16)
        pad = jnp.zeros((4, L), bf16)
        if first:
            tail = [biases, one, cots, none, pad]
        else:
            tail = [one, biases, none, cots, pad]
        tail = jnp.concatenate([t.astype(f32) for t in tail], axis=0).astype(bf16)
        whole = jnp.concatenate([points, tail], axis=0)
        out[...] = jnp.broadcast_to(whole[None], out.shape)

    fill(src_ref[...], sd_ref[pl.ds(si, 1), :], sc_ref[pl.ds(si, 1), :], True, SHIFT, out_s)
    fill(tgt_ref[...], td_ref[pl.ds(ti, 1), :], tc_ref[pl.ds(ti, 1), :], False, 0.0, out_t)


def cot_of(block, first):
    return join3(block, 70 if first else 73)


def sweep_kernel(xg, yg, plan, wu_out, wv_out, ya, bv, wu, col, tot):
    step = pl.program_id(0)

    @pl.when(step == 0)
    def _():
        for k in range(NB):
            block = yg[k]
            ya[:, k * L : (k + 1) * L] = block
            bv[:, k * L : (k + 1) * L] = jnp.broadcast_to(cot_of(block, False), (8, L))
        col[...] = jnp.zeros_like(col)
        tot[...] = jnp.zeros_like(tot)

    row_id = lax.broadcasted_iota(jnp.int32, (KP, L), 0)
    pick = jnp.where((row_id >= 70) & (row_id < 73), 1.0, 0.0).astype(bf16)
    ones = jnp.ones((8, L), f32)
    wide = 512
    for s in range(STEP):
        xa = xg[s]
        bu = lax.dot_general(xa, pick, (((0,), (0,)), ((), ())), preferred_element_type=f32)
        bu3 = bu.reshape(16, 8, L)
        acc = jnp.zeros((16, 8, L), f32)
        for n in range(COLS // wide):
            dots = lax.dot_general(
                xa, ya[:, n * wide : (n + 1) * wide], (((0,), (0,)), ((), ())), preferred_element_type=f32
            )
            p = jnp.exp2(dots * GAIN)
            plan[s * L : (s + 1) * L, n * wide : (n + 1) * wide] = p.astype(bf16)
            for m in range(wide // L):
                lo = n * wide + m * L
                pm = p[:, m * L : (m + 1) * L].reshape(16, 8, L)
                mixed = pm * (bu3 + bv[:, lo : lo + L][None])
                acc = acc + mixed
                col[:, lo : lo + L] += jnp.sum(mixed, axis=0)
        part = lax.dot_general(
            ones, acc.reshape(L, L), (((1,), (1,)), ((), ())), precision=HI, preferred_element_type=f32
        )
        wu[pl.ds(step * STEP + s, 1), :] = part[:1]
        own = cot_of(xa, True)
        tot[0:8] += jnp.sum(acc * bu3, axis=0)
        tot[8:9] += own * own

    @pl.when(step == pl.num_programs(0) - 1)
    def _():
        wv = jnp.concatenate(
            [jnp.sum(col[:, k * L : (k + 1) * L], axis=0, keepdims=True) for k in range(NB)], axis=0
        )
        cv = jnp.concatenate([bv[0:1, k * L : (k + 1) * L] for k in range(NB)], axis=0)
        bw = jnp.sum(tot[0:8]) + jnp.sum(wv * cv)
        bb = jnp.sum(tot[8:9]) / NA + jnp.sum(cv * cv) / NB
        mark = lax.broadcasted_iota(jnp.int32, (8, L), 0)
        head = jnp.concatenate([wu[...], jnp.where(mark == 0, bw, bb)], axis=0)
        wu_out[...] = jnp.broadcast_to(head[None], wu_out.shape)
        tail = jnp.concatenate([wv, jnp.zeros((8, L), f32)], axis=0)
        wv_out[...] = jnp.broadcast_to(tail[None], wv_out.shape)


def relay_kernel(got, send_in, send):
    del send_in
    total = got[0]
    for k in range(1, got.shape[0]):
        total = total + got[k]
    send[...] = jnp.broadcast_to(total[None], send.shape)


def grad_kernel(
    plan, xg, yg, wu_in, wv_in, pay_s, pay_t, sum_s, sum_t, scal, ay, ru, rv, bu_all, left, acc_s
):
    step = pl.program_id(0)
    last = pl.num_programs(0) - 1

    @pl.when(step == 0)
    def _():
        wu = wu_in[0]
        wv = wv_in[0]
        for k in range(1, NA):
            wu = wu + wu_in[k]
        for k in range(1, NB):
            wv = wv + wv_in[k]
        bw = wv[16:17]
        bb = wv[17:18]
        alpha = bb / (bw + ridge_shift * bb)
        si = lax.axis_index("x") * 4 + lax.axis_index("y")
        ti = lax.axis_index("c") * 8 + lax.axis_index("z")
        scal[0:1, :] = alpha
        scal[1:2, :] = bb
        scal[2:8, :] = jnp.zeros((6, L), f32)
        ru[...] = wu[0:16]
        rv[...] = wv[0:16]
        sum_s[...] = jnp.broadcast_to(ru[pl.ds(si, 1), :], sum_s.shape)
        sum_t[...] = jnp.broadcast_to(rv[pl.ds(ti, 1), :], sum_t.shape)
        for k in range(NA):
            c = cot_of(xg[k], True)
            bu_all[k : k + 1, :] = c
            ru[k : k + 1, :] = c - alpha * (ru[k : k + 1, :] + ridge_shift * c)
        for k in range(NB):
            c = cot_of(yg[k], False)
            r = c - alpha * (rv[k : k + 1, :] + ridge_shift * c)
            rv[k : k + 1, :] = r
            ay[:, k * L : (k + 1) * L] = stack_side(yg[k], c, r)
        left[...] = jnp.zeros_like(left)
        acc_s[...] = jnp.zeros_like(acc_s)

    p = plan[...]
    lhs = []
    for s in range(STEP):
        at = step * STEP + s
        lhs.append(stack_side(xg[at], bu_all[pl.ds(at, 1), :], ru[pl.ds(at, 1), :]))
    ax = jnp.concatenate(lhs, axis=1)
    left[...] += jnp.dot(ax, p, preferred_element_type=f32)
    right = lax.dot_general(ay[...], p, (((1,), (1,)), ((), ())), preferred_element_type=f32)
    for s in range(STEP):
        at = step * STEP + s
        piece = right[:, s * L : (s + 1) * L]
        block, quad = finish_side(piece, bu_all[pl.ds(at, 1), :], ru[pl.ds(at, 1), :])
        pay_s[pl.ds(at, 1)] = block[None]
        acc_s[0:1, :] += quad

    @pl.when(step == last)
    def _():
        total = acc_s[0:1, :]
        square = jnp.zeros((1, L), f32)
        for k in range(NB):
            r = rv[k : k + 1, :]
            c = cot_of(yg[k], False)
            piece = left[:, k * L : (k + 1) * L]
            block, quad = finish_side(piece, c, r)
            pay_t[k] = block
            total = total + quad
            square = square + r * r / NB + ru[k : k + 1, :] * ru[k : k + 1, :] / NA
        quad = jnp.full((1, L), jnp.sum(total), f32)
        rr = jnp.full((1, L), jnp.sum(square), f32)
        extra = jnp.concatenate([t.astype(f32) for t in split3(quad) + split3(rr)], axis=0)
        for k in range(NA):
            tail = pay_s[k, 128:144, :].astype(f32)
            tail = jnp.concatenate([tail[0:3], extra, tail[9:16]], axis=0)
            pay_s[k, 128:144, :] = tail.astype(bf16)


def stack_side(block, c, r):
    pts = block[0:D]
    wide = pts.astype(f32)
    hi, mid, low = split3(r)
    tail = jnp.concatenate(
        [jnp.ones((1, L), f32), hi.astype(f32), mid.astype(f32), low.astype(f32), jnp.zeros((12, L), f32)],
        axis=0,
    )
    return jnp.concatenate([pts, (wide * c).astype(bf16), (wide * r).astype(bf16), tail.astype(bf16)], axis=0)


def finish_side(piece, c, r):
    base = piece[0:D]
    mass = piece[192:193]
    pushed = piece[193:194] + piece[194:195] + piece[195:196]
    t_b = c * base + piece[D : 2 * D]
    t_r = r * base + piece[2 * D : 3 * D]
    s_r = r * mass + pushed
    hi, mid, low = split3(s_r)
    tail = jnp.concatenate([hi.astype(f32), mid.astype(f32), low.astype(f32), jnp.zeros((13, L), f32)], axis=0)
    block = jnp.concatenate([t_b, t_r, tail], axis=0).astype(bf16)
    return block, r * s_r


def merge_kernel(got, send_in, total_out, send):
    total = got[0].astype(f32)
    for k in range(1, NA):
        total = total + got[k].astype(f32)
    total_out[...] = total
    quad = join3(total, 131)
    rr = join3(total, 134)
    extra = jnp.concatenate([t.astype(f32) for t in split3(quad) + split3(rr)], axis=0)
    for k in range(NB):
        tail = send_in[k].astype(f32)
        send[k] = jnp.concatenate([tail[0:3], extra, tail[9:16]], axis=0).astype(bf16)


def final_kernel(sum_src, got, src_ref, tgt_ref, sum_s, sum_t, scal, out_s, out_t):
    tot_t = got[0].astype(f32)
    for k in range(1, NB):
        tot_t = tot_t + got[k].astype(f32)
    tot_s = sum_src[...]
    alpha = scal[0:1, :]
    bb = scal[1:2, :]
    rr = join3(tot_t, 134)
    quad = join3(tot_t, 131) + ridge_shift * rr
    ratio = rr / bb
    step = rr / (quad - ratio * rr / alpha)
    scale = 2.0 / (blur_scale * D)
    c_b = scale * (alpha + step * ratio)
    c_r = scale * step

    def combine(points, tot, s_b, out):
        s = c_b * s_b + c_r * join3(tot, 128)
        out[...] = points.astype(f32) * s - (c_b * tot[0:D] + c_r * tot[D : 2 * D])

    combine(src_ref[...], tot_s, sum_s[0:1, :], out_s)
    combine(tgt_ref[...], tot_t, sum_t[0:1, :], out_t)


def exchange(v, axes):
    return lax.all_to_all(v, axes, 0, 0, tiled=True)


def body(src_points, tgt_points, src_dual, tgt_dual, src_cot, tgt_cot):
    pay_s, pay_t = call(pack_kernel, (sds((NA, KP, L), bf16), sds((NB, KP, L), bf16)))(
        src_points,
        tgt_points,
        src_dual.reshape(-1, L),
        tgt_dual.reshape(-1, L),
        src_cot.reshape(-1, L),
        tgt_cot.reshape(-1, L),
    )
    xg = exchange(pay_s, SA)
    yg = exchange(pay_t, TA)
    steps = NA // STEP
    full = lambda *shape: pl.BlockSpec(shape, lambda i: (0,) * len(shape))
    plan, wu, wv = call(
        sweep_kernel,
        (sds((ROWS, COLS), bf16), sds((NA, 24, L), f32), sds((NB, 24, L), f32)),
        grid=(steps,),
        in_specs=[pl.BlockSpec((STEP, KP, L), lambda i: (i, 0, 0)), full(NB, KP, L)],
        out_specs=(pl.BlockSpec((BLK, COLS), lambda i: (i, 0)), full(NA, 24, L), full(NB, 24, L)),
        scratch_shapes=[
            pltpu.VMEM((KP, COLS), bf16),
            pltpu.VMEM((8, COLS), f32),
            pltpu.VMEM((NA, L), f32),
            pltpu.VMEM((8, COLS), f32),
            pltpu.VMEM((16, L), f32),
        ],
    )(xg, yg)
    wu = exchange(wu, SA)
    tail = lambda n, rows, at: pl.BlockSpec((n, rows, L), lambda i: (0, at, 0))
    wv = call(
        relay_kernel,
        sds((NB, 24, L), f32),
        grid=(1,),
        in_specs=[tail(NA, 8, 2), tail(NB, 8, 2)],
        out_specs=tail(NB, 8, 2),
        input_output_aliases={1: 0},
    )(wu, wv)
    wv = exchange(wv, TA)
    pay_s, pay_t, sum_s, sum_t, scal = call(
        grad_kernel,
        (
            sds((NA, PR, L), bf16),
            sds((NB, PR, L), bf16),
            sds((8, L), f32),
            sds((8, L), f32),
            sds((8, L), f32),
        ),
        grid=(steps,),
        in_specs=[
            pl.BlockSpec((BLK, COLS), lambda i: (i, 0)),
            full(NA, KP, L),
            full(NB, KP, L),
            full(NA, 24, L),
            full(NB, 24, L),
        ],
        out_specs=(full(NA, PR, L), full(NB, PR, L), full(8, L), full(8, L), full(8, L)),
        scratch_shapes=[
            pltpu.VMEM((MA, COLS), bf16),
            pltpu.VMEM((NA, L), f32),
            pltpu.VMEM((NB, L), f32),
            pltpu.VMEM((NA, L), f32),
            pltpu.VMEM((MA, COLS), f32),
            pltpu.VMEM((8, L), f32),
        ],
    )(plan, xg, yg, wu, wv)
    got_s = exchange(pay_s, SA)
    sum_src, pay_t = call(
        merge_kernel,
        (sds((PR, L), f32), sds((NB, PR, L), bf16)),
        grid=(1,),
        in_specs=[full(NA, PR, L), tail(NB, 16, 8)],
        out_specs=(full(PR, L), tail(NB, 16, 8)),
        input_output_aliases={1: 1},
    )(got_s, pay_t)
    got_t = exchange(pay_t, TA)
    return call(final_kernel, (sds((D, L), f32), sds((D, L), f32)))(
        sum_src, got_t, src_points, tgt_points, sum_s, sum_t, scal
    )


def solution(mesh):
    grid = Mesh(mesh.devices.reshape(4, 2, 4, 8), ("x", "c", "y", "z"))
    in_specs = (
        P(None, ("x", "c", "y", "z")),
        P(None, ("y", "z", "x", "c")),
        P(("x", "c")),
        P(("y", "z")),
        P(("x", "c")),
        P(("y", "z")),
    )
    out_specs = (P(None, ("x", "c", "y", "z")), P(None, ("y", "z", "x", "c")))
    return jax.shard_map(body, mesh=grid, in_specs=in_specs, out_specs=out_specs, check_vma=False)
```

time: 922 us -> 131 us (0.14)
  blocking collectives: 593 us -> 103 us
  waiting for transfers between devices: 203 us -> 0 us
  matrix products: 71.2 us -> 0 us
  Pallas kernels: 0 us -> 26.4 us
  between operations: 23.4 us -> 0.64 us
  local copies, waits for them, and re-layouts: 19.3 us -> 0 us
    psum x7 -> x0, blocking collectives: 526 us -> none  [the longest x2 225 us: reduce_rows(): return lax.psum(term, 'col')]
    psum x2 -> x0, waiting for transfers between devices: 203 us -> none  [the longest x1 149 us: reduce_rows(): return lax.psum(term, 'col')]
    all_to_all x0 -> x6, blocking collectives: none -> 103 us  [exchange(): return lax.all_to_all(v, axes, 0, 0, tiled=True)]
    dot_general x40 -> x0, matrix products: 71.2 us -> none  [the longest x24 37.6 us: plan_tile(): lax.dot_general(piece, tgt_block, (((0,), (0,)), ((), ())), preferred_ele...]
    all_gather x2 -> x0, blocking collectives: 67.2 us -> none  [the longest x1 43 us: body(): src_block = lax.all_gather(src_points, 'col', axis=1, tiled=True)]
    pallas_call x0 -> x6, Pallas kernels: none -> 26.4 us  [the longest x1 10.6 us: body(): call(sweep_kernel, (sds((ROWS, COLS), bf16), sds((NA, 24, L), f32), sds((...]
    dynamic_slice x50 -> x0, local copies, waits for them, and re-layouts: 13.9 us -> none  [the longest x8 10.7 us: body(): lax.scan(visit_grad, jnp.zeros((width, tgt_cols), jnp.float32), (src_tile...]
  transfers between devices with their start and end apart: 2 -> 0, of which waited for: 2 -> 0; matrix products, arithmetic and copies ran while one was open for 0% -> 0% of each run, Pallas kernels for 0% -> 0%
where the time goes in v1:
time: 131 us; the launch traced here: 130 us
  blocking collectives  103 us (79%)
  Pallas kernels  26.4 us (20%)
    all_to_all x6, blocking collectives, exchange(): return lax.all_to_all(v, axes, 0, 0, tiled=True)  103 us
    pallas_call x1, Pallas kernels, body(): call(sweep_kernel, (sds((ROWS, COLS), bf16), sds((NA, 24, L), f32), sds((...  10.6 us
    pallas_call x1, Pallas kernels, body(): call(grad_kernel, (sds((NA, PR, L), bf16), sds((NB, PR, L), bf16), sds((8...  8.98 us

profile of v1, /device:TPU:1, one launch (start us, length us, event | category | flops | bytes accessed | tf_op | source)
XLA Modules:
  0.0 130.5 jit_solution(1452959626743291253)
XLA Ops:
  0.6 1.7 %shard_map.77 = (bf16[16,80,128]{2,1,0:T(8,128)(2,1)}, bf16[16,80,128]{2,1,0:T(8,128)(2,1)}) custom-call(bf16[64,128]{1,0:T(8,128)(2,1)} %src_ref.3, bf16[64,128]{1,0:T(8,128)(2,1)} %tgt_ref.3, f32[32,128]{1,0:T(8,128)} %bitcast.4, f32[8,128]{1,0:T(8,128)} %bitcast.6, f32[32,128]{1,0:T(8,128)} %bitcast.5, f32[8,128]{1,0:T(8,128)} %bitcast.7), custom_call_target="tpu_custom_call" | custom-call | tf_op jit(solution)/shard_map/pallas_call | solution.py:294
  2.4 15.5 %all_to_all.30.xg = bf16[16,80,128]{2,1,0:T(8,128)(2,1)} all-to-all(bf16[16,80,128]{2,1,0:T(8,128)(2,1)} %get-tuple-element.14), channel_id=1, replica_groups=mesh['x'=4,'c'=2,'y'=4,'z'=8] {'x','y'}, dimensions={0} | all-to-all | bytes 655360 | tf_op jit(solution)/shard_map/all_to_all | solution.py:290
  17.9 21.6 %all_to_all.31.yg = bf16[16,80,128]{2,1,0:T(8,128)(2,1)} all-to-all(bf16[16,80,128]{2,1,0:T(8,128)(2,1)} %get-tuple-element.15), channel_id=1, replica_groups=mesh['x'=4,'c'=2,'y'=4,'z'=8] {'c','z'}, dimensions={0} | all-to-all | bytes 655360 | tf_op jit(solution)/shard_map/all_to_all | solution.py:290
  39.4 10.6 %shard_map.78 = (bf16[2048,2048]{1,0:T(8,128)(2,1)}, f32[16,24,128]{2,1,0:T(8,128)}, f32[16,24,128]{2,1,0:T(8,128)}) custom-call(bf16[16,80,128]{2,1,0:T(8,128)(2,1)} %all_to_all.30.xg, bf16[16,80,128]{2,1,0:T(8,128)(2,1)} %all_to_all.31.yg), custom_call_target="tpu_custom_call" | custom-call | tf_op jit(solution)/shard_map/pallas_call | solution.py:306
  50.0 11.2 %all_to_all.32.got.wu_in = f32[16,24,128]{2,1,0:T(8,128)} all-to-all(f32[16,24,128]{2,1,0:T(8,128)} %get-tuple-element.17), channel_id=1, replica_groups=mesh['x'=4,'c'=2,'y'=4,'z'=8] {'x','y'}, dimensions={0} | all-to-all | bytes 393216 | tf_op jit(solution)/shard_map/all_to_all | solution.py:290
  61.2 1.5 %shard_map.79 = f32[16,24,128]{2,1,0:T(8,128)} custom-call(f32[16,24,128]{2,1,0:T(8,128)} %all_to_all.32.got.wu_in, f32[16,24,128]{2,1,0:T(8,128)} %get-tuple-element.18.send_in), custom_call_target="tpu_custom_call", output_to_operand_aliasing={{}: (1, {})} | custom-call | tf_op jit(solution)/shard_map/pallas_call | solution.py:322
  62.8 15.0 %all_to_all.33.wv_in = f32[16,24,128]{2,1,0:T(8,128)} all-to-all(f32[16,24,128]{2,1,0:T(8,128)} %shard_map.79), channel_id=1, replica_groups=mesh['x'=4,'c'=2,'y'=4,'z'=8] {'c','z'}, dimensions={0} | all-to-all | bytes 393216 | tf_op jit(solution)/shard_map/all_to_all | solution.py:290
  77.7 9.0 %shard_map.80 = (bf16[16,144,128]{2,1,0:T(8,128)(2,1)}, bf16[16,144,128]{2,1,0:T(8,128)(2,1)}, f32[8,128]{1,0:T(8,128)}, f32[8,128]{1,0:T(8,128)}, f32[8,128]{1,0:T(8,128)}) custom-call(bf16[2048,2048]{1,0:T(8,128)(2,1)} %get-tuple-element.16.plan, bf16[16,80,128]{2,1,0:T(8,128)(2,1)} %all_to_all.30.xg, bf16[16,80,128]{2,1,0:T(8,128)(2,1)} %all_to_all.31.yg, ...), custom_call_target="tpu_custom_call" | custom-call | tf_op jit(solution)/shard_map/pallas_call | solution.py:331
  86.7 15.1 %all_to_all.34.got = bf16[16,144,128]{2,1,0:T(8,128)(2,1)} all-to-all(bf16[16,144,128]{2,1,0:T(8,128)(2,1)} %get-tuple-element.19), channel_id=1, replica_groups=mesh['x'=4,'c'=2,'y'=4,'z'=8] {'x','y'}, dimensions={0} | all-to-all | bytes 1179648 | tf_op jit(solution)/shard_map/all_to_all | solution.py:290
  101.8 1.8 %shard_map.81 = (f32[144,128]{1,0:T(8,128)}, bf16[16,144,128]{2,1,0:T(8,128)(2,1)}) custom-call(bf16[16,144,128]{2,1,0:T(8,128)(2,1)} %all_to_all.34.got, bf16[16,144,128]{2,1,0:T(8,128)(2,1)} %get-tuple-element.20.send_in), custom_call_target="tpu_custom_call", output_to_operand_aliasing={{1}: (1, {})} | custom-call | tf_op jit(solution)/shard_map/pallas_call | solution.py:359
  103.7 25.0 %all_to_all.35.got = bf16[16,144,128]{2,1,0:T(8,128)(2,1)} all-to-all(bf16[16,144,128]{2,1,0:T(8,128)(2,1)} %get-tuple-element.22), channel_id=1, replica_groups=mesh['x'=4,'c'=2,'y'=4,'z'=8] {'c','z'}, dimensions={0} | all-to-all | bytes 1179648 | tf_op jit(solution)/shard_map/all_to_all | solution.py:290
  128.7 1.8 %shard_map.82 = (f32[64,128]{1,0:T(8,128)}, f32[64,128]{1,0:T(8,128)}) custom-call(f32[144,128]{1,0:T(8,128)} %get-tuple-element.21.sum_src, bf16[16,144,128]{2,1,0:T(8,128)(2,1)} %all_to_all.35.got, bf16[64,128]{1,0:T(8,128)(2,1)} %src_ref.3, bf16[64,128]{1,0:T(8,128)(2,1)} %tgt_ref.3, f32[8,128]{1,0:T(8,128)} %get-tuple-element.23.sum_s, ...), custom_call_target="tpu_custom_call" | custom-call | tf_op jit(solution)/shard_map/pallas_call | solution.py:368

commit v2 on v0

v2 whole, which is shorter than its diff:
```python
import jax
import jax.numpy as jnp
import numpy as np
from jax import lax
from jax.experimental import pallas as pl
from jax.experimental.pallas import tpu as pltpu
from jax.sharding import Mesh, PartitionSpec as P

blur_scale = 0.25
ridge_shift = 0.5
D = 64
L = 128
KP = 80
SA = ("x", "y")
NA = 16
NB = 16
NZ = 8
ROWS = NA * L
COLS = NB * L
MB = 144
MW = 80
PR = 144
LOG2E = 1.4426950408889634
GAIN = 2.0 * LOG2E / (blur_scale * D)
SHIFT = 15.0 / GAIN
f32 = jnp.float32
bf16 = jnp.bfloat16
HI = lax.Precision.HIGHEST
VMEM = 24 * 1024 * 1024


def split3(v):
    hi = v.astype(bf16)
    rest = v - hi.astype(f32)
    mid = rest.astype(bf16)
    low = (rest - mid.astype(f32)).astype(bf16)
    return hi, mid, low


def join3(block, at):
    return (
        block[at : at + 1].astype(f32)
        + block[at + 1 : at + 2].astype(f32)
        + block[at + 2 : at + 3].astype(f32)
    )


def sds(shape, dtype):
    return jax.ShapeDtypeStruct(shape, dtype)


def call(kernel, out_shape, flops=0, **kw):
    cost = pl.CostEstimate(flops=flops, bytes_accessed=1 << 20, transcendentals=0)
    return pl.pallas_call(
        kernel,
        out_shape=out_shape,
        cost_estimate=cost,
        compiler_params=pltpu.CompilerParams(vmem_limit_bytes=VMEM),
        **kw,
    )


def encode(points, dual, cot, first):
    one = jnp.ones((3, L), f32)
    none = jnp.zeros((3, L), f32)
    wide = points.astype(f32)
    norm = jnp.sum(wide * wide, axis=0, keepdims=True)
    bias = (D / 2.0) * dual - 0.5 * norm
    if first:
        bias = bias - SHIFT
    biases = [t.astype(f32) for t in split3(bias)]
    cots = [t.astype(f32) for t in split3(cot)]
    tail = biases + [one] + cots + [none] if first else [one] + biases + [none] + cots
    tail = jnp.concatenate(tail + [jnp.zeros((4, L), f32)], axis=0).astype(bf16)
    return jnp.concatenate([points, tail], axis=0)


def cot_of(block, first):
    return join3(block, 70 if first else 73)


def encode_src(points, dual, cot, out):
    at = lax.axis_index("y") * 8 + lax.axis_index("z")
    out[...] = encode(points[...], dual[pl.ds(at, 1), :], cot[pl.ds(at, 1), :], True)


def encode_tgt(points, other, dual, cot, out):
    core = lax.axis_index("c")
    at = lax.axis_index("x") * 2
    own = points[...].astype(f32)
    sib = other[...].astype(f32)
    flip = core == 0
    low = jnp.where(flip, own, sib).astype(bf16)
    high = jnp.where(flip, sib, own).astype(bf16)
    both = jnp.concatenate(
        [
            encode(low, dual[pl.ds(at, 1), :], cot[pl.ds(at, 1), :], False),
            encode(high, dual[pl.ds(at + 1, 1), :], cot[pl.ds(at + 1, 1), :], False),
        ],
        axis=0,
    )
    out[...] = jnp.broadcast_to(both[None], out.shape)


def sweep_kernel(g0, g1, g2, g3, yg, plan, xs, cots, wu_out, wv_out, xt, ya, bub, bvb, row, col):
    mx = lax.axis_index("x")
    my = lax.axis_index("y")
    for m, g in enumerate((g0, g1, g2, g3)):
        for k in range(4):
            at = lax.rem(mx + 4 - k, 4) * 4 + lax.rem(my + 4 - m, 4)
            xs[pl.ds(at, 1)] = g[k][None]
    pad = jnp.zeros((L - KP, L), f32)
    row_id = lax.broadcasted_iota(jnp.int32, (L, L), 0)
    pick = jnp.where((row_id >= 70) & (row_id < 73), 1.0, 0.0).astype(bf16)
    for k in range(NA):
        sl = slice(k * L, (k + 1) * L)
        block = xs[k]
        turned = jnp.concatenate([block.astype(f32), pad], axis=0).T.astype(bf16)
        xt[sl, :] = turned
        bub[sl, :] = jnp.dot(turned, pick, preferred_element_type=f32)
        cots[k : k + 1, :] = cot_of(block, True)
        other = yg[k]
        ya[:, sl] = jnp.concatenate([other, pad.astype(bf16)], axis=0)
        c = cot_of(other, False)
        cots[NA + k : NA + k + 1, :] = c
        bvb[:, sl] = jnp.broadcast_to(c, (8, L))
    rb, wide = 512, 256
    for n in range(COLS // wide):
        for r in range(ROWS // rb):
            rows = slice(r * rb, (r + 1) * rb)
            dots = jnp.dot(xt[rows, :], ya[:, n * wide : (n + 1) * wide], preferred_element_type=f32)
            p = jnp.exp2(dots * GAIN)
            plan[rows, n * wide : (n + 1) * wide] = p.astype(bf16)
            bu = bub[rows, :].reshape(rb // 8, 8, L)
            acc = None if n == 0 else row[rows, :].reshape(rb // 8, 8, L)
            for m in range(wide // L):
                sl = slice(n * wide + m * L, n * wide + (m + 1) * L)
                mixed = p[:, m * L : (m + 1) * L].reshape(rb // 8, 8, L) * (bu + bvb[:, sl][None])
                acc = mixed if acc is None else acc + mixed
                down = jnp.sum(mixed, axis=0)
                col[:, sl] = down if r == 0 else col[:, sl] + down
            row[rows, :] = acc.reshape(rb, L)
    wu = jnp.concatenate(
        [jnp.sum(row[k * L : (k + 1) * L, :].T, axis=0, keepdims=True) for k in range(NA)], axis=0
    )
    wv = jnp.concatenate(
        [jnp.sum(col[:, k * L : (k + 1) * L], axis=0, keepdims=True) for k in range(NB)], axis=0
    )
    bu = cots[0:NA]
    bv = cots[NA : NA + NB]
    bw = jnp.sum(wu * bu + wv * bv)
    bb = jnp.sum(bu * bu) / NA + jnp.sum(bv * bv) / NB
    mark = lax.broadcasted_iota(jnp.int32, (8, L), 0)
    head = jnp.concatenate([wu, jnp.where(mark == 0, bw, bb)], axis=0)
    wu_out[...] = jnp.broadcast_to(head[None], wu_out.shape)
    wv_out[...] = wv


def stack_cot(block, c):
    pts = block[0:D]
    tail = [jnp.ones((1, L), f32)] + [t.astype(f32) for t in split3(c)] + [jnp.zeros((12, L), f32)]
    tail = jnp.concatenate(tail, axis=0).astype(bf16)
    return jnp.concatenate([pts, (pts.astype(f32) * c).astype(bf16), tail], axis=0)


def stack_one(block, c):
    tail = [t.astype(f32) for t in split3(c)] + [jnp.zeros((13, L), f32)]
    tail = jnp.concatenate(tail, axis=0).astype(bf16)
    return jnp.concatenate([(block[0:D].astype(f32) * c).astype(bf16), tail], axis=0)


def first_kernel(plan, xs, yg, cots, right, left, ax, ay):
    for k in range(NA):
        ax[:, k * L : (k + 1) * L] = stack_cot(xs[k], cots[k : k + 1, :])
        ay[:, k * L : (k + 1) * L] = stack_cot(yg[k], cots[NA + k : NA + k + 1, :])
    wide = 256
    for r in range(ROWS // wide):
        part = lax.dot_general(
            ay[...], plan[r * wide : (r + 1) * wide, :], (((1,), (1,)), ((), ())), preferred_element_type=f32
        )
        for m in range(2):
            at = 2 * r + m
            right[:, at * L : (at + 1) * L] = fold_cot(part[:, m * L : (m + 1) * L], cots[at : at + 1, :])
    for n in range(COLS // wide):
        part = jnp.dot(ax[...], plan[:, n * wide : (n + 1) * wide], preferred_element_type=f32)
        for m in range(2):
            at = 2 * n + m
            c = cots[NA + at : NA + at + 1, :]
            left[:, at * L : (at + 1) * L] = fold_cot(part[:, m * L : (m + 1) * L], c)


def fold_cot(part, c):
    tail = part[2 * D : 2 * D + 16]
    pushed = tail[1:2] + tail[2:3] + tail[3:4]
    tail = jnp.concatenate([tail[0:1], pushed, jnp.zeros((14, L), f32)], axis=0)
    return jnp.concatenate([part[0:D], c * part[0:D] + part[D : 2 * D], tail], axis=0)


def relay_kernel(got, own, sib, send):
    total = got[0]
    for k in range(1, got.shape[0]):
        total = total + got[k]
    whole = jnp.concatenate([own[...] + sib[...], total], axis=0)
    send[...] = jnp.broadcast_to(whole[None], send.shape)


def second_kernel(plan, yg, cots, wu_in, wv_in, right, out, sums, aw):
    wu = wu_in[0, 0:NA]
    for k in range(1, NA):
        wu = wu + wu_in[k, 0:NA]
    wv = wv_in[0, 0:NB]
    for k in range(1, NZ):
        wv = wv + wv_in[k, 0:NB]
    sums[0:NA] = wu
    sums[NA : NA + NB] = wv
    for k in range(NB):
        w = sums[NA + k : NA + k + 1, :] + ridge_shift * cots[NA + k : NA + k + 1, :]
        aw[:, k * L : (k + 1) * L] = stack_one(yg[k], w)
    wide = 256
    for r in range(ROWS // wide):
        part = lax.dot_general(
            aw[...], plan[r * wide : (r + 1) * wide, :], (((1,), (1,)), ((), ())), preferred_element_type=f32
        )
        for m in range(2):
            at = 2 * r + m
            sl = slice(at * L, (at + 1) * L)
            w = sums[at : at + 1, :] + ridge_shift * cots[at : at + 1, :]
            piece = part[:, m * L : (m + 1) * L]
            pushed = piece[D : D + 1] + piece[D + 1 : D + 2] + piece[D + 2 : D + 3]
            out[0:D, sl] = w * right[0:D, sl] + piece[0:D]
            out[D : D + 8, sl] = jnp.broadcast_to(pushed, (8, L))


def step_of(wv_in, wv_sib):
    total = wv_in[0, NB : NB + 8]
    for k in range(1, NZ):
        total = total + wv_in[k, NB : NB + 8]
    for k in range(NZ):
        total = total + wv_sib[k, NB : NB + 8]
    bw = total[0:1]
    bb = total[1:2]
    return bb / (bw + ridge_shift * bb), bb


def payload_of(t_b, t_r, s_r, rest):
    tail = jnp.concatenate([t.astype(f32) for t in split3(s_r)] + rest, axis=0)
    return jnp.concatenate([t_b, t_r, tail], axis=0).astype(bf16)


def send_kernel(right, second, cots, sums, wv_in, wv_sib, left_tail, pay, scal):
    alpha, bb = step_of(wv_in, wv_sib)
    bu, bv = cots[0:NA], cots[NA : NA + NB]
    ru = bu - alpha * (sums[0:NA] + ridge_shift * bu)
    rv = bv - alpha * (sums[NA : NA + NB] + ridge_shift * bv)
    rr = jnp.sum(ru * ru) / NA + jnp.sum(rv * rv) / NB
    quad = jnp.zeros((1, L), f32)
    s_rows = []
    for k in range(NA):
        sl = slice(k * L, (k + 1) * L)
        r = ru[k : k + 1]
        mass = right[2 * D : 2 * D + 1, sl]
        pushed = right[2 * D + 1 : 2 * D + 2, sl] - alpha * second[D : D + 1, sl]
        s_r = r * mass + pushed
        s_rows.append(s_r)
        quad = quad + r * (s_r + pushed)
        v = rv[k : k + 1]
        quad = quad + v * v * left_tail[0:1, sl]
    quad = jnp.full((1, L), jnp.sum(quad), f32)
    rr = jnp.full((1, L), rr, f32)
    extra = [t.astype(f32) for t in split3(quad) + split3(rr)] + [jnp.zeros((7, L), f32)]
    for k in range(NA):
        sl = slice(k * L, (k + 1) * L)
        t_b = right[D : 2 * D, sl]
        t_r = t_b - alpha * second[0:D, sl]
        pay[k] = payload_of(t_b, t_r, s_rows[k], extra)
    scal[0:1, :] = alpha
    scal[1:2, :] = bb
    scal[2:8, :] = jnp.zeros((6, L), f32)


def third_kernel(plan, xs, cots, sums, left, scal, mine, other, aw):
    core = lax.axis_index("c")
    for k in range(NA):
        w = sums[k : k + 1, :] + ridge_shift * cots[k : k + 1, :]
        aw[:, k * L : (k + 1) * L] = stack_one(xs[k], w)
    alpha = scal[0:1, :]
    none = [jnp.zeros((13, L), f32)]
    wide = 256
    for n in range(COLS // wide):
        part = jnp.dot(aw[...], plan[:, n * wide : (n + 1) * wide], preferred_element_type=f32)
        blocks = []
        for m in range(2):
            at = 2 * n + m
            sl = slice(at * L, (at + 1) * L)
            piece = part[:, m * L : (m + 1) * L]
            c = cots[NA + at : NA + at + 1, :]
            w = sums[NA + at : NA + at + 1, :] + ridge_shift * c
            r = c - alpha * w
            t_b = left[D : 2 * D, sl]
            t_r = t_b - alpha * (w * left[0:D, sl] + piece[0:D])
            pushed = piece[D : D + 1] + piece[D + 1 : D + 2] + piece[D + 2 : D + 3]
            s_r = r * left[2 * D : 2 * D + 1, sl] + left[2 * D + 1 : 2 * D + 2, sl] - alpha * pushed
            blocks.append(payload_of(t_b, t_r, s_r, none))

        @pl.when(core == 0)
        def _():
            mine[n] = blocks[0]
            other[n] = blocks[1]

        @pl.when(core != 0)
        def _():
            mine[n] = blocks[1]
            other[n] = blocks[0]


def join_kernel(mine, got, send):
    a = mine[...].astype(f32)
    b = got[...].astype(f32)
    total = a + b
    send[...] = total.astype(bf16)
    for k in range(NZ):
        s = join3(mine[k], 128) + join3(got[k], 128)
        tail = jnp.concatenate([t.astype(f32) for t in split3(s)] + [jnp.zeros((13, L), f32)], axis=0)
        send[k, 128:144, :] = tail.astype(bf16)


def pass_kernel(got, send_in, send):
    total = got[0].astype(f32)
    for k in range(1, NA):
        total = total + got[k].astype(f32)
    quad = join3(total, 3)
    rr = join3(total, 6)
    extra = jnp.concatenate([t.astype(f32) for t in split3(quad) + split3(rr)], axis=0)
    for k in range(NZ):
        tail = send_in[k].astype(f32)
        send[k] = jnp.concatenate([tail[0:3], extra, tail[9:16]], axis=0).astype(bf16)


def total_kernel(got, out):
    total = got[0].astype(f32)
    for k in range(1, got.shape[0]):
        total = total + got[k].astype(f32)
    out[...] = total


def final_kernel(tot_s, tot_t, sib, src_ref, tgt_ref, sums, scal, out_s, out_t):
    alpha = scal[0:1, :]
    bb = scal[1:2, :]
    more = sib[0].astype(f32)
    for k in range(1, NZ):
        more = more + sib[k].astype(f32)
    rr = join3(tot_t[...], 134) + join3(more, 6)
    quad = join3(tot_t[...], 131) + join3(more, 3) + ridge_shift * rr
    ratio = rr / bb
    step = rr / (quad - ratio * rr / alpha)
    scale = 2.0 / (blur_scale * D)
    c_b = scale * (alpha + step * ratio)
    c_r = scale * step
    si = lax.axis_index("x") * 4 + lax.axis_index("y")
    ti = lax.axis_index("z") * 2 + lax.axis_index("c")

    def combine(points, tot, s_b, out):
        s = c_b * s_b + c_r * join3(tot, 128)
        out[...] = points[...].astype(f32) * s - (c_b * tot[0:D] + c_r * tot[D : 2 * D])

    combine(src_ref, tot_s[...], sums[pl.ds(si, 1), :], out_s)
    combine(tgt_ref, tot_t[...], sums[pl.ds(NA + ti, 1), :], out_t)


def exchange(v, axes):
    return lax.all_to_all(v, axes, 0, 0, tiled=True)


def shift(v, axis, n, k):
    return lax.ppermute(v, axis, [(i, (i + k) % n) for i in range(n)])


def swap(v):
    return shift(v, "c", 2, 1)


def body(src_points, tgt_points, src_dual, tgt_dual, src_cot, tgt_cot):
    whole = lambda v: v.reshape(-1, L)
    own = call(encode_src, sds((KP, L), bf16))(src_points, whole(src_dual), whole(src_cot))
    send = call(encode_tgt, sds((NZ, 2 * KP, L), bf16))(
        tgt_points, swap(tgt_points), whole(tgt_dual), whole(tgt_cot)
    )
    yg = exchange(send, "z").reshape(NB, KP, L)
    g0 = jnp.stack([own] + [shift(own, "x", 4, k) for k in (1, 2, 3)], axis=0)
    g1, g2, g3 = [shift(g0, "y", 4, k) for k in (1, 2, 3)]
    unit = ROWS * COLS * 2
    vm = pltpu.VMEM
    plan, xs, cots, wu, wv = call(
        sweep_kernel,
        (
            sds((ROWS, COLS), bf16),
            sds((NA, KP, L), bf16),
            sds((NA + NB, L), f32),
            sds((NA, 24, L), f32),
            sds((NB, L), f32),
        ),
        flops=unit * 400,
        scratch_shapes=[
            vm((ROWS, L), bf16),
            vm((L, COLS), bf16),
            vm((ROWS, L), f32),
            vm((8, COLS), f32),
            vm((ROWS, L), f32),
            vm((8, COLS), f32),
        ],
    )(g0, g1, g2, g3, yg)
    wu = exchange(wu, SA)
    right, left = call(
        first_kernel,
        (sds((MB, ROWS), f32), sds((MB, COLS), f32)),
        flops=unit * 512,
        scratch_shapes=[vm((MB, ROWS), bf16), vm((MB, COLS), bf16)],
    )(plan, xs, yg, cots)

    def tail(n, rows, at):
        return pl.BlockSpec((n, rows, L), lambda i: (0, at, 0))

    def full(*shape):
        return pl.BlockSpec(shape, lambda i: (0,) * len(shape))

    send = call(
        relay_kernel,
        sds((NZ, 24, L), f32),
        grid=(1,),
        in_specs=[tail(NA, 8, 2), full(NB, L), full(NB, L)],
        out_specs=full(NZ, 24, L),
    )(wu, wv, swap(wv))
    wv = exchange(send, "z")
    wv_sib = swap(wv)
    second, sums = call(
        second_kernel,
        (sds((D + 8, ROWS), f32), sds((NA + NB, L), f32)),
        flops=unit * 256,
        scratch_shapes=[vm((MW, COLS), bf16)],
    )(plan, yg, cots, wu, wv, right)
    pay, scal = call(
        send_kernel,
        (sds((NA, PR, L), bf16), sds((8, L), f32)),
        grid=(1,),
        in_specs=[
            full(MB, ROWS),
            full(D + 8, ROWS),
            full(NA + NB, L),
            full(NA + NB, L),
            full(NZ, 24, L),
            full(NZ, 24, L),
            pl.BlockSpec((8, COLS), lambda i: (2 * D // 8, 0)),
        ],
        out_specs=(full(NA, PR, L), full(8, L)),
    )(right, second, cots, sums, wv, wv_sib, left)
    got_s = exchange(pay, SA)
    mine, other = call(
        third_kernel,
        (sds((NZ, PR, L), bf16), sds((NZ, PR, L), bf16)),
        flops=unit * 256,
        scratch_shapes=[vm((MW, ROWS), bf16)],
    )(plan, xs, cots, sums, left, scal)
    send = call(join_kernel, sds((NZ, PR, L), bf16), flops=unit * 64)(mine, swap(other))
    send = call(
        pass_kernel,
        sds((NZ, PR, L), bf16),
        grid=(1,),
        in_specs=[tail(NA, 16, 8), tail(NZ, 16, 8)],
        out_specs=tail(NZ, 16, 8),
        input_output_aliases={1: 0},
    )(got_s, send)
    got_t = exchange(send, "z")
    tot_s = call(total_kernel, sds((PR, L), f32), flops=unit * 64)(got_s)
    tot_t = call(total_kernel, sds((PR, L), f32), flops=unit * 64)(got_t)
    return call(
        final_kernel,
        (sds((D, L), f32), sds((D, L), f32)),
        grid=(1,),
        in_specs=[
            full(PR, L),
            full(PR, L),
            tail(NZ, 16, 8),
            full(D, L),
            full(D, L),
            full(NA + NB, L),
            full(8, L),
        ],
        out_specs=(full(D, L), full(D, L)),
    )(tot_s, tot_t, swap(got_t), src_points, tgt_points, sums, scal)


def solution(mesh):
    grid = Mesh(mesh.devices.reshape(4, 2, 4, 8), ("x", "c", "y", "z"))
    in_specs = (
        P(None, ("x", "c", "y", "z")),
        P(None, ("y", "z", "x", "c")),
        P(("x", "c")),
        P(("y", "z")),
        P(("x", "c")),
        P(("y", "z")),
    )
    out_specs = (P(None, ("x", "c", "y", "z")), P(None, ("y", "z", "x", "c")))
    return jax.shard_map(body, mesh=grid, in_specs=in_specs, out_specs=out_specs, check_vma=False)
```

time: 922 us -> 116 us (0.13)
  blocking collectives: 593 us -> 15.4 us
  waiting for transfers between devices: 203 us -> 17.6 us
  matrix products: 71.2 us -> 0 us
  starting transfers between devices: 0.08 us -> 44.9 us
  between operations: 23.4 us -> 0.76 us
  Pallas kernels: 0 us -> 18.3 us
    psum x7 -> x0, blocking collectives: 526 us -> none  [the longest x2 225 us: reduce_rows(): return lax.psum(term, 'col')]
    psum x2 -> x0, waiting for transfers between devices: 203 us -> none  [the longest x1 149 us: reduce_rows(): return lax.psum(term, 'col')]
    dot_general x40 -> x0, matrix products: 71.2 us -> none  [the longest x24 37.6 us: plan_tile(): lax.dot_general(piece, tgt_block, (((0,), (0,)), ((), ())), preferred_ele...]
    all_gather x2 -> x0, blocking collectives: 67.2 us -> none  [the longest x1 43 us: body(): src_block = lax.all_gather(src_points, 'col', axis=1, tiled=True)]
    ppermute x0 -> x11, starting transfers between devices: none -> 25 us  [shift(): return lax.ppermute(v, axis, [(i, (i + k) % n) for i in range(n)])]
    all_to_all x0 -> x4, starting transfers between devices: none -> 19.9 us  [exchange(): return lax.all_to_all(v, axes, 0, 0, tiled=True)]
    pallas_call x0 -> x13, Pallas kernels: none -> 18.3 us  [the longest x1 5.35 us: body(): call(sweep_kernel, (sds((ROWS, COLS), bf16), sds((NA, KP, L), bf16), sds(...]
    unnamed x13 -> x26, local copies, waits for them, and re-layouts: 2.28 us -> 18.5 us
  transfers between devices with their start and end apart: 2 -> 15, of which waited for: 2 -> 11; matrix products, arithmetic and copies ran while one was open for 0% -> 0% of each run, Pallas kernels for 0% -> 9%
where the time goes in v2:
time: 116 us; the launch traced here: 115 us
  starting transfers between devices  44.9 us (39%)
  local copies, waits for them, and re-layouts  18.5 us (16%)
  Pallas kernels  18.3 us (16%)
  waiting for transfers between devices  17.6 us (15%)
  blocking collectives  15.4 us (13%)
    ppermute x11, starting transfers between devices, shift(): return lax.ppermute(v, axis, [(i, (i + k) % n) for i in range(n)])  25 us
    all_to_all x4, starting transfers between devices, exchange(): return lax.all_to_all(v, axes, 0, 0, tiled=True)  19.9 us
    unnamed x26, local copies, waits for them, and re-layouts  18.5 us
    all_to_all x1, blocking collectives, exchange(): return lax.all_to_all(v, axes, 0, 0, tiled=True)  15.4 us
    ppermute x11, waiting for transfers between devices, shift(): return lax.ppermute(v, axis, [(i, (i + k) % n) for i in range(n)])  12.5 us
    pallas_call x1, Pallas kernels, body(): call(sweep_kernel, (sds((ROWS, COLS), bf16), sds((NA, KP, L), bf16), sds(...  5.35 us
    all_to_all x4, waiting for transfers between devices, exchange(): return lax.all_to_all(v, axes, 0, 0, tiled=True)  5.03 us
    pallas_call x1, Pallas kernels, body(): call(first_kernel, (sds((MB, ROWS), f32), sds((MB, COLS), f32)), flops=un...  4.17 us
  transfers between devices with their start and end apart: 15, of which 11 were waited for; matrix products, arithmetic and copies ran while one was open for 0% of the time, Pallas kernels for 9%

profile of v2, /device:TPU:1, one launch (start us, length us, event | category | flops | bytes accessed | tf_op | source)
XLA Modules:
  0.0 115.5 jit_solution(8487745043841125633)
XLA Ops:
  0.6 3.3 %collective-permute-start.6 = (bf16[64,128]{1,0:T(8,128)(2,1)}, bf16[64,128]{1,0:T(8,128)(2,1)S(1)}, u32[]{:S(2)}, u32[]{:S(2)}) collective-permute-start(bf16[64,128]{1,0:T(8,128)(2,1)} %tgt_ref.1), channel_id=1, source_target_pairs={{0,32},{32,0},{1,33},{33,1},{2,34},{34,2},{3,35},{35,3},{4,36},{36... | collective-permute-start | bytes 49160 | tf_op jit(solution)/shard_map/ppermute | solution.py:375
  4.0 1.0 collective-permute-done.6.other
  5.0 0.0 copy-start.7
  5.0 0.7 copy-done.7
  5.7 0.0 copy-start.11
  5.7 0.7 copy-done.11
  6.4 0.0 copy-start.12
  6.4 0.7 copy-done.12
  7.1 0.8 shard_map.78
  7.9 6.5 %all-to-all-start = ((bf16[8,160,128]{2,1,0:T(8,128)(2,1)}), bf16[8,160,128]{2,1,0:T(8,128)(2,1)S(1)}, u32[]{:S(2)}, u32[]{:S(2)}) async-start(bf16[8,160,128]{2,1,0:T(8,128)(2,1)} %shard_map.78), calls=%async_computation | async-start | bytes 655360 | tf_op jit(solution)/shard_map/all_to_all | solution.py:371
  14.3 0.0 copy-start.5
  14.3 0.7 copy-done.5
  15.0 0.0 copy-start.9
  15.0 0.7 copy-done.9
  15.8 0.7 copy-done.10
  16.5 2.6 %collective-permute-start.2 = (bf16[80,128]{1,0:T(8,128)(2,1)S(1)}, bf16[80,128]{1,0:T(8,128)(2,1)S(1)}, u32[]{:S(2)}, u32[]{:S(2)}) collective-permute-start(bf16[80,128]{1,0:T(8,128)(2,1)S(1)} %shard_map.77), channel_id=1, source_target_pairs={{0,192},{64,0},{128,64},{192,128},{1,193},{65,1},{129,65},{193,129... | collective-permute-start | bytes 61448 | tf_op jit(solution)/shard_map/ppermute | solution.py:375
  19.1 0.5 collective-permute-start.1
  19.6 0.6 collective-permute-start
  20.2 0.0 collective-permute-done.2
  20.2 3.3 %collective-permute-done.1 = bf16[80,128]{1,0:T(8,128)(2,1)S(1)} collective-permute-done((bf16[80,128]{1,0:T(8,128)(2,1)S(1)}, bf16[80,128]{1,0:T(8,128)(2,1)S(1)}, u32[]{:S(2)}, u32[]{:S(2)}) %collective-permute-start.1) | collective-permute-done | bytes 20512 | tf_op jit(solution)/shard_map/ppermute | solution.py:375
  23.5 0.2 collective-permute-done
  23.7 2.8 %collective-permute-start.5 = (bf16[4,80,128]{2,1,0:T(8,128)(2,1)S(1)}, bf16[4,80,128]{2,1,0:T(8,128)(2,1)S(1)}, u32[]{:S(2)}, u32[]{:S(2)}) collective-permute-start(bf16[4,80,128]{2,1,0:T(8,128)(2,1)S(1)} %pad_maximum_fusion.g0), channel_id=1, source_target_pairs={{0,24},{8,0},{16,8},{24,16},{1,25},{9,1},{17,9},{25,17},{2,26},{10... | collective-permute-start | bytes 245768 | tf_op jit(solution)/shard_map/ppermute | solution.py:375
  26.5 0.3 collective-permute-start.4
  26.9 0.7 collective-permute-start.3
  27.6 0.4 collective-permute-done.5.g3
  28.0 3.4 %collective-permute-done.4.g2 = bf16[4,80,128]{2,1,0:T(8,128)(2,1)S(1)} collective-permute-done((bf16[4,80,128]{2,1,0:T(8,128)(2,1)S(1)}, bf16[4,80,128]{2,1,0:T(8,128)(2,1)S(1)}, u32[]{:S(2)}, u32[]{:S(2)}) %collective-permute-start.4) | collective-permute-done | bytes 81952 | tf_op jit(solution)/shard_map/ppermute | solution.py:375
  31.4 0.8 collective-permute-done.3.g1
  32.2 0.0 all-to-all-done
  32.2 5.3 %shard_map.79 = (bf16[2048,2048]{1,0:T(8,128)(2,1)S(1)}, bf16[16,80,128]{2,1,0:T(8,128)(2,1)S(1)}, f32[32,128]{1,0:T(8,128)S(1)}, f32[16,24,128]{2,1,0:T(8,128)}, f32[16,128]{1,0:T(8,128)S(1)}) custom-call(bf16[4,80,128]{2,1,0:T(8,128)(2,1)S(1)} %pad_maximum_fusion.g0, bf16[4,80,128]{2,1,0:T(8,128)(2,1)S(1)} %collective-permute-done.3.g1, ...), custom_call_target="tpu_custom_call" | custom-call | flops 3355443200 | bytes 1048576 | tf_op jit(solution)/shard_map/pallas_call | solution.py:393
  37.6 3.3 %copy-done = bf16[2048,2048]{1,0:T(8,128)(2,1)} copy-done((bf16[2048,2048]{1,0:T(8,128)(2,1)}, bf16[2048,2048]{1,0:T(8,128)(2,1)S(1)}, u32[]{:S(2)}) %copy-start) | copy-done | bytes 8388632
  40.9 3.5 %all-to-all-start.1 = ((f32[16,24,128]{2,1,0:T(8,128)}), f32[16,24,128]{2,1,0:T(8,128)S(1)}, u32[]{:S(2)}, u32[]{:S(2)}) async-start(f32[16,24,128]{2,1,0:T(8,128)} %get-tuple-element.19), calls=%async_computation.1 | async-start | bytes 393216 | tf_op jit(solution)/shard_map/all_to_all | solution.py:371
  44.4 3.6 %collective-permute-start.7 = (f32[16,128]{1,0:T(8,128)S(1)}, f32[16,128]{1,0:T(8,128)S(1)}, u32[]{:S(2)}, u32[]{:S(2)}) collective-permute-start(f32[16,128]{1,0:T(8,128)S(1)} %get-tuple-element.20.own), channel_id=1, source_target_pairs={{0,32},{32,0},{1,33},{33,1},{2,34},{34,2},{3,35},{35,3},{4,36},{36... | collective-permute-start | bytes 24584 | tf_op jit(solution)/shard_map/ppermute | solution.py:375
  47.9 0.8 collective-permute-done.7.sib
  48.8 2.5 %all-to-all-done.1.got.wu_in = f32[16,24,128]{2,1,0:T(8,128)S(1)} async-done(((f32[16,24,128]{2,1,0:T(8,128)}), f32[16,24,128]{2,1,0:T(8,128)S(1)}, u32[]{:S(2)}, u32[]{:S(2)}) %all-to-all-start.1) | async-done | bytes 196640 | tf_op jit(solution)/shard_map/all_to_all | solution.py:371
  51.3 0.7 shard_map.81
  51.9 6.4 %all-to-all-start.2 = ((f32[8,24,128]{2,1,0:T(8,128)}), f32[8,24,128]{2,1,0:T(8,128)S(1)}, u32[]{:S(2)}, u32[]{:S(2)}) async-start(f32[8,24,128]{2,1,0:T(8,128)} %shard_map.81), calls=%async_computation.2 | async-start | bytes 196608 | tf_op jit(solution)/shard_map/all_to_all | solution.py:371
  58.3 3.4 %copy-done.1 = bf16[2048,2048]{1,0:T(8,128)(2,1)S(1)} copy-done((bf16[2048,2048]{1,0:T(8,128)(2,1)S(1)}, bf16[2048,2048]{1,0:T(8,128)(2,1)}, u32[]{:S(2)}) %copy-start.1) | copy-done | bytes 8388632
  61.7 4.2 %shard_map.80 = (f32[144,2048]{1,0:T(8,128)S(1)}, f32[144,2048]{1,0:T(8,128)S(1)}) custom-call(bf16[2048,2048]{1,0:T(8,128)(2,1)S(1)} %copy-done.1, bf16[16,80,128]{2,1,0:T(8,128)(2,1)S(1)} %get-tuple-element.16.xs, bf16[16,80,128]{2,1,0:T(8,128)(2,1)S(1)} %bitcast.10, f32[32,128]{1,0:T(8,128)S(1)} %get-tuple-element.17.cots), custom_call_target="tpu_custom_call" | custom-call | flops 4294967296 | bytes 1048576 | tf_op jit(solution)/shard_map/pallas_call | solution.py:413
  65.9 0.0 all-to-all-done.2.wv_in
  65.9 6.6 %collective-permute-start.8 = (f32[8,24,128]{2,1,0:T(8,128)S(1)}, f32[8,24,128]{2,1,0:T(8,128)S(1)}, u32[]{:S(2)}, u32[]{:S(2)}) collective-permute-start(f32[8,24,128]{2,1,0:T(8,128)S(1)} %all-to-all-done.2.wv_in), channel_id=1, source_target_pairs={{0,32},{32,0},{1,33},{33,1},{2,34},{34,2},{3,35},{35,3},{4,36},{36... | collective-permute-start | bytes 294920 | tf_op jit(solution)/shard_map/ppermute | solution.py:375
  72.5 3.4 %copy-done.2 = bf16[2048,2048]{1,0:T(8,128)(2,1)S(1)} copy-done((bf16[2048,2048]{1,0:T(8,128)(2,1)S(1)}, bf16[2048,2048]{1,0:T(8,128)(2,1)}, u32[]{:S(2)}) %copy-start.2) | copy-done | bytes 8388632
  75.9 2.7 %shard_map.82 = (f32[72,2048]{1,0:T(8,128)S(1)}, f32[32,128]{1,0:T(8,128)S(1)}) custom-call(bf16[2048,2048]{1,0:T(8,128)(2,1)S(1)} %copy-done.2, bf16[16,80,128]{2,1,0:T(8,128)(2,1)S(1)} %bitcast.11, f32[32,128]{1,0:T(8,128)S(1)} %get-tuple-element.17.cots, f32[16,24,128]{2,1,0:T(8,128)S(1)} %all-to-all-done.1.got.wu_in, ...), custom_call_target="tpu_custom_call" | custom-call | flops 2147483648 | bytes 1048576 | tf_op jit(solution)/shard_map/pallas_call | solution.py:435
  78.6 0.0 collective-permute-done.8.wv_sib
  78.6 0.2 shard_map.83
  78.8 0.0 copy-start.4
  78.8 0.9 copy-done.4
  79.7 3.6 %all-to-all-start.3 = ((bf16[16,144,128]{2,1,0:T(8,128)(2,1)}), bf16[16,144,128]{2,1,0:T(8,128)(2,1)S(1)}, u32[]{:S(2)}, u32[]{:S(2)}) async-start(bf16[16,144,128]{2,1,0:T(8,128)(2,1)} %copy-done.4), calls=%async_computation.3 | async-start | bytes 1179648 | tf_op jit(solution)/shard_map/all_to_all | solution.py:371
  83.3 0.0 copy-start.3
  83.3 3.4 %copy-done.3 = bf16[2048,2048]{1,0:T(8,128)(2,1)S(1)} copy-done((bf16[2048,2048]{1,0:T(8,128)(2,1)S(1)}, bf16[2048,2048]{1,0:T(8,128)(2,1)}, u32[]{:S(2)}) %copy-start.3) | copy-done | bytes 8388632
  86.7 3.4 %shard_map.85 = (bf16[8,144,128]{2,1,0:T(8,128)(2,1)S(1)}, bf16[8,144,128]{2,1,0:T(8,128)(2,1)S(1)}) custom-call(bf16[2048,2048]{1,0:T(8,128)(2,1)S(1)} %copy-done.3, bf16[16,80,128]{2,1,0:T(8,128)(2,1)S(1)} %get-tuple-element.16.xs, f32[32,128]{1,0:T(8,128)S(1)} %get-tuple-element.17.cots, f32[32,128]{1,0:T(8,128)S(1)} %get-tuple-element.22.sums, ...), custom_call_target="tpu_custom_call" | custom-call | flops 2147483648 | bytes 1048576 | tf_op jit(solution)/shard_map/pallas_call | solution.py:457
  90.1 0.2 collective-permute-start.9
  90.3 1.4 %collective-permute-done.9.got = bf16[8,144,128]{2,1,0:T(8,128)(2,1)S(1)} collective-permute-done((bf16[8,144,128]{2,1,0:T(8,128)(2,1)S(1)}, bf16[8,144,128]{2,1,0:T(8,128)(2,1)S(1)}, u32[]{:S(2)}, u32[]{:S(2)}) %collective-permute-start.9) | collective-permute-done | bytes 294944 | tf_op jit(solution)/shard_map/ppermute | solution.py:375
  91.8 0.1 shard_map.86.send_in
  91.9 2.5 %all-to-all-done.3.got = bf16[16,144,128]{2,1,0:T(8,128)(2,1)S(1)} async-done(((bf16[16,144,128]{2,1,0:T(8,128)(2,1)}), bf16[16,144,128]{2,1,0:T(8,128)(2,1)S(1)}, u32[]{:S(2)}, u32[]{:S(2)}) %all-to-all-start.3) | async-done | bytes 589856 | tf_op jit(solution)/shard_map/all_to_all | solution.py:371
  94.4 0.1 shard_map.87
  94.4 15.4 %all_to_all.25.got = bf16[8,144,128]{2,1,0:T(8,128)(2,1)S(1)} all-to-all(bf16[8,144,128]{2,1,0:T(8,128)(2,1)S(1)} %shard_map.87), channel_id=1, replica_groups=mesh['x'=4,'c'=2,'y'=4,'z'=8] {'z'}, dimensions={0} | all-to-all | bytes 589824 | tf_op jit(solution)/shard_map/all_to_all | solution.py:371
  109.8 3.8 %collective-permute-start.10 = (bf16[8,144,128]{2,1,0:T(8,128)(2,1)S(1)}, bf16[8,144,128]{2,1,0:T(8,128)(2,1)S(1)}, u32[]{:S(2)}, u32[]{:S(2)}) collective-permute-start(bf16[8,144,128]{2,1,0:T(8,128)(2,1)S(1)} %all_to_all.25.got), channel_id=1, source_target_pairs={{0,32},{32,0},{1,33},{33,1},{2,34},{34,2},{3,35},{35,3},{4,36},{36... | collective-permute-start | bytes 884744 | tf_op jit(solution)/shard_map/ppermute | solution.py:375
  113.6 0.1 shard_map.84.tot_s
  113.7 0.0 copy-start.6
  113.7 0.0 copy-start.8
  113.7 1.1 collective-permute-done.10.sib
  114.8 0.0 copy-done.6
  114.8 0.0 copy-done.8
  114.8 0.7 shard_map.89
  (7 shorter events, 0.1 us)
Async XLA Ops:
  0.6 4.4 %collective-permute-start.6 = (bf16[64,128]{1,0:T(8,128)(2,1)}, bf16[64,128]{1,0:T(8,128)(2,1)S(1)}, u32[]{:S(2)}, u32[]{:S(2)}) collective-permute-start(bf16[64,128]{1,0:T(8,128)(2,1)} %tgt_ref.1), channel_id=1, source_target_pairs={{0,32},{32,0},{1,33},{33,1},{2,34},{34,2},{3,35},{35,3},{4,36},{36... | collective-permute-start | bytes 49160 | tf_op jit(solution)/shard_map/ppermute | solution.py:375
  5.0 0.7 copy-start.7
  5.7 0.7 copy-start.11
  6.4 0.7 copy-start.12
  7.9 24.4 %all-to-all-start = ((bf16[8,160,128]{2,1,0:T(8,128)(2,1)}), bf16[8,160,128]{2,1,0:T(8,128)(2,1)S(1)}, u32[]{:S(2)}, u32[]{:S(2)}) async-start(bf16[8,160,128]{2,1,0:T(8,128)(2,1)} %shard_map.78), calls=%async_computation | async-start | bytes 655360 | tf_op jit(solution)/shard_map/all_to_all | solution.py:371
  14.3 0.7 copy-start.5
  15.0 0.7 copy-start.9
  15.8 0.7 copy-start.10
  16.5 3.7 %collective-permute-start.2 = (bf16[80,128]{1,0:T(8,128)(2,1)S(1)}, bf16[80,128]{1,0:T(8,128)(2,1)S(1)}, u32[]{:S(2)}, u32[]{:S(2)}) collective-permute-start(bf16[80,128]{1,0:T(8,128)(2,1)S(1)} %shard_map.77), channel_id=1, source_target_pairs={{0,192},{64,0},{128,64},{192,128},{1,193},{65,1},{129,65},{193,129... | collective-permute-start | bytes 61448 | tf_op jit(solution)/shard_map/ppermute | solution.py:375
  19.1 4.4 %collective-permute-start.1 = (bf16[80,128]{1,0:T(8,128)(2,1)S(1)}, bf16[80,128]{1,0:T(8,128)(2,1)S(1)}, u32[]{:S(2)}, u32[]{:S(2)}) collective-permute-start(bf16[80,128]{1,0:T(8,128)(2,1)S(1)} %shard_map.77), channel_id=1, source_target_pairs={{0,128},{64,192},{128,0},{192,64},{1,129},{65,193},{129,1},{193,65... | collective-permute-start | bytes 61448 | tf_op jit(solution)/shard_map/ppermute | solution.py:375
  19.6 4.1 %collective-permute-start = (bf16[80,128]{1,0:T(8,128)(2,1)S(1)}, bf16[80,128]{1,0:T(8,128)(2,1)S(1)}, u32[]{:S(2)}, u32[]{:S(2)}) collective-permute-start(bf16[80,128]{1,0:T(8,128)(2,1)S(1)} %shard_map.77), channel_id=1, source_target_pairs={{0,64},{64,128},{128,192},{192,0},{1,65},{65,129},{129,193},{193,1... | collective-permute-start | bytes 61448 | tf_op jit(solution)/shard_map/ppermute | solution.py:375
  23.7 4.3 %collective-permute-start.5 = (bf16[4,80,128]{2,1,0:T(8,128)(2,1)S(1)}, bf16[4,80,128]{2,1,0:T(8,128)(2,1)S(1)}, u32[]{:S(2)}, u32[]{:S(2)}) collective-permute-start(bf16[4,80,128]{2,1,0:T(8,128)(2,1)S(1)} %pad_maximum_fusion.g0), channel_id=1, source_target_pairs={{0,24},{8,0},{16,8},{24,16},{1,25},{9,1},{17,9},{25,17},{2,26},{10... | collective-permute-start | bytes 245768 | tf_op jit(solution)/shard_map/ppermute | solution.py:375
  26.5 4.9 %collective-permute-start.4 = (bf16[4,80,128]{2,1,0:T(8,128)(2,1)S(1)}, bf16[4,80,128]{2,1,0:T(8,128)(2,1)S(1)}, u32[]{:S(2)}, u32[]{:S(2)}) collective-permute-start(bf16[4,80,128]{2,1,0:T(8,128)(2,1)S(1)} %pad_maximum_fusion.g0), channel_id=1, source_target_pairs={{0,16},{8,24},{16,0},{24,8},{1,17},{9,25},{17,1},{25,9},{2,18},{10... | collective-permute-start | bytes 245768 | tf_op jit(solution)/shard_map/ppermute | solution.py:375
  26.9 5.3 %collective-permute-start.3 = (bf16[4,80,128]{2,1,0:T(8,128)(2,1)S(1)}, bf16[4,80,128]{2,1,0:T(8,128)(2,1)S(1)}, u32[]{:S(2)}, u32[]{:S(2)}) collective-permute-start(bf16[4,80,128]{2,1,0:T(8,128)(2,1)S(1)} %pad_maximum_fusion.g0), channel_id=1, source_target_pairs={{0,8},{8,16},{16,24},{24,0},{1,9},{9,17},{17,25},{25,1},{2,10},{10... | collective-permute-start | bytes 245768 | tf_op jit(solution)/shard_map/ppermute | solution.py:375
  37.6 3.3 %copy-start = (bf16[2048,2048]{1,0:T(8,128)(2,1)}, bf16[2048,2048]{1,0:T(8,128)(2,1)S(1)}, u32[]{:S(2)}) copy-start(bf16[2048,2048]{1,0:T(8,128)(2,1)S(1)} %get-tuple-element.15.plan) | copy-start | bytes 25165828
  40.9 10.4 %all-to-all-start.1 = ((f32[16,24,128]{2,1,0:T(8,128)}), f32[16,24,128]{2,1,0:T(8,128)S(1)}, u32[]{:S(2)}, u32[]{:S(2)}) async-start(f32[16,24,128]{2,1,0:T(8,128)} %get-tuple-element.19), calls=%async_computation.1 | async-start | bytes 393216 | tf_op jit(solution)/shard_map/all_to_all | solution.py:371
  44.4 4.4 %collective-permute-start.7 = (f32[16,128]{1,0:T(8,128)S(1)}, f32[16,128]{1,0:T(8,128)S(1)}, u32[]{:S(2)}, u32[]{:S(2)}) collective-permute-start(f32[16,128]{1,0:T(8,128)S(1)} %get-tuple-element.20.own), channel_id=1, source_target_pairs={{0,32},{32,0},{1,33},{33,1},{2,34},{34,2},{3,35},{35,3},{4,36},{36... | collective-permute-start | bytes 24584 | tf_op jit(solution)/shard_map/ppermute | solution.py:375
  51.9 13.9 %all-to-all-start.2 = ((f32[8,24,128]{2,1,0:T(8,128)}), f32[8,24,128]{2,1,0:T(8,128)S(1)}, u32[]{:S(2)}, u32[]{:S(2)}) async-start(f32[8,24,128]{2,1,0:T(8,128)} %shard_map.81), calls=%async_computation.2 | async-start | bytes 196608 | tf_op jit(solution)/shard_map/all_to_all | solution.py:371
  58.3 3.4 %copy-start.1 = (bf16[2048,2048]{1,0:T(8,128)(2,1)S(1)}, bf16[2048,2048]{1,0:T(8,128)(2,1)}, u32[]{:S(2)}) copy-start(bf16[2048,2048]{1,0:T(8,128)(2,1)} %copy-done) | copy-start | bytes 25165828
  65.9 12.7 %collective-permute-start.8 = (f32[8,24,128]{2,1,0:T(8,128)S(1)}, f32[8,24,128]{2,1,0:T(8,128)S(1)}, u32[]{:S(2)}, u32[]{:S(2)}) collective-permute-start(f32[8,24,128]{2,1,0:T(8,128)S(1)} %all-to-all-done.2.wv_in), channel_id=1, source_target_pairs={{0,32},{32,0},{1,33},{33,1},{2,34},{34,2},{3,35},{35,3},{4,36},{36... | collective-permute-start | bytes 294920 | tf_op jit(solution)/shard_map/ppermute | solution.py:375
  72.5 3.4 %copy-start.2 = (bf16[2048,2048]{1,0:T(8,128)(2,1)S(1)}, bf16[2048,2048]{1,0:T(8,128)(2,1)}, u32[]{:S(2)}) copy-start(bf16[2048,2048]{1,0:T(8,128)(2,1)} %copy-done) | copy-start | bytes 25165828
  78.8 0.9 copy-start.4
  79.7 14.7 %all-to-all-start.3 = ((bf16[16,144,128]{2,1,0:T(8,128)(2,1)}), bf16[16,144,128]{2,1,0:T(8,128)(2,1)S(1)}, u32[]{:S(2)}, u32[]{:S(2)}) async-start(bf16[16,144,128]{2,1,0:T(8,128)(2,1)} %copy-done.4), calls=%async_computation.3 | async-start | bytes 1179648 | tf_op jit(solution)/shard_map/all_to_all | solution.py:371
  83.3 3.4 %copy-start.3 = (bf16[2048,2048]{1,0:T(8,128)(2,1)S(1)}, bf16[2048,2048]{1,0:T(8,128)(2,1)}, u32[]{:S(2)}) copy-start(bf16[2048,2048]{1,0:T(8,128)(2,1)} %copy-done) | copy-start | bytes 25165828
  90.1 1.7 %collective-permute-start.9 = (bf16[8,144,128]{2,1,0:T(8,128)(2,1)S(1)}, bf16[8,144,128]{2,1,0:T(8,128)(2,1)S(1)}, u32[]{:S(2)}, u32[]{:S(2)}) collective-permute-start(bf16[8,144,128]{2,1,0:T(8,128)(2,1)S(1)} %get-tuple-element.27), channel_id=1, source_target_pairs={{0,32},{32,0},{1,33},{33,1},{2,34},{34,2},{3,35},{35,3},{4,36},{36... | collective-permute-start | bytes 884744 | tf_op jit(solution)/shard_map/ppermute | solution.py:375
  109.8 5.0 %collective-permute-start.10 = (bf16[8,144,128]{2,1,0:T(8,128)(2,1)S(1)}, bf16[8,144,128]{2,1,0:T(8,128)(2,1)S(1)}, u32[]{:S(2)}, u32[]{:S(2)}) collective-permute-start(bf16[8,144,128]{2,1,0:T(8,128)(2,1)S(1)} %all_to_all.25.got), channel_id=1, source_target_pairs={{0,32},{32,0},{1,33},{33,1},{2,34},{34,2},{3,35},{35,3},{4,36},{36... | collective-permute-start | bytes 884744 | tf_op jit(solution)/shard_map/ppermute | solution.py:375
  113.7 1.1 copy-start.6
  113.7 1.1 copy-start.8

commit v3 on v2

v3 whole, which is shorter than its diff:
```python
import jax
import jax.numpy as jnp
import numpy as np
from jax import lax
from jax.experimental import pallas as pl
from jax.experimental.pallas import tpu as pltpu
from jax.sharding import Mesh, PartitionSpec as P

blur_scale = 0.25
ridge_shift = 0.5
D = 64
L = 128
KP = 80
SA = ("x", "y")
TA = ("c", "z")
NA = 16
NB = 16
NZ = 8
ROWS = NA * L
COLS = NB * L
MB = 144
MW = 80
PR = 144
LOG2E = 1.4426950408889634
GAIN = 2.0 * LOG2E / (blur_scale * D)
SHIFT = 15.0 / GAIN
f32 = jnp.float32
bf16 = jnp.bfloat16
HI = lax.Precision.HIGHEST
VMEM = 24 * 1024 * 1024


def split3(v):
    hi = v.astype(bf16)
    rest = v - hi.astype(f32)
    mid = rest.astype(bf16)
    low = (rest - mid.astype(f32)).astype(bf16)
    return hi, mid, low


def join3(block, at):
    return (
        block[at : at + 1].astype(f32)
        + block[at + 1 : at + 2].astype(f32)
        + block[at + 2 : at + 3].astype(f32)
    )


def sds(shape, dtype):
    return jax.ShapeDtypeStruct(shape, dtype)


def call(kernel, out_shape, flops=0, **kw):
    cost = pl.CostEstimate(flops=flops, bytes_accessed=1 << 20, transcendentals=0)
    return pl.pallas_call(
        kernel,
        out_shape=out_shape,
        cost_estimate=cost,
        compiler_params=pltpu.CompilerParams(vmem_limit_bytes=VMEM),
        **kw,
    )


def encode(points, dual, cot, first):
    one = jnp.ones((3, L), f32)
    none = jnp.zeros((3, L), f32)
    wide = points.astype(f32)
    norm = jnp.sum(wide * wide, axis=0, keepdims=True)
    bias = (D / 2.0) * dual - 0.5 * norm
    if first:
        bias = bias - SHIFT
    biases = [t.astype(f32) for t in split3(bias)]
    cots = [t.astype(f32) for t in split3(cot)]
    tail = biases + [one] + cots + [none] if first else [one] + biases + [none] + cots
    tail = jnp.concatenate(tail + [jnp.zeros((4, L), f32)], axis=0).astype(bf16)
    return jnp.concatenate([points, tail], axis=0)


def cot_of(block, first):
    return join3(block, 70 if first else 73)


def encode_src(points, dual, cot, out):
    at = lax.axis_index("y") * 8 + lax.axis_index("z")
    out[...] = encode(points[...], dual[pl.ds(at, 1), :], cot[pl.ds(at, 1), :], True)


def encode_tgt(points, other, dual, cot, after, out):
    del after
    core = lax.axis_index("c")
    at = lax.axis_index("x") * 2
    own = points[...].astype(f32)
    sib = other[...].astype(f32)
    flip = core == 0
    low = jnp.where(flip, own, sib).astype(bf16)
    high = jnp.where(flip, sib, own).astype(bf16)
    both = jnp.concatenate(
        [
            encode(low, dual[pl.ds(at, 1), :], cot[pl.ds(at, 1), :], False),
            encode(high, dual[pl.ds(at + 1, 1), :], cot[pl.ds(at + 1, 1), :], False),
        ],
        axis=0,
    )
    out[...] = jnp.broadcast_to(both[None], out.shape)


def sweep_kernel(
    g0, g1, g2, g3, yg, plan, xs, cots, wu_out, wv_out, right, left, xt, ya, bub, bvb, row, col, ax, ay
):
    mx = lax.axis_index("x")
    my = lax.axis_index("y")
    for m, g in enumerate((g0, g1, g2, g3)):
        for k in range(4):
            at = lax.rem(mx + 4 - k, 4) * 4 + lax.rem(my + 4 - m, 4)
            xs[pl.ds(at, 1)] = g[k][None]
    pad = jnp.zeros((L - KP, L), f32)
    row_id = lax.broadcasted_iota(jnp.int32, (L, L), 0)
    pick = jnp.where((row_id >= 70) & (row_id < 73), 1.0, 0.0).astype(bf16)
    for k in range(NA):
        sl = slice(k * L, (k + 1) * L)
        block = xs[k]
        ax[:, sl] = stack_cot(block, cot_of(block, True))
        turned = jnp.concatenate([block.astype(f32), pad], axis=0).T.astype(bf16)
        xt[sl, :] = turned
        bub[sl, :] = jnp.dot(turned, pick, preferred_element_type=f32)
        cots[k : k + 1, :] = cot_of(block, True)
        other = yg[k]
        ay[:, sl] = stack_cot(other, cot_of(other, False))
        ya[:, sl] = jnp.concatenate([other, pad.astype(bf16)], axis=0)
        c = cot_of(other, False)
        cots[NA + k : NA + k + 1, :] = c
        bvb[:, sl] = jnp.broadcast_to(c, (8, L))
    rb, wide = 512, 256
    for r in range(ROWS // rb):
        rows = slice(r * rb, (r + 1) * rb)
        bu = bub[rows, :].reshape(rb // 8, 8, L)
        for n in range(COLS // wide):
            dots = jnp.dot(xt[rows, :], ya[:, n * wide : (n + 1) * wide], preferred_element_type=f32)
            p = jnp.exp2(dots * GAIN)
            plan[rows, n * wide : (n + 1) * wide] = p.astype(bf16)
            acc = None if n == 0 else row[rows, :].reshape(rb // 8, 8, L)
            for m in range(wide // L):
                sl = slice(n * wide + m * L, n * wide + (m + 1) * L)
                mixed = p[:, m * L : (m + 1) * L].reshape(rb // 8, 8, L) * (bu + bvb[:, sl][None])
                acc = mixed if acc is None else acc + mixed
                down = jnp.sum(mixed, axis=0)
                col[:, sl] = down if r == 0 else col[:, sl] + down
            row[rows, :] = acc.reshape(rb, L)
        part = lax.dot_general(ay[...], plan[rows, :], (((1,), (1,)), ((), ())), preferred_element_type=f32)
        for m in range(rb // L):
            at = r * (rb // L) + m
            right[:, at * L : (at + 1) * L] = fold_cot(part[:, m * L : (m + 1) * L], cots[at : at + 1, :])
    for n in range(COLS // wide):
        part = jnp.dot(ax[...], plan[:, n * wide : (n + 1) * wide], preferred_element_type=f32)
        for m in range(2):
            at = 2 * n + m
            c = cots[NA + at : NA + at + 1, :]
            left[:, at * L : (at + 1) * L] = fold_cot(part[:, m * L : (m + 1) * L], c)
    wu = jnp.concatenate(
        [jnp.sum(row[k * L : (k + 1) * L, :].T, axis=0, keepdims=True) for k in range(NA)], axis=0
    )
    wv = jnp.concatenate(
        [jnp.sum(col[:, k * L : (k + 1) * L], axis=0, keepdims=True) for k in range(NB)], axis=0
    )
    bu = cots[0:NA]
    bv = cots[NA : NA + NB]
    bw = jnp.sum(wu * bu + wv * bv)
    bb = jnp.sum(bu * bu) / NA + jnp.sum(bv * bv) / NB
    mark = lax.broadcasted_iota(jnp.int32, (8, L), 0)
    head = jnp.concatenate([wu, jnp.where(mark == 0, bw, bb)], axis=0)
    wu_out[...] = jnp.broadcast_to(head[None], wu_out.shape)
    wv_out[...] = wv


def stack_cot(block, c):
    pts = block[0:D]
    tail = [jnp.ones((1, L), f32)] + [t.astype(f32) for t in split3(c)] + [jnp.zeros((12, L), f32)]
    tail = jnp.concatenate(tail, axis=0).astype(bf16)
    return jnp.concatenate([pts, (pts.astype(f32) * c).astype(bf16), tail], axis=0)


def stack_one(block, c):
    tail = [t.astype(f32) for t in split3(c)] + [jnp.zeros((13, L), f32)]
    tail = jnp.concatenate(tail, axis=0).astype(bf16)
    return jnp.concatenate([(block[0:D].astype(f32) * c).astype(bf16), tail], axis=0)


def fold_cot(part, c):
    tail = part[2 * D : 2 * D + 16]
    pushed = tail[1:2] + tail[2:3] + tail[3:4]
    tail = jnp.concatenate([tail[0:1], pushed, jnp.zeros((14, L), f32)], axis=0)
    return jnp.concatenate([part[0:D], c * part[0:D] + part[D : 2 * D], tail], axis=0)


def relay_kernel(got, own, send):
    total = got[0]
    for k in range(1, got.shape[0]):
        total = total + got[k]
    whole = jnp.concatenate([own[...], total], axis=0)
    send[...] = jnp.broadcast_to(whole[None], send.shape)


def payload_of(t_b, t_r, s_r, rest):
    tail = jnp.concatenate([t.astype(f32) for t in split3(s_r)] + rest, axis=0)
    return jnp.concatenate([t_b, t_r, tail], axis=0).astype(bf16)


def left_kernel(plan, xs, cots, wu_in, wv_in, left, right_tail, mine, other, sums, scal, aw):
    wu = wu_in[0, 0:NA]
    for k in range(1, NA):
        wu = wu + wu_in[k, 0:NA]
    wv = wv_in[0]
    for k in range(1, NB):
        wv = wv + wv_in[k]
    bw = wv[NB : NB + 1]
    bb = wv[NB + 1 : NB + 2]
    wv = wv[0:NB]
    alpha = bb / (bw + ridge_shift * bb)
    scal[0:1, :] = alpha
    scal[1:2, :] = bb
    scal[2:8, :] = jnp.zeros((6, L), f32)
    sums[0:NA] = wu
    sums[NA : NA + NB] = wv
    bu, bv = cots[0:NA], cots[NA : NA + NB]
    ru = bu - alpha * (wu + ridge_shift * bu)
    rv = bv - alpha * (wv + ridge_shift * bv)
    rr = jnp.full((1, L), jnp.sum(ru * ru) / NA + jnp.sum(rv * rv) / NB, f32)
    for k in range(NA):
        w = wu[k : k + 1] + ridge_shift * bu[k : k + 1]
        aw[:, k * L : (k + 1) * L] = stack_one(xs[k], w)
    core = lax.axis_index("c")
    quad = jnp.zeros((1, L), f32)
    tails = []
    wide = 256
    for n in range(COLS // wide):
        part = jnp.dot(aw[...], plan[:, n * wide : (n + 1) * wide], preferred_element_type=f32)
        blocks = []
        for m in range(2):
            at = 2 * n + m
            sl = slice(at * L, (at + 1) * L)
            piece = part[:, m * L : (m + 1) * L]
            r = rv[at : at + 1]
            w = wv[at : at + 1] + ridge_shift * bv[at : at + 1]
            t_b = left[D : 2 * D, sl]
            t_r = t_b - alpha * (w * left[0:D, sl] + piece[0:D])
            pushed = piece[D : D + 1] + piece[D + 1 : D + 2] + piece[D + 2 : D + 3]
            pushed = left[2 * D + 1 : 2 * D + 2, sl] - alpha * pushed
            s_r = r * left[2 * D : 2 * D + 1, sl] + pushed
            quad = quad + r * (s_r + pushed)
            u = ru[at : at + 1]
            quad = quad + u * u * right_tail[0:1, sl]
            blocks.append(jnp.concatenate([t_b, t_r], axis=0).astype(bf16))
            tails.append(split3(s_r))

        @pl.when(core == 0)
        def _():
            mine[n, 0 : 2 * D] = blocks[0]
            other[n, 0 : 2 * D] = blocks[1]

        @pl.when(core != 0)
        def _():
            mine[n, 0 : 2 * D] = blocks[1]
            other[n, 0 : 2 * D] = blocks[0]

    quad = jnp.full((1, L), jnp.sum(quad), f32)
    extra = [t.astype(f32) for t in split3(quad) + split3(rr)] + [jnp.zeros((7, L), f32)]
    for n in range(NZ):
        pair = [
            jnp.concatenate([t.astype(f32) for t in tails[2 * n + m]] + extra, axis=0).astype(bf16) for m in range(2)
        ]

        @pl.when(core == 0)
        def _():
            mine[n, 2 * D :] = pair[0]
            other[n, 2 * D :] = pair[1]

        @pl.when(core != 0)
        def _():
            mine[n, 2 * D :] = pair[1]
            other[n, 2 * D :] = pair[0]


def right_kernel(plan, yg, cots, sums, right, out, aw):
    for k in range(NB):
        w = sums[NA + k : NA + k + 1, :] + ridge_shift * cots[NA + k : NA + k + 1, :]
        aw[:, k * L : (k + 1) * L] = stack_one(yg[k], w)
    wide = 256
    for r in range(ROWS // wide):
        part = lax.dot_general(
            aw[...], plan[r * wide : (r + 1) * wide, :], (((1,), (1,)), ((), ())), preferred_element_type=f32
        )
        for m in range(2):
            at = 2 * r + m
            sl = slice(at * L, (at + 1) * L)
            w = sums[at : at + 1, :] + ridge_shift * cots[at : at + 1, :]
            piece = part[:, m * L : (m + 1) * L]
            pushed = piece[D : D + 1] + piece[D + 1 : D + 2] + piece[D + 2 : D + 3]
            out[0:D, sl] = w * right[0:D, sl] + piece[0:D]
            out[D : D + 8, sl] = jnp.broadcast_to(pushed, (8, L))


def send_kernel(right, second, cots, sums, scal, mine, got, pay, send):
    alpha = scal[0:1, :]
    a = mine[0, 2 * D :].astype(f32)
    b = got[0, 2 * D :].astype(f32)
    quad = join3(a, 3) + join3(b, 3)
    rr = join3(a, 6) + join3(b, 6)
    extra = [t.astype(f32) for t in split3(quad) + split3(rr)] + [jnp.zeros((7, L), f32)]
    for k in range(NA):
        sl = slice(k * L, (k + 1) * L)
        c = cots[k : k + 1, :]
        r = c - alpha * (sums[k : k + 1, :] + ridge_shift * c)
        pushed = right[2 * D + 1 : 2 * D + 2, sl] - alpha * second[D : D + 1, sl]
        s_r = r * right[2 * D : 2 * D + 1, sl] + pushed
        t_b = right[D : 2 * D, sl]
        t_r = t_b - alpha * second[0:D, sl]
        pay[k] = payload_of(t_b, t_r, s_r, extra)
    for k in range(NZ):
        t = mine[k, 0 : 2 * D].astype(f32) + got[k, 0 : 2 * D].astype(f32)
        s = join3(mine[k, 2 * D :], 0) + join3(got[k, 2 * D :], 0)
        send[k] = payload_of(t[0:D], t[D:], s, [jnp.zeros((13, L), f32)])


def pass_kernel(got, send_in, tot, send):
    total = got[0].astype(f32)
    for k in range(1, NA):
        total = total + got[k].astype(f32)
    tot[...] = total
    quad = join3(total, 131)
    rr = join3(total, 134)
    extra = [t.astype(f32) for t in split3(quad) + split3(rr)]
    for k in range(NZ):
        tail = send_in[k].astype(f32)
        send[k] = jnp.concatenate([tail[0:3]] + extra + [tail[9:16]], axis=0).astype(bf16)


def final_kernel(tot_s, got, src_ref, tgt_ref, sums, scal, out_s, out_t):
    tot_t = got[0].astype(f32)
    for k in range(1, NZ):
        tot_t = tot_t + got[k].astype(f32)
    alpha = scal[0:1, :]
    bb = scal[1:2, :]
    rr = join3(tot_t, 134)
    quad = join3(tot_t, 131) + ridge_shift * rr
    ratio = rr / bb
    step = rr / (quad - ratio * rr / alpha)
    scale = 2.0 / (blur_scale * D)
    c_b = scale * (alpha + step * ratio)
    c_r = scale * step
    si = lax.axis_index("x") * 4 + lax.axis_index("y")
    ti = lax.axis_index("z") * 2 + lax.axis_index("c")

    def combine(points, tot, s_b, out):
        s = c_b * s_b + c_r * join3(tot, 128)
        out[...] = points[...].astype(f32) * s - (c_b * tot[0:D] + c_r * tot[D : 2 * D])

    combine(src_ref, tot_s[...], sums[pl.ds(si, 1), :], out_s)
    combine(tgt_ref, tot_t, sums[pl.ds(NA + ti, 1), :], out_t)


def exchange(v, axes):
    return lax.all_to_all(v, axes, 0, 0, tiled=True)


def shift(v, axis, n, k):
    return lax.ppermute(v, axis, [(i, (i + k) % n) for i in range(n)])


def swap(v):
    return shift(v, "c", 2, 1)


def body(src_points, tgt_points, src_dual, tgt_dual, src_cot, tgt_cot):
    whole = lambda v: v.reshape(-1, L)
    own = call(encode_src, sds((KP, L), bf16))(src_points, whole(src_dual), whole(src_cot))
    g0 = jnp.stack([own] + [shift(own, "x", 4, k) for k in (1, 2, 3)], axis=0)
    send = call(encode_tgt, sds((NZ, 2 * KP, L), bf16))(
        tgt_points, swap(tgt_points), whole(tgt_dual), whole(tgt_cot), g0
    )
    yg = exchange(send, "z").reshape(NB, KP, L)
    g1, g2, g3 = [shift(g0, "y", 4, k) for k in (1, 2, 3)]
    unit = ROWS * COLS * 2
    vm = pltpu.VMEM
    plan, xs, cots, wu, wv, right, left = call(
        sweep_kernel,
        (
            sds((ROWS, COLS), bf16),
            sds((NA, KP, L), bf16),
            sds((NA + NB, L), f32),
            sds((NA, 24, L), f32),
            sds((NB, L), f32),
            sds((MB, ROWS), f32),
            sds((MB, COLS), f32),
        ),
        flops=unit * 900,
        scratch_shapes=[
            vm((ROWS, L), bf16),
            vm((L, COLS), bf16),
            vm((ROWS, L), f32),
            vm((8, COLS), f32),
            vm((ROWS, L), f32),
            vm((8, COLS), f32),
            vm((MB, ROWS), bf16),
            vm((MB, COLS), bf16),
        ],
    )(g0, g1, g2, g3, yg)
    wu = exchange(wu, SA)

    def tail(n, rows, at):
        return pl.BlockSpec((n, rows, L), lambda i: (0, at, 0))

    def full(*shape):
        return pl.BlockSpec(shape, lambda i: (0,) * len(shape))

    send = call(
        relay_kernel,
        sds((NB, 24, L), f32),
        grid=(1,),
        in_specs=[tail(NA, 8, 2), full(NB, L)],
        out_specs=full(NB, 24, L),
    )(wu, wv)
    wv = exchange(send, TA)
    half = sds((NZ, PR, L), bf16)
    mine, other, sums, scal = call(
        left_kernel,
        (half, half, sds((NA + NB, L), f32), sds((8, L), f32)),
        flops=unit * 256,
        grid=(1,),
        in_specs=[
            full(ROWS, COLS),
            full(NA, KP, L),
            full(NA + NB, L),
            full(NA, 24, L),
            full(NB, 24, L),
            full(MB, COLS),
            pl.BlockSpec((8, ROWS), lambda i: (2 * D // 8, 0)),
        ],
        out_specs=(full(NZ, PR, L), full(NZ, PR, L), full(NA + NB, L), full(8, L)),
        scratch_shapes=[vm((MW, ROWS), bf16)],
    )(plan, xs, cots, wu, wv, left, right)
    got = swap(other)
    second = call(
        right_kernel,
        sds((D + 8, ROWS), f32),
        flops=unit * 256,
        scratch_shapes=[vm((MW, COLS), bf16)],
    )(plan, yg, cots, sums, right)
    pay, send = call(send_kernel, (sds((NA, PR, L), bf16), half))(right, second, cots, sums, scal, mine, got)
    got_s = exchange(pay, SA)
    tot_s, send = call(
        pass_kernel,
        (sds((PR, L), f32), half),
        grid=(1,),
        in_specs=[full(NA, PR, L), tail(NZ, 16, 8)],
        out_specs=(full(PR, L), tail(NZ, 16, 8)),
        input_output_aliases={1: 1},
    )(got_s, send)
    got_t = exchange(send, "z")
    return call(final_kernel, (sds((D, L), f32), sds((D, L), f32)))(
        tot_s, got_t, src_points, tgt_points, sums, scal
    )


def solution(mesh):
    grid = Mesh(mesh.devices.reshape(4, 2, 4, 8), ("x", "c", "y", "z"))
    in_specs = (
        P(None, ("x", "c", "y", "z")),
        P(None, ("y", "z", "x", "c")),
        P(("x", "c")),
        P(("y", "z")),
        P(("x", "c")),
        P(("y", "z")),
    )
    out_specs = (P(None, ("x", "c", "y", "z")), P(None, ("y", "z", "x", "c")))
    return jax.shard_map(body, mesh=grid, in_specs=in_specs, out_specs=out_specs, check_vma=False)
```

time: 116 us -> 108 us (0.931)
  blocking collectives: 15.4 us -> 57.9 us
  starting transfers between devices: 44.9 us -> 19.3 us
  local copies, waits for them, and re-layouts: 18.5 us -> 4.24 us
  waiting for transfers between devices: 17.6 us -> 8.15 us
  Pallas kernels: 18.3 us -> 16.8 us
    all_to_all x1 -> x4, blocking collectives: 15.4 us -> 57.9 us  [exchange(): return lax.all_to_all(v, axes, 0, 0, tiled=True)]
    unnamed x26 -> x16, local copies, waits for them, and re-layouts: 18.5 us -> 4.24 us
    ppermute x11 -> x8, starting transfers between devices: 25 us -> 11.1 us  [shift(): return lax.ppermute(v, axis, [(i, (i + k) % n) for i in range(n)])]
    all_to_all x4 -> x1, starting transfers between devices: 19.9 us -> 8.19 us  [exchange(): return lax.all_to_all(v, axes, 0, 0, tiled=True)]
    ppermute x11 -> x8, waiting for transfers between devices: 12.5 us -> 6.65 us  [shift(): return lax.ppermute(v, axis, [(i, (i + k) % n) for i in range(n)])]
    pallas_call x10 -> x6, Pallas kernels: 12.1 us -> 7.45 us  [the longest x1 3.72 us: body(): call(left_kernel, (half, half, sds((NA + NB, L), f32), sds((8, L), f32)),...]
    all_to_all x4 -> x1, waiting for transfers between devices: 5.03 us -> 1.49 us  [exchange(): return lax.all_to_all(v, axes, 0, 0, tiled=True)]
    pallas_call x1, Pallas kernels: 5.35 us -> 8.51 us  [body(): call(sweep_kernel, (sds((ROWS, COLS), bf16), sds((NA, KP, L), bf16), sds(...]
  transfers between devices with their start and end apart: 15 -> 9, of which waited for: 11 -> 6; matrix products, arithmetic and copies ran while one was open for 0% -> 0% of each run, Pallas kernels for 9% -> 3%
where the time goes in v3:
time: 108 us; the launch traced here: 107 us
  blocking collectives  57.9 us (54%)
  starting transfers between devices  19.3 us (18%)
  Pallas kernels  16.8 us (16%)
  waiting for transfers between devices  8.15 us (8%)
  local copies, waits for them, and re-layouts  4.24 us (4%)
    all_to_all x4, blocking collectives, exchange(): return lax.all_to_all(v, axes, 0, 0, tiled=True)  57.9 us
    ppermute x8, starting transfers between devices, shift(): return lax.ppermute(v, axis, [(i, (i + k) % n) for i in range(n)])  11.1 us
    pallas_call x1, Pallas kernels, body(): call(sweep_kernel, (sds((ROWS, COLS), bf16), sds((NA, KP, L), bf16), sds(...  8.51 us
    all_to_all x1, starting transfers between devices, exchange(): return lax.all_to_all(v, axes, 0, 0, tiled=True)  8.19 us
    ppermute x8, waiting for transfers between devices, shift(): return lax.ppermute(v, axis, [(i, (i + k) % n) for i in range(n)])  6.65 us
    unnamed x16, local copies, waits for them, and re-layouts  4.24 us
    pallas_call x1, Pallas kernels, body(): call(left_kernel, (half, half, sds((NA + NB, L), f32), sds((8, L), f32)),...  3.72 us
    pallas_call x1, Pallas kernels, body(): call(right_kernel, sds((D + 8, ROWS), f32), flops=unit * 256, scratch_sha...  2.7 us
  transfers between devices with their start and end apart: 9, of which 6 were waited for; matrix products, arithmetic and copies ran while one was open for 0% of the time, Pallas kernels for 3%

profile of v3, /device:TPU:1, one launch (start us, length us, event | category | flops | bytes accessed | tf_op | source)
XLA Modules:
  0.0 107.1 jit_solution(557639656251032453)
XLA Ops:
  0.6 0.0 copy-start.2
  0.6 0.7 copy-done.2
  1.4 0.0 copy-start.4
  1.4 0.7 copy-done.4
  2.1 0.0 copy-start.5
  2.1 0.7 copy-done.5
  2.8 3.4 %collective-permute-start.2 = (bf16[80,128]{1,0:T(8,128)(2,1)S(1)}, bf16[80,128]{1,0:T(8,128)(2,1)S(1)}, u32[]{:S(2)}, u32[]{:S(2)}) collective-permute-start(bf16[80,128]{1,0:T(8,128)(2,1)S(1)} %shard_map.77), channel_id=1, source_target_pairs={{0,192},{64,0},{128,64},{192,128},{1,193},{65,1},{129,65},{193,129... | collective-permute-start | bytes 61448 | tf_op jit(solution)/shard_map/ppermute | solution.py:366
  6.2 0.5 collective-permute-start.1
  6.7 0.6 collective-permute-start
  7.3 1.5 %collective-permute-start.6 = (bf16[64,128]{1,0:T(8,128)(2,1)}, bf16[64,128]{1,0:T(8,128)(2,1)S(1)}, u32[]{:S(2)}, u32[]{:S(2)}) collective-permute-start(bf16[64,128]{1,0:T(8,128)(2,1)} %tgt_ref.1), channel_id=1, source_target_pairs={{0,32},{32,0},{1,33},{33,1},{2,34},{34,2},{3,35},{35,3},{4,36},{36... | collective-permute-start | bytes 49160 | tf_op jit(solution)/shard_map/ppermute | solution.py:366
  8.8 0.0 collective-permute-done.2
  8.8 1.5 %collective-permute-done.1 = bf16[80,128]{1,0:T(8,128)(2,1)S(1)} collective-permute-done((bf16[80,128]{1,0:T(8,128)(2,1)S(1)}, bf16[80,128]{1,0:T(8,128)(2,1)S(1)}, u32[]{:S(2)}, u32[]{:S(2)}) %collective-permute-start.1) | collective-permute-done | bytes 20512 | tf_op jit(solution)/shard_map/ppermute | solution.py:366
  10.3 0.2 collective-permute-done
  10.6 0.0 collective-permute-done.6.other
  10.6 0.0 copy-start
  10.6 0.7 copy-done
  11.3 0.0 copy-start.6
  11.3 0.7 copy-done.6
  12.0 0.0 copy-start.7
  12.0 0.7 copy-done.7
  12.7 0.8 shard_map.78
  13.5 8.2 %all-to-all-start = ((bf16[8,160,128]{2,1,0:T(8,128)(2,1)}), bf16[8,160,128]{2,1,0:T(8,128)(2,1)S(1)}, u32[]{:S(2)}, u32[]{:S(2)}) async-start(bf16[8,160,128]{2,1,0:T(8,128)(2,1)} %shard_map.78), calls=%async_computation | async-start | bytes 655360 | tf_op jit(solution)/shard_map/all_to_all | solution.py:362
  21.6 2.7 %collective-permute-start.5 = (bf16[4,80,128]{2,1,0:T(8,128)(2,1)S(1)}, bf16[4,80,128]{2,1,0:T(8,128)(2,1)S(1)}, u32[]{:S(2)}, u32[]{:S(2)}) collective-permute-start(bf16[4,80,128]{2,1,0:T(8,128)(2,1)S(1)} %pad_maximum_fusion.after.g0), channel_id=1, source_target_pairs={{0,24},{8,0},{16,8},{24,16},{1,25},{9,1},{17,9},{25,17},{2,26},{10... | collective-permute-start | bytes 245768 | tf_op jit(solution)/shard_map/ppermute | solution.py:366
  24.4 0.3 collective-permute-start.4
  24.7 0.7 collective-permute-start.3
  25.4 0.4 collective-permute-done.5.g3
  25.9 3.4 %collective-permute-done.4.g2 = bf16[4,80,128]{2,1,0:T(8,128)(2,1)S(1)} collective-permute-done((bf16[4,80,128]{2,1,0:T(8,128)(2,1)S(1)}, bf16[4,80,128]{2,1,0:T(8,128)(2,1)S(1)}, u32[]{:S(2)}, u32[]{:S(2)}) %collective-permute-start.4) | collective-permute-done | bytes 81952 | tf_op jit(solution)/shard_map/ppermute | solution.py:366
  29.3 1.1 %collective-permute-done.3.g1 = bf16[4,80,128]{2,1,0:T(8,128)(2,1)S(1)} collective-permute-done((bf16[4,80,128]{2,1,0:T(8,128)(2,1)S(1)}, bf16[4,80,128]{2,1,0:T(8,128)(2,1)S(1)}, u32[]{:S(2)}, u32[]{:S(2)}) %collective-permute-start.3) | collective-permute-done | bytes 81952 | tf_op jit(solution)/shard_map/ppermute | solution.py:366
  30.4 1.5 %all-to-all-done = bf16[8,160,128]{2,1,0:T(8,128)(2,1)S(1)} async-done(((bf16[8,160,128]{2,1,0:T(8,128)(2,1)}), bf16[8,160,128]{2,1,0:T(8,128)(2,1)S(1)}, u32[]{:S(2)}, u32[]{:S(2)}) %all-to-all-start) | async-done | bytes 327712 | tf_op jit(solution)/shard_map/all_to_all | solution.py:362
  31.8 8.5 %shard_map.79 = (bf16[2048,2048]{1,0:T(8,128)(2,1)S(1)}, bf16[16,80,128]{2,1,0:T(8,128)(2,1)S(1)}, f32[32,128]{1,0:T(8,128)S(1)}, f32[16,24,128]{2,1,0:T(8,128)S...) custom-call(bf16[4,80,128]{2,1,0:T(8,128)(2,1)S(1)} %pad_maximum_fusion.after.g0, ...), custom_call_target="tpu_custom_call" | custom-call | flops 7549747200 | bytes 1048576 | tf_op jit(solution)/shard_map/pallas_call | solution.py:384
  40.4 13.1 %all_to_all.25.got.wu_in = f32[16,24,128]{2,1,0:T(8,128)S(1)} all-to-all(f32[16,24,128]{2,1,0:T(8,128)S(1)} %get-tuple-element.21), channel_id=1, replica_groups=mesh['x'=4,'c'=2,'y'=4,'z'=8] {'x','y'}, dimensions={0} | all-to-all | bytes 393216 | tf_op jit(solution)/shard_map/all_to_all | solution.py:362
  53.5 15.9 %all_to_all.26.wv_in = f32[16,24,128]{2,1,0:T(8,128)S(1)} all-to-all(f32[16,24,128]{2,1,0:T(8,128)S(1)} %shard_map.80), channel_id=1, replica_groups=mesh['x'=4,'c'=2,'y'=4,'z'=8] {'c','z'}, dimensions={0} | all-to-all | bytes 393216 | tf_op jit(solution)/shard_map/all_to_all | solution.py:362
  69.4 3.7 %shard_map.81 = (bf16[8,144,128]{2,1,0:T(8,128)(2,1)S(1)}, bf16[8,144,128]{2,1,0:T(8,128)(2,1)S(1)}, f32[32,128]{1,0:T(8,128)S(1)}, f32[8,128]{1,0:T(8,128)S(1)}) custom-call(bf16[2048,2048]{1,0:T(8,128)(2,1)S(1)} %get-tuple-element.18.plan, bf16[16,80,128]{2,1,0:T(8,128)(2,1)S(1)} %get-tuple-element.20.xs, f32[32,128]{1,0:T(8,128)S(1)} %get-tuple-element.19.cots, ...), custom_call_target="tpu_custom_call" | custom-call | flops 2147483648 | bytes 1048576 | tf_op jit(solution)/shard_map/pallas_call | solution.py:424
  73.1 1.3 %collective-permute-start.7 = (bf16[8,144,128]{2,1,0:T(8,128)(2,1)S(1)}, bf16[8,144,128]{2,1,0:T(8,128)(2,1)S(1)}, u32[]{:S(2)}, u32[]{:S(2)}) collective-permute-start(bf16[8,144,128]{2,1,0:T(8,128)(2,1)S(1)} %get-tuple-element.27), channel_id=1, source_target_pairs={{0,32},{32,0},{1,33},{33,1},{2,34},{34,2},{3,35},{35,3},{4,36},{36... | collective-permute-start | bytes 884744 | tf_op jit(solution)/shard_map/ppermute | solution.py:366
  74.4 2.7 %shard_map.82.second = f32[72,2048]{1,0:T(8,128)S(1)} custom-call(bf16[2048,2048]{1,0:T(8,128)(2,1)S(1)} %get-tuple-element.18.plan, bf16[16,80,128]{2,1,0:T(8,128)(2,1)S(1)} %bitcast.10, f32[32,128]{1,0:T(8,128)S(1)} %get-tuple-element.19.cots, f32[32,128]{1,0:T(8,128)S(1)} %get-tuple-element.24.sums, f32[144,2048]{1,0:T(8,128)S(1)} %get-tuple-element.17.right_tail.right), custom_call_target="tpu_custom_call" | custom-call | flops 2147483648 | bytes 1048576 | tf_op jit(solution)/shard_map/pallas_call | solution.py:442
  77.1 0.0 collective-permute-done.7.got
  77.1 0.2 shard_map.83
  77.3 0.0 copy-start.1
  77.3 0.0 copy-start.3
  77.3 15.1 %all_to_all.27.got = bf16[16,144,128]{2,1,0:T(8,128)(2,1)S(1)} all-to-all(bf16[16,144,128]{2,1,0:T(8,128)(2,1)S(1)} %get-tuple-element.28), channel_id=1, replica_groups=mesh['x'=4,'c'=2,'y'=4,'z'=8] {'x','y'}, dimensions={0} | all-to-all | bytes 1179648 | tf_op jit(solution)/shard_map/all_to_all | solution.py:362
  92.4 0.1 shard_map.84
  92.5 13.9 %all_to_all.28.got = bf16[8,144,128]{2,1,0:T(8,128)(2,1)S(1)} all-to-all(bf16[8,144,128]{2,1,0:T(8,128)(2,1)S(1)} %get-tuple-element.31), channel_id=1, replica_groups=mesh['x'=4,'c'=2,'y'=4,'z'=8] {'z'}, dimensions={0} | all-to-all | bytes 589824 | tf_op jit(solution)/shard_map/all_to_all | solution.py:362
  106.4 0.0 copy-done.1
  106.4 0.0 copy-done.3
  106.4 0.7 shard_map.85
  (3 shorter events, 0.1 us)
Async XLA Ops:
  0.6 0.7 copy-start.2
  1.4 0.7 copy-start.4
  2.1 0.7 copy-start.5
  2.8 6.0 %collective-permute-start.2 = (bf16[80,128]{1,0:T(8,128)(2,1)S(1)}, bf16[80,128]{1,0:T(8,128)(2,1)S(1)}, u32[]{:S(2)}, u32[]{:S(2)}) collective-permute-start(bf16[80,128]{1,0:T(8,128)(2,1)S(1)} %shard_map.77), channel_id=1, source_target_pairs={{0,192},{64,0},{128,64},{192,128},{1,193},{65,1},{129,65},{193,129... | collective-permute-start | bytes 61448 | tf_op jit(solution)/shard_map/ppermute | solution.py:366
  6.2 4.1 %collective-permute-start.1 = (bf16[80,128]{1,0:T(8,128)(2,1)S(1)}, bf16[80,128]{1,0:T(8,128)(2,1)S(1)}, u32[]{:S(2)}, u32[]{:S(2)}) collective-permute-start(bf16[80,128]{1,0:T(8,128)(2,1)S(1)} %shard_map.77), channel_id=1, source_target_pairs={{0,128},{64,192},{128,0},{192,64},{1,129},{65,193},{129,1},{193,65... | collective-permute-start | bytes 61448 | tf_op jit(solution)/shard_map/ppermute | solution.py:366
  6.7 3.8 %collective-permute-start = (bf16[80,128]{1,0:T(8,128)(2,1)S(1)}, bf16[80,128]{1,0:T(8,128)(2,1)S(1)}, u32[]{:S(2)}, u32[]{:S(2)}) collective-permute-start(bf16[80,128]{1,0:T(8,128)(2,1)S(1)} %shard_map.77), channel_id=1, source_target_pairs={{0,64},{64,128},{128,192},{192,0},{1,65},{65,129},{129,193},{193,1... | collective-permute-start | bytes 61448 | tf_op jit(solution)/shard_map/ppermute | solution.py:366
  7.3 3.3 %collective-permute-start.6 = (bf16[64,128]{1,0:T(8,128)(2,1)}, bf16[64,128]{1,0:T(8,128)(2,1)S(1)}, u32[]{:S(2)}, u32[]{:S(2)}) collective-permute-start(bf16[64,128]{1,0:T(8,128)(2,1)} %tgt_ref.1), channel_id=1, source_target_pairs={{0,32},{32,0},{1,33},{33,1},{2,34},{34,2},{3,35},{35,3},{4,36},{36... | collective-permute-start | bytes 49160 | tf_op jit(solution)/shard_map/ppermute | solution.py:366
  10.6 0.7 copy-start
  11.3 0.7 copy-start.6
  12.0 0.7 copy-start.7
  13.5 18.4 %all-to-all-start = ((bf16[8,160,128]{2,1,0:T(8,128)(2,1)}), bf16[8,160,128]{2,1,0:T(8,128)(2,1)S(1)}, u32[]{:S(2)}, u32[]{:S(2)}) async-start(bf16[8,160,128]{2,1,0:T(8,128)(2,1)} %shard_map.78), calls=%async_computation | async-start | bytes 655360 | tf_op jit(solution)/shard_map/all_to_all | solution.py:362
  21.6 4.2 %collective-permute-start.5 = (bf16[4,80,128]{2,1,0:T(8,128)(2,1)S(1)}, bf16[4,80,128]{2,1,0:T(8,128)(2,1)S(1)}, u32[]{:S(2)}, u32[]{:S(2)}) collective-permute-start(bf16[4,80,128]{2,1,0:T(8,128)(2,1)S(1)} %pad_maximum_fusion.after.g0), channel_id=1, source_target_pairs={{0,24},{8,0},{16,8},{24,16},{1,25},{9,1},{17,9},{25,17},{2,26},{10... | collective-permute-start | bytes 245768 | tf_op jit(solution)/shard_map/ppermute | solution.py:366
  24.4 4.9 %collective-permute-start.4 = (bf16[4,80,128]{2,1,0:T(8,128)(2,1)S(1)}, bf16[4,80,128]{2,1,0:T(8,128)(2,1)S(1)}, u32[]{:S(2)}, u32[]{:S(2)}) collective-permute-start(bf16[4,80,128]{2,1,0:T(8,128)(2,1)S(1)} %pad_maximum_fusion.after.g0), channel_id=1, source_target_pairs={{0,16},{8,24},{16,0},{24,8},{1,17},{9,25},{17,1},{25,9},{2,18},{10... | collective-permute-start | bytes 245768 | tf_op jit(solution)/shard_map/ppermute | solution.py:366
  24.7 5.6 %collective-permute-start.3 = (bf16[4,80,128]{2,1,0:T(8,128)(2,1)S(1)}, bf16[4,80,128]{2,1,0:T(8,128)(2,1)S(1)}, u32[]{:S(2)}, u32[]{:S(2)}) collective-permute-start(bf16[4,80,128]{2,1,0:T(8,128)(2,1)S(1)} %pad_maximum_fusion.after.g0), channel_id=1, source_target_pairs={{0,8},{8,16},{16,24},{24,0},{1,9},{9,17},{17,25},{25,1},{2,10},{10... | collective-permute-start | bytes 245768 | tf_op jit(solution)/shard_map/ppermute | solution.py:366
  73.1 4.0 %collective-permute-start.7 = (bf16[8,144,128]{2,1,0:T(8,128)(2,1)S(1)}, bf16[8,144,128]{2,1,0:T(8,128)(2,1)S(1)}, u32[]{:S(2)}, u32[]{:S(2)}) collective-permute-start(bf16[8,144,128]{2,1,0:T(8,128)(2,1)S(1)} %get-tuple-element.27), channel_id=1, source_target_pairs={{0,32},{32,0},{1,33},{33,1},{2,34},{34,2},{3,35},{35,3},{4,36},{36... | collective-permute-start | bytes 884744 | tf_op jit(solution)/shard_map/ppermute | solution.py:366
  77.3 29.1 %copy-start.1 = (bf16[64,128]{1,0:T(8,128)(2,1)S(1)}, bf16[64,128]{1,0:T(8,128)(2,1)}, u32[]{:S(2)}) copy-start(bf16[64,128]{1,0:T(8,128)(2,1)} %tgt_ref.1) | copy-start | bytes 49156
  77.3 29.1 %copy-start.3 = (bf16[64,128]{1,0:T(8,128)(2,1)S(1)}, bf16[64,128]{1,0:T(8,128)(2,1)}, u32[]{:S(2)}) copy-start(bf16[64,128]{1,0:T(8,128)(2,1)} %src_ref.1) | copy-start | bytes 49156

commit v4 on v3

v4 whole, which is shorter than its diff:
```python
import jax
import jax.numpy as jnp
import numpy as np
from jax import lax
from jax.experimental import pallas as pl
from jax.experimental.pallas import tpu as pltpu
from jax.sharding import Mesh, PartitionSpec as P

blur_scale = 0.25
ridge_shift = 0.5
D = 64
L = 128
KP = 80
SA = ("x", "y")
NA = 16
NB = 16
NZ = 8
ROWS = NA * L
COLS = NB * L
MA = 208
PR = 144
LOG2E = 1.4426950408889634
GAIN = 2.0 * LOG2E / (blur_scale * D)
SHIFT = 15.0 / GAIN
f32 = jnp.float32
bf16 = jnp.bfloat16
HI = lax.Precision.HIGHEST
VMEM = 24 * 1024 * 1024
WIDE = 60 * 1024 * 1024


def split3(v):
    hi = v.astype(bf16)
    rest = v - hi.astype(f32)
    mid = rest.astype(bf16)
    low = (rest - mid.astype(f32)).astype(bf16)
    return hi, mid, low


def join3(block, at):
    return (
        block[at : at + 1].astype(f32)
        + block[at + 1 : at + 2].astype(f32)
        + block[at + 2 : at + 3].astype(f32)
    )


def sds(shape, dtype):
    return jax.ShapeDtypeStruct(shape, dtype)


def call(kernel, out_shape, flops=0, limit=VMEM, **kw):
    cost = pl.CostEstimate(flops=flops, bytes_accessed=1 << 20, transcendentals=0)
    return pl.pallas_call(
        kernel,
        out_shape=out_shape,
        cost_estimate=cost,
        compiler_params=pltpu.CompilerParams(vmem_limit_bytes=limit),
        **kw,
    )


def rows16(rows):
    mark = lax.broadcasted_iota(jnp.int32, (16, L), 0)
    out = jnp.zeros((16, L), f32)
    for k, row in enumerate(rows):
        out = jnp.where(mark == k, jnp.broadcast_to(row, (16, L)), out)
    return out


def parts(v):
    return [t.astype(f32) for t in split3(v)]


def encode(points, dual, cot, first):
    one = [jnp.ones((1, L), f32)] * 3
    none = [jnp.zeros((1, L), f32)] * 3
    wide = points.astype(f32)
    norm = jnp.sum(wide * wide, axis=0, keepdims=True)
    bias = (D / 2.0) * dual - 0.5 * norm
    if first:
        bias = bias - SHIFT
    tail = parts(bias) + one + parts(cot) + none if first else one + parts(bias) + none + parts(cot)
    return jnp.concatenate([points, rows16(tail).astype(bf16)], axis=0)


def cot_of(block, first):
    return join3(block, 70 if first else 73)


def encode_kernel(src, tgt, other, src_dual, src_cot, tgt_dual, tgt_cot, own, out):
    at = lax.axis_index("y") * 8 + lax.axis_index("z")
    own[...] = encode(src[...], src_dual[pl.ds(at, 1), :], src_cot[pl.ds(at, 1), :], True)
    at = lax.axis_index("x") * 2
    flip = lax.axis_index("c") == 0
    near = tgt[...].astype(f32)
    far = other[...].astype(f32)
    low = jnp.where(flip, near, far).astype(bf16)
    high = jnp.where(flip, far, near).astype(bf16)
    both = jnp.concatenate(
        [
            encode(low, tgt_dual[pl.ds(at, 1), :], tgt_cot[pl.ds(at, 1), :], False),
            encode(high, tgt_dual[pl.ds(at + 1, 1), :], tgt_cot[pl.ds(at + 1, 1), :], False),
        ],
        axis=0,
    )
    out[...] = jnp.broadcast_to(both[None], out.shape)


def sweep_kernel(g0, g1, g2, g3, yg, plan, xs, cots, wu_out, part_out, xt, ya, bub, bvb, row, col):
    mx = lax.axis_index("x")
    my = lax.axis_index("y")
    for m, g in enumerate((g0, g1, g2, g3)):
        for k in range(4):
            at = lax.rem(mx + 4 - k, 4) * 4 + lax.rem(my + 4 - m, 4)
            xs[pl.ds(at, 1)] = g[k][None]
    pad = jnp.zeros((L - KP, L), f32)
    row_id = lax.broadcasted_iota(jnp.int32, (L, L), 0)
    pick = jnp.where((row_id >= 70) & (row_id < 73), 1.0, 0.0).astype(bf16)
    for k in range(NA):
        sl = slice(k * L, (k + 1) * L)
        block = xs[k]
        turned = jnp.concatenate([block.astype(f32), pad], axis=0).T.astype(bf16)
        xt[sl, :] = turned
        bub[sl, :] = jnp.dot(turned, pick, preferred_element_type=f32)
        cots[k : k + 1, :] = cot_of(block, True)
        other = yg[k]
        ya[:, sl] = jnp.concatenate([other, pad.astype(bf16)], axis=0)
        c = cot_of(other, False)
        cots[NA + k : NA + k + 1, :] = c
        bvb[:, sl] = jnp.broadcast_to(c, (8, L))
    rb, wide = 512, 256
    for r in range(ROWS // rb):
        rows = slice(r * rb, (r + 1) * rb)
        bu = bub[rows, :].reshape(rb // 8, 8, L)
        for n in range(COLS // wide):
            dots = jnp.dot(xt[rows, :], ya[:, n * wide : (n + 1) * wide], preferred_element_type=f32)
            p = jnp.exp2(dots * GAIN)
            plan[rows, n * wide : (n + 1) * wide] = p.astype(bf16)
            acc = None if n == 0 else row[rows, :].reshape(rb // 8, 8, L)
            for m in range(wide // L):
                sl = slice(n * wide + m * L, n * wide + (m + 1) * L)
                mixed = p[:, m * L : (m + 1) * L].reshape(rb // 8, 8, L) * (bu + bvb[:, sl][None])
                acc = mixed if acc is None else acc + mixed
                down = jnp.sum(mixed, axis=0)
                col[:, sl] = down if r == 0 else col[:, sl] + down
            row[rows, :] = acc.reshape(rb, L)
    wu = jnp.concatenate(
        [jnp.sum(row[k * L : (k + 1) * L, :].T, axis=0, keepdims=True) for k in range(NA)], axis=0
    )
    wv = jnp.concatenate(
        [jnp.sum(col[:, k * L : (k + 1) * L], axis=0, keepdims=True) for k in range(NB)], axis=0
    )
    bu = cots[0:NA]
    bv = cots[NA : NA + NB]
    bw = jnp.sum(wu * bu + wv * bv)
    bb = jnp.sum(bu * bu) / NA + jnp.sum(bv * bv) / NB
    mark = lax.broadcasted_iota(jnp.int32, (8, L), 0)
    wu_out[...] = wu
    part_out[...] = jnp.concatenate([wv, jnp.where(mark == 0, bw, bb)], axis=0)


def mix_kernel(wu, parts, send, own):
    total = parts[0] + parts[1]
    own[...] = total[0:NB]
    whole = jnp.concatenate([wu[...], total[NB:]], axis=0)
    send[...] = jnp.broadcast_to(whole[None], send.shape)


def relay_kernel(got, own, send):
    total = got[0]
    for k in range(1, got.shape[0]):
        total = total + got[k]
    whole = jnp.concatenate([own[...], total], axis=0)
    send[...] = jnp.broadcast_to(whole[None], send.shape)


def stack_side(out, sl, block, c, r):
    pts = block[0:D]
    wide = pts.astype(f32)
    out[0:D, sl] = pts
    out[D : 2 * D, sl] = (wide * c).astype(bf16)
    out[2 * D : 3 * D, sl] = (wide * r).astype(bf16)
    out[3 * D : MA, sl] = rows16([jnp.ones((1, L), f32)] + parts(r)).astype(bf16)


def finish_side(piece, c, r):
    base = piece[0:D]
    mass = piece[3 * D : 3 * D + 1]
    pushed = piece[3 * D + 1 : 3 * D + 2] + piece[3 * D + 2 : 3 * D + 3] + piece[3 * D + 3 : 3 * D + 4]
    t_b = c * base + piece[D : 2 * D]
    t_r = r * base + piece[2 * D : 3 * D]
    return t_b, t_r, r * mass + pushed, pushed, mass


def step_kernel(plan, xs, yg, cots, wu_in, wv_in, pay, mine, other, sums, scal, ax, ay):
    wu = wu_in[0, 0:NA]
    for k in range(1, NA):
        wu = wu + wu_in[k, 0:NA]
    wv = wv_in[0]
    for k in range(1, NZ):
        wv = wv + wv_in[k]
    bw = wv[NB : NB + 1]
    bb = wv[NB + 1 : NB + 2]
    wv = wv[0:NB]
    alpha = bb / (bw + ridge_shift * bb)
    scal[0:1, :] = alpha
    scal[1:2, :] = bb
    scal[2:8, :] = jnp.zeros((6, L), f32)
    sums[0:NA] = wu
    sums[NA : NA + NB] = wv
    bu, bv = cots[0:NA], cots[NA : NA + NB]
    ru = bu - alpha * (wu + ridge_shift * bu)
    rv = bv - alpha * (wv + ridge_shift * bv)
    rr = jnp.full((1, L), jnp.sum(ru * ru) / NA + jnp.sum(rv * rv) / NB, f32)
    for k in range(NA):
        stack_side(ax, slice(k * L, (k + 1) * L), xs[k], bu[k : k + 1], ru[k : k + 1])
    for k in range(NB):
        stack_side(ay, slice(k * L, (k + 1) * L), yg[k], bv[k : k + 1], rv[k : k + 1])
    flip = lax.axis_index("c") == 0
    quad = jnp.zeros((1, L), f32)
    tails = []
    wide = 256
    for n in range(COLS // wide):
        part = jnp.dot(ax[...], plan[:, n * wide : (n + 1) * wide], preferred_element_type=f32)
        blocks = []
        for m in range(2):
            at = 2 * n + m
            r = rv[at : at + 1]
            t_b, t_r, s_r, pushed, _ = finish_side(part[:, m * L : (m + 1) * L], bv[at : at + 1], r)
            quad = quad + r * (s_r + pushed)
            blocks.append((t_b, t_r))
            tails.append(s_r)
        (b0, r0), (b1, r1) = blocks
        mine[n, 0:D] = jnp.where(flip, b0, b1).astype(bf16)
        mine[n, D : 2 * D] = jnp.where(flip, r0, r1).astype(bf16)
        other[n, 0:D] = jnp.where(flip, b1, b0).astype(bf16)
        other[n, D : 2 * D] = jnp.where(flip, r1, r0).astype(bf16)
    for n in range(ROWS // wide):
        part = lax.dot_general(
            ay[...], plan[n * wide : (n + 1) * wide, :], (((1,), (1,)), ((), ())), preferred_element_type=f32
        )
        for m in range(2):
            at = 2 * n + m
            r = ru[at : at + 1]
            t_b, t_r, s_r, _, mass = finish_side(part[:, m * L : (m + 1) * L], bu[at : at + 1], r)
            quad = quad + r * r * mass
            pay[at, 0:D] = t_b.astype(bf16)
            pay[at, D : 2 * D] = t_r.astype(bf16)
            pay[at, 2 * D : PR] = rows16(parts(s_r)).astype(bf16)
    quad = jnp.full((1, L), jnp.sum(quad), f32)
    extra = parts(quad) + parts(rr)
    for n in range(NZ):
        s0, s1 = tails[2 * n], tails[2 * n + 1]
        mine[n, 2 * D : PR] = rows16(parts(jnp.where(flip, s0, s1)) + extra).astype(bf16)
        other[n, 2 * D : PR] = rows16(parts(jnp.where(flip, s1, s0)) + extra).astype(bf16)


def join_kernel(mine, both, pay_in, pay, send):
    got = both.at[1 - lax.axis_index("c")]
    a = mine[0, 2 * D :].astype(f32)
    b = got[0, 2 * D :].astype(f32)
    quad = join3(a, 3) + join3(b, 3)
    rr = join3(a, 6) + join3(b, 6)
    mark = lax.broadcasted_iota(jnp.int32, (16, L), 0)
    extra = rows16([jnp.zeros((1, L), f32)] * 3 + parts(quad) + parts(rr))
    for k in range(NA):
        pay[k] = jnp.where(mark < 3, pay_in[k].astype(f32), extra).astype(bf16)
    for k in range(NZ):
        send[k, 0 : 2 * D] = (mine[k, 0 : 2 * D].astype(f32) + got[k, 0 : 2 * D].astype(f32)).astype(bf16)
        s = join3(mine[k, 2 * D :], 0) + join3(got[k, 2 * D :], 0)
        send[k, 2 * D : PR] = rows16(parts(s)).astype(bf16)


def pass_kernel(got, send_in, tot, send):
    total = got[0].astype(f32)
    for k in range(1, NA):
        total = total + got[k].astype(f32)
    tot[...] = total
    quad = join3(total, 131)
    rr = join3(total, 134)
    mark = lax.broadcasted_iota(jnp.int32, (16, L), 0)
    extra = rows16([jnp.zeros((1, L), f32)] * 3 + parts(quad) + parts(rr))
    for k in range(NZ):
        send[k] = jnp.where(mark < 3, send_in[k].astype(f32), extra).astype(bf16)


def final_kernel(tot_s, got, src_ref, tgt_ref, sums, scal, out_s, out_t):
    tot_t = got[0].astype(f32)
    for k in range(1, NZ):
        tot_t = tot_t + got[k].astype(f32)
    alpha = scal[0:1, :]
    bb = scal[1:2, :]
    rr = join3(tot_t, 134)
    quad = join3(tot_t, 131) + ridge_shift * rr
    ratio = rr / bb
    step = rr / (quad - ratio * rr / alpha)
    scale = 2.0 / (blur_scale * D)
    c_b = scale * (alpha + step * ratio)
    c_r = scale * step
    si = lax.axis_index("x") * 4 + lax.axis_index("y")
    ti = lax.axis_index("z") * 2 + lax.axis_index("c")

    def combine(points, tot, s_b, out):
        s = c_b * s_b + c_r * join3(tot, 128)
        out[...] = points[...].astype(f32) * s - (c_b * tot[0:D] + c_r * tot[D : 2 * D])

    combine(src_ref, tot_s[...], sums[pl.ds(si, 1), :], out_s)
    combine(tgt_ref, tot_t, sums[pl.ds(NA + ti, 1), :], out_t)


def exchange(v, axes):
    return lax.all_to_all(v, axes, 0, 0, tiled=True)


def shift(v, axis, n, k):
    return lax.ppermute(v, axis, [(i, (i + k) % n) for i in range(n)])


def swap(v):
    return shift(v, "c", 2, 1)


def pair(v):
    return lax.all_gather(v, "c", axis=0, tiled=False)


def body(src_points, tgt_points, src_dual, tgt_dual, src_cot, tgt_cot):
    whole = lambda v: v.reshape(-1, L)
    own, send = call(encode_kernel, (sds((KP, L), bf16), sds((NZ, 2 * KP, L), bf16)), limit=WIDE)(
        src_points,
        tgt_points,
        swap(tgt_points),
        whole(src_dual),
        whole(src_cot),
        whole(tgt_dual),
        whole(tgt_cot),
    )
    g0 = jnp.stack([own] + [shift(own, "x", 4, k) for k in (1, 2, 3)], axis=0)
    yg = exchange(send, "z").reshape(NB, KP, L)
    g1, g2, g3 = [shift(g0, "y", 4, k) for k in (1, 2, 3)]
    unit = ROWS * COLS * 2
    vm = pltpu.VMEM
    plan, xs, cots, wu, part = call(
        sweep_kernel,
        (
            sds((ROWS, COLS), bf16),
            sds((NA, KP, L), bf16),
            sds((NA + NB, L), f32),
            sds((NA, L), f32),
            sds((NB + 8, L), f32),
        ),
        flops=unit * 400,
        scratch_shapes=[
            vm((ROWS, L), bf16),
            vm((L, COLS), bf16),
            vm((ROWS, L), f32),
            vm((8, COLS), f32),
            vm((ROWS, L), f32),
            vm((8, COLS), f32),
        ],
    )(g0, g1, g2, g3, yg)

    def tail(n, rows, at):
        return pl.BlockSpec((n, rows, L), lambda i: (0, at, 0))

    def full(*shape):
        return pl.BlockSpec(shape, lambda i: (0,) * len(shape))

    send, wv = call(
        mix_kernel,
        (sds((NA, 24, L), f32), sds((NB, L), f32)),
        grid=(1,),
        in_specs=[full(NA, L), full(2, NB + 8, L)],
        out_specs=(full(NA, 24, L), full(NB, L)),
    )(wu, pair(part))
    wu = exchange(send, SA)
    send = call(
        relay_kernel,
        sds((NZ, 24, L), f32),
        grid=(1,),
        in_specs=[tail(NA, 8, 2), full(NB, L)],
        out_specs=full(NZ, 24, L),
    )(wu, wv)
    wv = exchange(send, "z")
    half = sds((NZ, PR, L), bf16)
    pay, mine, other, sums, scal = call(
        step_kernel,
        (sds((NA, PR, L), bf16), half, half, sds((NA + NB, L), f32), sds((8, L), f32)),
        flops=unit * 256,
        scratch_shapes=[vm((MA, ROWS), bf16), vm((MA, COLS), bf16)],
    )(plan, xs, yg, cots, wu, wv)
    pay, send = call(
        join_kernel,
        (sds((NA, PR, L), bf16), half),
        grid=(1,),
        in_specs=[full(NZ, PR, L), full(2, NZ, PR, L), tail(NA, 16, 8)],
        out_specs=(tail(NA, 16, 8), full(NZ, PR, L)),
        input_output_aliases={2: 0},
    )(mine, pair(other), pay)
    got_s = exchange(pay, SA)
    tot_s, send = call(
        pass_kernel,
        (sds((PR, L), f32), half),
        grid=(1,),
        in_specs=[full(NA, PR, L), tail(NZ, 16, 8)],
        out_specs=(full(PR, L), tail(NZ, 16, 8)),
        input_output_aliases={1: 1},
    )(got_s, send)
    got_t = exchange(send, "z")
    return call(final_kernel, (sds((D, L), f32), sds((D, L), f32)))(
        tot_s, got_t, src_points, tgt_points, sums, scal
    )


def solution(mesh):
    grid = Mesh(mesh.devices.reshape(4, 2, 4, 8), ("x", "c", "y", "z"))
    in_specs = (
        P(None, ("x", "c", "y", "z")),
        P(None, ("y", "z", "x", "c")),
        P(("x", "c")),
        P(("y", "z")),
        P(("x", "c")),
        P(("y", "z")),
    )
    out_specs = (P(None, ("x", "c", "y", "z")), P(None, ("y", "z", "x", "c")))
    return jax.shard_map(body, mesh=grid, in_specs=in_specs, out_specs=out_specs, check_vma=False)
```

time: 108 us -> 104 us (0.963)
  Pallas kernels: 16.8 us -> 12.1 us
  blocking collectives: 57.9 us -> 61.7 us
  local copies, waits for them, and re-layouts: 4.24 us -> 0.62 us
  starting transfers between devices: 19.3 us -> 17.2 us
  waiting for transfers between devices: 8.15 us -> 9.42 us
    all_gather x0 -> x2, blocking collectives: none -> 9.96 us  [pair(): return lax.all_gather(v, 'c', axis=0, tiled=False)]
    all_to_all x4, blocking collectives: 57.9 us -> 51.8 us  [exchange(): return lax.all_to_all(v, axes, 0, 0, tiled=True)]
    pallas_call x1, Pallas kernels: 8.51 us -> 4.8 us  [body(): call(sweep_kernel, (sds((ROWS, COLS), bf16), sds((NA, KP, L), bf16), sds(...]
    unnamed x16 -> x6, local copies, waits for them, and re-layouts: 4.24 us -> 0.62 us
    ppermute x8 -> x7, waiting for transfers between devices: 6.65 us -> 9.42 us  [shift(): return lax.ppermute(v, axis, [(i, (i + k) % n) for i in range(n)])]
    all_to_all x1, starting transfers between devices: 8.19 us -> 6.45 us  [exchange(): return lax.all_to_all(v, axes, 0, 0, tiled=True)]
    all_to_all x1, waiting for transfers between devices: 1.49 us -> 0.01 us  [exchange(): return lax.all_to_all(v, axes, 0, 0, tiled=True)]
    pallas_call x6 -> x5, Pallas kernels: 7.47 us -> 6.48 us  [the longest x1 4.74 us: body(): call(step_kernel, (sds((NA, PR, L), bf16), half, half, sds((NA + NB, L),...]
  transfers between devices with their start and end apart: 9 -> 8, of which waited for: 6 -> 6; matrix products, arithmetic and copies ran while one was open for 0% -> 1% of each run, Pallas kernels for 3% -> 0%
where the time goes in v4:
time: 104 us; the launch traced here: 103 us
  blocking collectives  61.7 us (59%)
  starting transfers between devices  17.2 us (17%)
  Pallas kernels  12.1 us (12%)
  waiting for transfers between devices  9.42 us (9%)
    all_to_all x4, blocking collectives, exchange(): return lax.all_to_all(v, axes, 0, 0, tiled=True)  51.8 us
    ppermute x7, starting transfers between devices, shift(): return lax.ppermute(v, axis, [(i, (i + k) % n) for i in range(n)])  10.8 us
    all_gather x2, blocking collectives, pair(): return lax.all_gather(v, 'c', axis=0, tiled=False)  9.96 us
    ppermute x7, waiting for transfers between devices, shift(): return lax.ppermute(v, axis, [(i, (i + k) % n) for i in range(n)])  9.42 us
    all_to_all x1, starting transfers between devices, exchange(): return lax.all_to_all(v, axes, 0, 0, tiled=True)  6.45 us
    pallas_call x1, Pallas kernels, body(): call(sweep_kernel, (sds((ROWS, COLS), bf16), sds((NA, KP, L), bf16), sds(...  4.8 us
    pallas_call x1, Pallas kernels, body(): call(step_kernel, (sds((NA, PR, L), bf16), half, half, sds((NA + NB, L),...  4.74 us
  transfers between devices with their start and end apart: 8, of which 6 were waited for; matrix products, arithmetic and copies ran while one was open for 1% of the time, Pallas kernels for 0%

profile of v4, /device:TPU:1, one launch (start us, length us, event | category | flops | bytes accessed | tf_op | source)
XLA Modules:
  0.0 102.5 jit_solution(15594270516649491687)
XLA Ops:
  0.6 3.3 %collective-permute-start = (bf16[64,128]{1,0:T(8,128)(2,1)}, bf16[64,128]{1,0:T(8,128)(2,1)S(1)}, u32[]{:S(2)}, u32[]{:S(2)}) collective-permute-start(bf16[64,128]{1,0:T(8,128)(2,1)} %tgt_ref.1), channel_id=1, source_target_pairs={{0,32},{32,0},{1,33},{33,1},{2,34},{34,2},{3,35},{35,3},{4,36},{36... | collective-permute-start | bytes 49160 | tf_op jit(solution)/shard_map/ppermute | solution.py:317
  4.0 1.0 %collective-permute-done.other = bf16[64,128]{1,0:T(8,128)(2,1)S(1)} collective-permute-done((bf16[64,128]{1,0:T(8,128)(2,1)}, bf16[64,128]{1,0:T(8,128)(2,1)S(1)}, u32[]{:S(2)}, u32[]{:S(2)}) %collective-permute-start) | collective-permute-done | bytes 16416 | tf_op jit(solution)/shard_map/ppermute | solution.py:317
  5.0 0.0 copy-start.2
  5.0 0.6 copy-done.2
  5.6 1.6 %shard_map.77 = (bf16[80,128]{1,0:T(8,128)(2,1)}, bf16[8,160,128]{2,1,0:T(8,128)(2,1)}) custom-call(bf16[64,128]{1,0:T(8,128)(2,1)} %src_ref.1, bf16[64,128]{1,0:T(8,128)(2,1)} %tgt_ref.1, bf16[64,128]{1,0:T(8,128)(2,1)} %copy-done.2, f32[32,128]{1,0:T(8,128)} %bitcast.19, f32[32,128]{1,0:T(8,128)} %bitcast.20, f32[8,128]{1,0:T(8,128)} %bitcast.21, ...), custom_call_target="tpu_custom_call" | custom-call | bytes 1048576 | tf_op jit(solution)/shard_map/pallas_call | solution.py:330
  7.2 6.5 %all-to-all-start = ((bf16[8,160,128]{2,1,0:T(8,128)(2,1)}), bf16[8,160,128]{2,1,0:T(8,128)(2,1)S(1)}, u32[]{:S(2)}, u32[]{:S(2)}) async-start(bf16[8,160,128]{2,1,0:T(8,128)(2,1)} %get-tuple-element.21), calls=%async_computation | async-start | bytes 655360 | tf_op jit(solution)/shard_map/all_to_all | solution.py:313
  13.6 2.5 %collective-permute-start.3 = (bf16[80,128]{1,0:T(8,128)(2,1)}, bf16[80,128]{1,0:T(8,128)(2,1)S(1)}, u32[]{:S(2)}, u32[]{:S(2)}) collective-permute-start(bf16[80,128]{1,0:T(8,128)(2,1)} %get-tuple-element.20), channel_id=1, source_target_pairs={{0,192},{64,0},{128,64},{192,128},{1,193},{65,1},{129,65},{193,129... | collective-permute-start | bytes 61448 | tf_op jit(solution)/shard_map/ppermute | solution.py:317
  16.1 0.5 collective-permute-start.2
  16.6 0.6 collective-permute-start.1
  17.2 0.0 collective-permute-done.3
  17.2 3.2 %collective-permute-done.2 = bf16[80,128]{1,0:T(8,128)(2,1)S(1)} collective-permute-done((bf16[80,128]{1,0:T(8,128)(2,1)}, bf16[80,128]{1,0:T(8,128)(2,1)S(1)}, u32[]{:S(2)}, u32[]{:S(2)}) %collective-permute-start.2) | collective-permute-done | bytes 20512 | tf_op jit(solution)/shard_map/ppermute | solution.py:317
  20.5 0.5 collective-permute-done.1
  21.0 0.7 pad_maximum_fusion.g0
  21.7 2.8 %collective-permute-start.6 = (bf16[4,80,128]{2,1,0:T(8,128)(2,1)S(1)}, bf16[4,80,128]{2,1,0:T(8,128)(2,1)S(1)}, u32[]{:S(2)}, u32[]{:S(2)}) collective-permute-start(bf16[4,80,128]{2,1,0:T(8,128)(2,1)S(1)} %pad_maximum_fusion.g0), channel_id=1, source_target_pairs={{0,24},{8,0},{16,8},{24,16},{1,25},{9,1},{17,9},{25,17},{2,26},{10... | collective-permute-start | bytes 245768 | tf_op jit(solution)/shard_map/ppermute | solution.py:317
  24.5 0.3 collective-permute-start.5
  24.9 0.7 collective-permute-start.4
  25.6 0.4 collective-permute-done.6.g3
  26.0 3.4 %collective-permute-done.5.g2 = bf16[4,80,128]{2,1,0:T(8,128)(2,1)S(1)} collective-permute-done((bf16[4,80,128]{2,1,0:T(8,128)(2,1)S(1)}, bf16[4,80,128]{2,1,0:T(8,128)(2,1)S(1)}, u32[]{:S(2)}, u32[]{:S(2)}) %collective-permute-start.5) | collective-permute-done | bytes 81952 | tf_op jit(solution)/shard_map/ppermute | solution.py:317
  29.4 0.8 collective-permute-done.4.g1
  30.2 0.0 all-to-all-done
  30.2 4.8 %shard_map.78 = (bf16[2048,2048]{1,0:T(8,128)(2,1)S(1)}, bf16[16,80,128]{2,1,0:T(8,128)(2,1)S(1)}, f32[32,128]{1,0:T(8,128)S(1)}, f32[16,128]{1,0:T(8,128)S(1)}, f32[24,128]{1,0:T(8,128)S(1)}) custom-call(bf16[4,80,128]{2,1,0:T(8,128)(2,1)S(1)} %pad_maximum_fusion.g0, bf16[4,80,128]{2,1,0:T(8,128)(2,1)S(1)} %collective-permute-done.4.g1, ...), custom_call_target="tpu_custom_call" | custom-call | flops 3355443200 | bytes 1048576 | tf_op jit(solution)/shard_map/pallas_call | solution.py:344
  35.0 0.0 copy-start
  35.0 0.0 copy-start.1
  35.1 5.0 %all-gather = f32[48,128]{1,0:T(8,128)S(1)} all-gather(f32[24,128]{1,0:T(8,128)S(1)} %get-tuple-element.26), channel_id=2, replica_groups=mesh['x'=4,'c'=2,'y'=4,'z'=8] {'c'}, dimensions={0}, use_global_device_ids=true | all-gather | bytes 36864 | tf_op jit(solution)/shard_map/all_gather | solution.py:325
  40.0 10.0 %all_to_all.25.got.wu_in = f32[16,24,128]{2,1,0:T(8,128)S(1)} all-to-all(f32[16,24,128]{2,1,0:T(8,128)S(1)} %get-tuple-element.27), channel_id=1, replica_groups=mesh['x'=4,'c'=2,'y'=4,'z'=8] {'x','y'}, dimensions={0} | all-to-all | bytes 393216 | tf_op jit(solution)/shard_map/all_to_all | solution.py:313
  50.1 14.4 %all_to_all.26.wv_in = f32[8,24,128]{2,1,0:T(8,128)S(1)} all-to-all(f32[8,24,128]{2,1,0:T(8,128)S(1)} %shard_map.80), channel_id=1, replica_groups=mesh['x'=4,'c'=2,'y'=4,'z'=8] {'z'}, dimensions={0} | all-to-all | bytes 196608 | tf_op jit(solution)/shard_map/all_to_all | solution.py:313
  64.5 4.7 %shard_map.81 = (bf16[16,144,128]{2,1,0:T(8,128)(2,1)S(1)}, bf16[8,144,128]{2,1,0:T(8,128)(2,1)S(1)}, bf16[8,144,128]{2,1,0:T(8,128)(2,1)S(1)}, f32[32,128]{1,0:T(8,128)S(1)}, f32[8,128]{1,0:T(8,128)S(1)}) custom-call(bf16[2048,2048]{1,0:T(8,128)(2,1)S(1)} %get-tuple-element.22.plan, bf16[16,80,128]{2,1,0:T(8,128)(2,1)S(1)} %get-tuple-element.23.xs, ...), custom_call_target="tpu_custom_call" | custom-call | flops 2147483648 | bytes 1048576 | tf_op jit(solution)/shard_map/pallas_call | solution.py:387
  69.2 5.0 %all-gather.1 = bf16[16,144,128]{2,1,0:T(8,128)(2,1)S(1)} all-gather(bf16[8,144,128]{2,1,0:T(8,128)(2,1)S(1)} %get-tuple-element.30), channel_id=3, replica_groups=mesh['x'=4,'c'=2,'y'=4,'z'=8] {'c'}, dimensions={0}, use_global_device_ids=true | all-gather | bytes 884736 | tf_op jit(solution)/shard_map/all_gather | solution.py:325
  74.2 0.1 shard_map.82
  74.4 14.6 %all_to_all.27.got = bf16[16,144,128]{2,1,0:T(8,128)(2,1)S(1)} all-to-all(bf16[16,144,128]{2,1,0:T(8,128)(2,1)S(1)} %get-tuple-element.32), channel_id=1, replica_groups=mesh['x'=4,'c'=2,'y'=4,'z'=8] {'x','y'}, dimensions={0} | all-to-all | bytes 1179648 | tf_op jit(solution)/shard_map/all_to_all | solution.py:313
  89.0 0.1 shard_map.83
  89.1 12.8 %all_to_all.28.got = bf16[8,144,128]{2,1,0:T(8,128)(2,1)S(1)} all-to-all(bf16[8,144,128]{2,1,0:T(8,128)(2,1)S(1)} %get-tuple-element.35), channel_id=1, replica_groups=mesh['x'=4,'c'=2,'y'=4,'z'=8] {'z'}, dimensions={0} | all-to-all | bytes 589824 | tf_op jit(solution)/shard_map/all_to_all | solution.py:313
  101.8 0.0 copy-done
  101.8 0.0 copy-done.1
  101.8 0.7 shard_map.84
  (2 shorter events, 0.0 us)
Async XLA Ops:
  0.6 4.4 %collective-permute-start = (bf16[64,128]{1,0:T(8,128)(2,1)}, bf16[64,128]{1,0:T(8,128)(2,1)S(1)}, u32[]{:S(2)}, u32[]{:S(2)}) collective-permute-start(bf16[64,128]{1,0:T(8,128)(2,1)} %tgt_ref.1), channel_id=1, source_target_pairs={{0,32},{32,0},{1,33},{33,1},{2,34},{34,2},{3,35},{35,3},{4,36},{36... | collective-permute-start | bytes 49160 | tf_op jit(solution)/shard_map/ppermute | solution.py:317
  5.0 0.6 copy-start.2
  7.2 23.0 %all-to-all-start = ((bf16[8,160,128]{2,1,0:T(8,128)(2,1)}), bf16[8,160,128]{2,1,0:T(8,128)(2,1)S(1)}, u32[]{:S(2)}, u32[]{:S(2)}) async-start(bf16[8,160,128]{2,1,0:T(8,128)(2,1)} %get-tuple-element.21), calls=%async_computation | async-start | bytes 655360 | tf_op jit(solution)/shard_map/all_to_all | solution.py:313
  13.6 3.6 %collective-permute-start.3 = (bf16[80,128]{1,0:T(8,128)(2,1)}, bf16[80,128]{1,0:T(8,128)(2,1)S(1)}, u32[]{:S(2)}, u32[]{:S(2)}) collective-permute-start(bf16[80,128]{1,0:T(8,128)(2,1)} %get-tuple-element.20), channel_id=1, source_target_pairs={{0,192},{64,0},{128,64},{192,128},{1,193},{65,1},{129,65},{193,129... | collective-permute-start | bytes 61448 | tf_op jit(solution)/shard_map/ppermute | solution.py:317
  16.1 4.3 %collective-permute-start.2 = (bf16[80,128]{1,0:T(8,128)(2,1)}, bf16[80,128]{1,0:T(8,128)(2,1)S(1)}, u32[]{:S(2)}, u32[]{:S(2)}) collective-permute-start(bf16[80,128]{1,0:T(8,128)(2,1)} %get-tuple-element.20), channel_id=1, source_target_pairs={{0,128},{64,192},{128,0},{192,64},{1,129},{65,193},{129,1},{193,65... | collective-permute-start | bytes 61448 | tf_op jit(solution)/shard_map/ppermute | solution.py:317
  16.6 4.3 %collective-permute-start.1 = (bf16[80,128]{1,0:T(8,128)(2,1)}, bf16[80,128]{1,0:T(8,128)(2,1)S(1)}, u32[]{:S(2)}, u32[]{:S(2)}) collective-permute-start(bf16[80,128]{1,0:T(8,128)(2,1)} %get-tuple-element.20), channel_id=1, source_target_pairs={{0,64},{64,128},{128,192},{192,0},{1,65},{65,129},{129,193},{193,1... | collective-permute-start | bytes 61448 | tf_op jit(solution)/shard_map/ppermute | solution.py:317
  21.7 4.3 %collective-permute-start.6 = (bf16[4,80,128]{2,1,0:T(8,128)(2,1)S(1)}, bf16[4,80,128]{2,1,0:T(8,128)(2,1)S(1)}, u32[]{:S(2)}, u32[]{:S(2)}) collective-permute-start(bf16[4,80,128]{2,1,0:T(8,128)(2,1)S(1)} %pad_maximum_fusion.g0), channel_id=1, source_target_pairs={{0,24},{8,0},{16,8},{24,16},{1,25},{9,1},{17,9},{25,17},{2,26},{10... | collective-permute-start | bytes 245768 | tf_op jit(solution)/shard_map/ppermute | solution.py:317
  24.5 4.9 %collective-permute-start.5 = (bf16[4,80,128]{2,1,0:T(8,128)(2,1)S(1)}, bf16[4,80,128]{2,1,0:T(8,128)(2,1)S(1)}, u32[]{:S(2)}, u32[]{:S(2)}) collective-permute-start(bf16[4,80,128]{2,1,0:T(8,128)(2,1)S(1)} %pad_maximum_fusion.g0), channel_id=1, source_target_pairs={{0,16},{8,24},{16,0},{24,8},{1,17},{9,25},{17,1},{25,9},{2,18},{10... | collective-permute-start | bytes 245768 | tf_op jit(solution)/shard_map/ppermute | solution.py:317
  24.9 5.3 %collective-permute-start.4 = (bf16[4,80,128]{2,1,0:T(8,128)(2,1)S(1)}, bf16[4,80,128]{2,1,0:T(8,128)(2,1)S(1)}, u32[]{:S(2)}, u32[]{:S(2)}) collective-permute-start(bf16[4,80,128]{2,1,0:T(8,128)(2,1)S(1)} %pad_maximum_fusion.g0), channel_id=1, source_target_pairs={{0,8},{8,16},{16,24},{24,0},{1,9},{9,17},{17,25},{25,1},{2,10},{10... | collective-permute-start | bytes 245768 | tf_op jit(solution)/shard_map/ppermute | solution.py:317
  35.0 66.8 %copy-start = (bf16[64,128]{1,0:T(8,128)(2,1)S(1)}, bf16[64,128]{1,0:T(8,128)(2,1)}, u32[]{:S(2)}) copy-start(bf16[64,128]{1,0:T(8,128)(2,1)} %src_ref.1) | copy-start | bytes 49156
  35.0 66.8 %copy-start.1 = (bf16[64,128]{1,0:T(8,128)(2,1)S(1)}, bf16[64,128]{1,0:T(8,128)(2,1)}, u32[]{:S(2)}) copy-start(bf16[64,128]{1,0:T(8,128)(2,1)} %tgt_ref.1) | copy-start | bytes 49156

commit v5 on v4

--- a/solution.py
+++ b/solution.py
@@ -105,6 +105,11 @@
         axis=0,
     )
     out[...] = jnp.broadcast_to(both[None], out.shape)
+
+
+def stack_kernel(a, b, c, d, out):
+    for k, part in enumerate((a, b, c, d)):
+        out[k] = part[...]
 
 
 def sweep_kernel(g0, g1, g2, g3, yg, plan, xs, cots, wu_out, part_out, xt, ya, bub, bvb, row, col):
@@ -336,7 +341,9 @@
         whole(tgt_dual),
         whole(tgt_cot),
     )
-    g0 = jnp.stack([own] + [shift(own, "x", 4, k) for k in (1, 2, 3)], axis=0)
+    g0 = call(stack_kernel, sds((4, KP, L), bf16), flops=10000000000)(
+        own, *[shift(own, "x", 4, k) for k in (1, 2, 3)]
+    )
     yg = exchange(send, "z").reshape(NB, KP, L)
     g1, g2, g3 = [shift(g0, "y", 4, k) for k in (1, 2, 3)]
     unit = ROWS * COLS * 2

time: 104 us -> 100 us (0.962)
  waiting for transfers between devices: 9.42 us -> 7.64 us
  blocking collectives: 61.7 us -> 60 us
    ppermute x7, waiting for transfers between devices: 9.42 us -> 5.98 us  [shift(): return lax.ppermute(v, axis, [(i, (i + k) % n) for i in range(n)])]
    ppermute x7, starting transfers between devices: 10.8 us -> 8.97 us  [shift(): return lax.ppermute(v, axis, [(i, (i + k) % n) for i in range(n)])]
    all_to_all x1, starting transfers between devices: 6.45 us -> 8.19 us  [exchange(): return lax.all_to_all(v, axes, 0, 0, tiled=True)]
    all_to_all x1, waiting for transfers between devices: 0.01 us -> 1.66 us  [exchange(): return lax.all_to_all(v, axes, 0, 0, tiled=True)]
    all_to_all x4, blocking collectives: 51.8 us -> 50.5 us  [exchange(): return lax.all_to_all(v, axes, 0, 0, tiled=True)]
  transfers between devices with their start and end apart: 8 -> 8, of which waited for: 6 -> 5; matrix products, arithmetic and copies ran while one was open for 1% -> 0% of each run, Pallas kernels for 0% -> 0%
where the time goes in v5:
time: 100 us; the launch traced here: 98.9 us
  blocking collectives  60 us (60%)
  starting transfers between devices  17.2 us (17%)
  Pallas kernels  12.1 us (12%)
  waiting for transfers between devices  7.64 us (8%)
  local copies, waits for them, and re-layouts  1.34 us (1%)
    all_to_all x4, blocking collectives, exchange(): return lax.all_to_all(v, axes, 0, 0, tiled=True)  50.5 us
    all_gather x2, blocking collectives, pair(): return lax.all_gather(v, 'c', axis=0, tiled=False)  9.54 us
    ppermute x7, starting transfers between devices, shift(): return lax.ppermute(v, axis, [(i, (i + k) % n) for i in range(n)])  8.97 us
    all_to_all x1, starting transfers between devices, exchange(): return lax.all_to_all(v, axes, 0, 0, tiled=True)  8.19 us
    ppermute x7, waiting for transfers between devices, shift(): return lax.ppermute(v, axis, [(i, (i + k) % n) for i in range(n)])  5.98 us
    pallas_call x1, Pallas kernels, body(): call(sweep_kernel, (sds((ROWS, COLS), bf16), sds((NA, KP, L), bf16), sds(...  4.82 us
    pallas_call x1, Pallas kernels, body(): call(step_kernel, (sds((NA, PR, L), bf16), half, half, sds((NA + NB, L),...  4.75 us
  transfers between devices with their start and end apart: 8, of which 5 were waited for; matrix products, arithmetic and copies ran while one was open for 0% of the time, Pallas kernels for 0%

profile of v5, /device:TPU:1, one launch (start us, length us, event | category | flops | bytes accessed | tf_op | source)
XLA Modules:
  0.0 98.9 jit_solution(17912795546062358414)
XLA Ops:
  0.6 3.3 %collective-permute-start = (bf16[64,128]{1,0:T(8,128)(2,1)}, bf16[64,128]{1,0:T(8,128)(2,1)S(1)}, u32[]{:S(2)}, u32[]{:S(2)}) collective-permute-start(bf16[64,128]{1,0:T(8,128)(2,1)} %tgt_ref.1), channel_id=1, source_target_pairs={{0,32},{32,0},{1,33},{33,1},{2,34},{34,2},{3,35},{35,3},{4,36},{36... | collective-permute-start | bytes 49160 | tf_op jit(solution)/shard_map/ppermute | solution.py:322
  4.0 1.0 %collective-permute-done.other = bf16[64,128]{1,0:T(8,128)(2,1)S(1)} collective-permute-done((bf16[64,128]{1,0:T(8,128)(2,1)}, bf16[64,128]{1,0:T(8,128)(2,1)S(1)}, u32[]{:S(2)}, u32[]{:S(2)}) %collective-permute-start) | collective-permute-done | bytes 16416 | tf_op jit(solution)/shard_map/ppermute | solution.py:322
  5.0 0.0 copy-start.3
  5.0 0.6 copy-done.3
  5.6 1.6 %shard_map.77 = (bf16[80,128]{1,0:T(8,128)(2,1)}, bf16[8,160,128]{2,1,0:T(8,128)(2,1)}) custom-call(bf16[64,128]{1,0:T(8,128)(2,1)} %src_ref.1, bf16[64,128]{1,0:T(8,128)(2,1)} %tgt_ref.1, bf16[64,128]{1,0:T(8,128)(2,1)} %copy-done.3, f32[32,128]{1,0:T(8,128)} %bitcast.11, f32[32,128]{1,0:T(8,128)} %bitcast.12, f32[8,128]{1,0:T(8,128)} %bitcast.13, ...), custom_call_target="tpu_custom_call" | custom-call | bytes 1048576 | tf_op jit(solution)/shard_map/pallas_call | solution.py:335
  7.2 0.7 collective-permute-start.3
  7.9 0.5 collective-permute-start.2
  8.5 0.6 collective-permute-start.1
  9.1 8.2 %all-to-all-start = ((bf16[8,160,128]{2,1,0:T(8,128)(2,1)}), bf16[8,160,128]{2,1,0:T(8,128)(2,1)S(1)}, u32[]{:S(2)}, u32[]{:S(2)}) async-start(bf16[8,160,128]{2,1,0:T(8,128)(2,1)} %get-tuple-element.21), calls=%async_computation | async-start | bytes 655360 | tf_op jit(solution)/shard_map/all_to_all | solution.py:318
  17.3 0.0 collective-permute-done.3.d
  17.3 0.0 collective-permute-done.2.c
  17.3 0.0 collective-permute-done.1.b
  17.3 0.0 copy-start.2
  17.3 0.7 copy-done.2
  18.0 2.7 %collective-permute-start.6 = (bf16[4,80,128]{2,1,0:T(8,128)(2,1)S(1)}, bf16[4,80,128]{2,1,0:T(8,128)(2,1)S(1)}, u32[]{:S(2)}, u32[]{:S(2)}) collective-permute-start(bf16[4,80,128]{2,1,0:T(8,128)(2,1)S(1)} %shard_map.78.g0), channel_id=1, source_target_pairs={{0,24},{8,0},{16,8},{24,16},{1,25},{9,1},{17,9},{25,17},{2,26},{10... | collective-permute-start | bytes 245768 | tf_op jit(solution)/shard_map/ppermute | solution.py:322
  20.8 0.3 collective-permute-start.5
  21.1 0.7 collective-permute-start.4
  21.8 0.4 collective-permute-done.6.g3
  22.2 3.6 %collective-permute-done.5.g2 = bf16[4,80,128]{2,1,0:T(8,128)(2,1)S(1)} collective-permute-done((bf16[4,80,128]{2,1,0:T(8,128)(2,1)S(1)}, bf16[4,80,128]{2,1,0:T(8,128)(2,1)S(1)}, u32[]{:S(2)}, u32[]{:S(2)}) %collective-permute-start.5) | collective-permute-done | bytes 81952 | tf_op jit(solution)/shard_map/ppermute | solution.py:322
  25.8 0.9 collective-permute-done.4.g1
  26.7 1.7 %all-to-all-done = bf16[8,160,128]{2,1,0:T(8,128)(2,1)S(1)} async-done(((bf16[8,160,128]{2,1,0:T(8,128)(2,1)}), bf16[8,160,128]{2,1,0:T(8,128)(2,1)S(1)}, u32[]{:S(2)}, u32[]{:S(2)}) %all-to-all-start) | async-done | bytes 327712 | tf_op jit(solution)/shard_map/all_to_all | solution.py:318
  28.4 4.8 %shard_map.79 = (bf16[2048,2048]{1,0:T(8,128)(2,1)S(1)}, bf16[16,80,128]{2,1,0:T(8,128)(2,1)S(1)}, f32[32,128]{1,0:T(8,128)S(1)}, f32[16,128]{1,0:T(8,128)S(1)}, f32[24,128]{1,0:T(8,128)S(1)}) custom-call(bf16[4,80,128]{2,1,0:T(8,128)(2,1)S(1)} %shard_map.78.g0, bf16[4,80,128]{2,1,0:T(8,128)(2,1)S(1)} %collective-permute-done.4.g1, ...), custom_call_target="tpu_custom_call" | custom-call | flops 3355443200 | bytes 1048576 | tf_op jit(solution)/shard_map/pallas_call | solution.py:351
  33.2 0.0 copy-start
  33.2 0.0 copy-start.1
  33.2 4.6 %all-gather = f32[48,128]{1,0:T(8,128)S(1)} all-gather(f32[24,128]{1,0:T(8,128)S(1)} %get-tuple-element.26), channel_id=2, replica_groups=mesh['x'=4,'c'=2,'y'=4,'z'=8] {'c'}, dimensions={0}, use_global_device_ids=true | all-gather | bytes 36864 | tf_op jit(solution)/shard_map/all_gather | solution.py:330
  37.8 12.9 %all_to_all.25.got.wu_in = f32[16,24,128]{2,1,0:T(8,128)S(1)} all-to-all(f32[16,24,128]{2,1,0:T(8,128)S(1)} %get-tuple-element.27), channel_id=1, replica_groups=mesh['x'=4,'c'=2,'y'=4,'z'=8] {'x','y'}, dimensions={0} | all-to-all | bytes 393216 | tf_op jit(solution)/shard_map/all_to_all | solution.py:318
  50.8 10.2 %all_to_all.26.wv_in = f32[8,24,128]{2,1,0:T(8,128)S(1)} all-to-all(f32[8,24,128]{2,1,0:T(8,128)S(1)} %shard_map.81), channel_id=1, replica_groups=mesh['x'=4,'c'=2,'y'=4,'z'=8] {'z'}, dimensions={0} | all-to-all | bytes 196608 | tf_op jit(solution)/shard_map/all_to_all | solution.py:318
  61.0 4.7 %shard_map.82 = (bf16[16,144,128]{2,1,0:T(8,128)(2,1)S(1)}, bf16[8,144,128]{2,1,0:T(8,128)(2,1)S(1)}, bf16[8,144,128]{2,1,0:T(8,128)(2,1)S(1)}, f32[32,128]{1,0:T(8,128)S(1)}, f32[8,128]{1,0:T(8,128)S(1)}) custom-call(bf16[2048,2048]{1,0:T(8,128)(2,1)S(1)} %get-tuple-element.22.plan, bf16[16,80,128]{2,1,0:T(8,128)(2,1)S(1)} %get-tuple-element.23.xs, ...), custom_call_target="tpu_custom_call" | custom-call | flops 2147483648 | bytes 1048576 | tf_op jit(solution)/shard_map/pallas_call | solution.py:394
  65.7 5.0 %all-gather.1 = bf16[16,144,128]{2,1,0:T(8,128)(2,1)S(1)} all-gather(bf16[8,144,128]{2,1,0:T(8,128)(2,1)S(1)} %get-tuple-element.30), channel_id=3, replica_groups=mesh['x'=4,'c'=2,'y'=4,'z'=8] {'c'}, dimensions={0}, use_global_device_ids=true | all-gather | bytes 884736 | tf_op jit(solution)/shard_map/all_gather | solution.py:330
  70.7 0.1 shard_map.83
  70.8 14.6 %all_to_all.27.got = bf16[16,144,128]{2,1,0:T(8,128)(2,1)S(1)} all-to-all(bf16[16,144,128]{2,1,0:T(8,128)(2,1)S(1)} %get-tuple-element.32), channel_id=1, replica_groups=mesh['x'=4,'c'=2,'y'=4,'z'=8] {'x','y'}, dimensions={0} | all-to-all | bytes 1179648 | tf_op jit(solution)/shard_map/all_to_all | solution.py:318
  85.4 0.1 shard_map.84
  85.5 12.8 %all_to_all.28.got = bf16[8,144,128]{2,1,0:T(8,128)(2,1)S(1)} all-to-all(bf16[8,144,128]{2,1,0:T(8,128)(2,1)S(1)} %get-tuple-element.35), channel_id=1, replica_groups=mesh['x'=4,'c'=2,'y'=4,'z'=8] {'z'}, dimensions={0} | all-to-all | bytes 589824 | tf_op jit(solution)/shard_map/all_to_all | solution.py:318
  98.3 0.0 copy-done
  98.3 0.0 copy-done.1
  98.3 0.7 shard_map.85
  (3 shorter events, 0.0 us)
Async XLA Ops:
  0.6 4.4 %collective-permute-start = (bf16[64,128]{1,0:T(8,128)(2,1)}, bf16[64,128]{1,0:T(8,128)(2,1)S(1)}, u32[]{:S(2)}, u32[]{:S(2)}) collective-permute-start(bf16[64,128]{1,0:T(8,128)(2,1)} %tgt_ref.1), channel_id=1, source_target_pairs={{0,32},{32,0},{1,33},{33,1},{2,34},{34,2},{3,35},{35,3},{4,36},{36... | collective-permute-start | bytes 49160 | tf_op jit(solution)/shard_map/ppermute | solution.py:322
  5.0 0.6 copy-start.3
  7.2 10.1 %collective-permute-start.3 = (bf16[80,128]{1,0:T(8,128)(2,1)}, bf16[80,128]{1,0:T(8,128)(2,1)S(1)}, u32[]{:S(2)}, u32[]{:S(2)}) collective-permute-start(bf16[80,128]{1,0:T(8,128)(2,1)} %get-tuple-element.20.a), channel_id=1, source_target_pairs={{0,192},{64,0},{128,64},{192,128},{1,193},{65,1},{129,65},{193,129... | collective-permute-start | bytes 61448 | tf_op jit(solution)/shard_map/ppermute | solution.py:322
  7.9 9.3 %collective-permute-start.2 = (bf16[80,128]{1,0:T(8,128)(2,1)}, bf16[80,128]{1,0:T(8,128)(2,1)S(1)}, u32[]{:S(2)}, u32[]{:S(2)}) collective-permute-start(bf16[80,128]{1,0:T(8,128)(2,1)} %get-tuple-element.20.a), channel_id=1, source_target_pairs={{0,128},{64,192},{128,0},{192,64},{1,129},{65,193},{129,1},{193,65... | collective-permute-start | bytes 61448 | tf_op jit(solution)/shard_map/ppermute | solution.py:322
  8.5 8.8 %collective-permute-start.1 = (bf16[80,128]{1,0:T(8,128)(2,1)}, bf16[80,128]{1,0:T(8,128)(2,1)S(1)}, u32[]{:S(2)}, u32[]{:S(2)}) collective-permute-start(bf16[80,128]{1,0:T(8,128)(2,1)} %get-tuple-element.20.a), channel_id=1, source_target_pairs={{0,64},{64,128},{128,192},{192,0},{1,65},{65,129},{129,193},{193,1... | collective-permute-start | bytes 61448 | tf_op jit(solution)/shard_map/ppermute | solution.py:322
  9.1 19.3 %all-to-all-start = ((bf16[8,160,128]{2,1,0:T(8,128)(2,1)}), bf16[8,160,128]{2,1,0:T(8,128)(2,1)S(1)}, u32[]{:S(2)}, u32[]{:S(2)}) async-start(bf16[8,160,128]{2,1,0:T(8,128)(2,1)} %get-tuple-element.21), calls=%async_computation | async-start | bytes 655360 | tf_op jit(solution)/shard_map/all_to_all | solution.py:318
  17.3 0.7 copy-start.2
  18.0 4.2 %collective-permute-start.6 = (bf16[4,80,128]{2,1,0:T(8,128)(2,1)S(1)}, bf16[4,80,128]{2,1,0:T(8,128)(2,1)S(1)}, u32[]{:S(2)}, u32[]{:S(2)}) collective-permute-start(bf16[4,80,128]{2,1,0:T(8,128)(2,1)S(1)} %shard_map.78.g0), channel_id=1, source_target_pairs={{0,24},{8,0},{16,8},{24,16},{1,25},{9,1},{17,9},{25,17},{2,26},{10... | collective-permute-start | bytes 245768 | tf_op jit(solution)/shard_map/ppermute | solution.py:322
  20.8 5.1 %collective-permute-start.5 = (bf16[4,80,128]{2,1,0:T(8,128)(2,1)S(1)}, bf16[4,80,128]{2,1,0:T(8,128)(2,1)S(1)}, u32[]{:S(2)}, u32[]{:S(2)}) collective-permute-start(bf16[4,80,128]{2,1,0:T(8,128)(2,1)S(1)} %shard_map.78.g0), channel_id=1, source_target_pairs={{0,16},{8,24},{16,0},{24,8},{1,17},{9,25},{17,1},{25,9},{2,18},{10... | collective-permute-start | bytes 245768 | tf_op jit(solution)/shard_map/ppermute | solution.py:322
  21.1 5.6 %collective-permute-start.4 = (bf16[4,80,128]{2,1,0:T(8,128)(2,1)S(1)}, bf16[4,80,128]{2,1,0:T(8,128)(2,1)S(1)}, u32[]{:S(2)}, u32[]{:S(2)}) collective-permute-start(bf16[4,80,128]{2,1,0:T(8,128)(2,1)S(1)} %shard_map.78.g0), channel_id=1, source_target_pairs={{0,8},{8,16},{16,24},{24,0},{1,9},{9,17},{17,25},{25,1},{2,10},{10... | collective-permute-start | bytes 245768 | tf_op jit(solution)/shard_map/ppermute | solution.py:322
  33.2 65.1 %copy-start = (bf16[64,128]{1,0:T(8,128)(2,1)S(1)}, bf16[64,128]{1,0:T(8,128)(2,1)}, u32[]{:S(2)}) copy-start(bf16[64,128]{1,0:T(8,128)(2,1)} %src_ref.1) | copy-start | bytes 49156
  33.2 65.0 %copy-start.1 = (bf16[64,128]{1,0:T(8,128)(2,1)S(1)}, bf16[64,128]{1,0:T(8,128)(2,1)}, u32[]{:S(2)}) copy-start(bf16[64,128]{1,0:T(8,128)(2,1)} %tgt_ref.1) | copy-start | bytes 49156

commit v6 on v5

--- a/solution.py
+++ b/solution.py
@@ -88,23 +88,16 @@
     return join3(block, 70 if first else 73)
 
 
-def encode_kernel(src, tgt, other, src_dual, src_cot, tgt_dual, tgt_cot, own, out):
+def encode_kernel(src, tgt, src_dual, src_cot, tgt_dual, tgt_cot, own, out):
     at = lax.axis_index("y") * 8 + lax.axis_index("z")
     own[...] = encode(src[...], src_dual[pl.ds(at, 1), :], src_cot[pl.ds(at, 1), :], True)
-    at = lax.axis_index("x") * 2
-    flip = lax.axis_index("c") == 0
-    near = tgt[...].astype(f32)
-    far = other[...].astype(f32)
-    low = jnp.where(flip, near, far).astype(bf16)
-    high = jnp.where(flip, far, near).astype(bf16)
-    both = jnp.concatenate(
-        [
-            encode(low, tgt_dual[pl.ds(at, 1), :], tgt_cot[pl.ds(at, 1), :], False),
-            encode(high, tgt_dual[pl.ds(at + 1, 1), :], tgt_cot[pl.ds(at + 1, 1), :], False),
-        ],
-        axis=0,
-    )
-    out[...] = jnp.broadcast_to(both[None], out.shape)
+    at = lax.axis_index("x") * 2 + lax.axis_index("c")
+    one = encode(tgt[...], tgt_dual[pl.ds(at, 1), :], tgt_cot[pl.ds(at, 1), :], False)
+    out[...] = jnp.broadcast_to(one[None], out.shape)
+
+
+def tgt_slot(k):
+    return (k % 2) * NZ + k // 2
 
 
 def stack_kernel(a, b, c, d, out):
@@ -129,7 +122,7 @@
         xt[sl, :] = turned
         bub[sl, :] = jnp.dot(turned, pick, preferred_element_type=f32)
         cots[k : k + 1, :] = cot_of(block, True)
-        other = yg[k]
+        other = yg[tgt_slot(k)]
         ya[:, sl] = jnp.concatenate([other, pad.astype(bf16)], axis=0)
         c = cot_of(other, False)
         cots[NA + k : NA + k + 1, :] = c
@@ -221,7 +214,7 @@
     for k in range(NA):
         stack_side(ax, slice(k * L, (k + 1) * L), xs[k], bu[k : k + 1], ru[k : k + 1])
     for k in range(NB):
-        stack_side(ay, slice(k * L, (k + 1) * L), yg[k], bv[k : k + 1], rv[k : k + 1])
+        stack_side(ay, slice(k * L, (k + 1) * L), yg[tgt_slot(k)], bv[k : k + 1], rv[k : k + 1])
     flip = lax.axis_index("c") == 0
     quad = jnp.zeros((1, L), f32)
     tails = []
@@ -322,20 +315,15 @@
     return lax.ppermute(v, axis, [(i, (i + k) % n) for i in range(n)])
 
 
-def swap(v):
-    return shift(v, "c", 2, 1)
-
-
 def pair(v):
     return lax.all_gather(v, "c", axis=0, tiled=False)
 
 
 def body(src_points, tgt_points, src_dual, tgt_dual, src_cot, tgt_cot):
     whole = lambda v: v.reshape(-1, L)
-    own, send = call(encode_kernel, (sds((KP, L), bf16), sds((NZ, 2 * KP, L), bf16)), limit=WIDE)(
+    own, send = call(encode_kernel, (sds((KP, L), bf16), sds((NZ, KP, L), bf16)), limit=WIDE)(
         src_points,
         tgt_points,
-        swap(tgt_points),
         whole(src_dual),
         whole(src_cot),
         whole(tgt_dual),
@@ -344,7 +332,7 @@
     g0 = call(stack_kernel, sds((4, KP, L), bf16), flops=10000000000)(
         own, *[shift(own, "x", 4, k) for k in (1, 2, 3)]
     )
-    yg = exchange(send, "z").reshape(NB, KP, L)
+    yg = pair(exchange(send, "z")).reshape(NB, KP, L)
     g1, g2, g3 = [shift(g0, "y", 4, k) for k in (1, 2, 3)]
     unit = ROWS * COLS * 2
     vm = pltpu.VMEM

time: 100 us -> 97.9 us (0.979)
  waiting for transfers between devices: 7.64 us -> 3.79 us
  blocking collectives: 60 us -> 63.2 us
    ppermute x7 -> x6, waiting for transfers between devices: 5.98 us -> 0.02 us  [shift(): return lax.ppermute(v, axis, [(i, (i + k) % n) for i in range(n)])]
    all_to_all x1, waiting for transfers between devices: 1.66 us -> 3.78 us  [exchange(): return lax.all_to_all(v, axes, 0, 0, tiled=True)]
    all_gather x2 -> x3, blocking collectives: 9.54 us -> 11.4 us  [pair(): return lax.all_gather(v, 'c', axis=0, tiled=False)]
    all_to_all x4, blocking collectives: 50.5 us -> 51.7 us  [exchange(): return lax.all_to_all(v, axes, 0, 0, tiled=True)]
    ppermute x7 -> x6, starting transfers between devices: 8.97 us -> 8.21 us  [shift(): return lax.ppermute(v, axis, [(i, (i + k) % n) for i in range(n)])]
  transfers between devices with their start and end apart: 8 -> 7, of which waited for: 5 -> 1; matrix products, arithmetic and copies ran while one was open for 0% -> 0% of each run, Pallas kernels for 0% -> 0%
where the time goes in v6:
time: 97.9 us; the launch traced here: 96.8 us
  blocking collectives  63.2 us (65%)
  starting transfers between devices  16.4 us (17%)
  Pallas kernels  12 us (12%)
  waiting for transfers between devices  3.79 us (4%)
    all_to_all x4, blocking collectives, exchange(): return lax.all_to_all(v, axes, 0, 0, tiled=True)  51.7 us
    all_gather x3, blocking collectives, pair(): return lax.all_gather(v, 'c', axis=0, tiled=False)  11.4 us
    ppermute x6, starting transfers between devices, shift(): return lax.ppermute(v, axis, [(i, (i + k) % n) for i in range(n)])  8.21 us
    all_to_all x1, starting transfers between devices, exchange(): return lax.all_to_all(v, axes, 0, 0, tiled=True)  8.19 us
    pallas_call x1, Pallas kernels, body(): call(sweep_kernel, (sds((ROWS, COLS), bf16), sds((NA, KP, L), bf16), sds(...  4.82 us
    pallas_call x1, Pallas kernels, body(): call(step_kernel, (sds((NA, PR, L), bf16), half, half, sds((NA + NB, L),...  4.71 us
    all_to_all x1, waiting for transfers between devices, exchange(): return lax.all_to_all(v, axes, 0, 0, tiled=True)  3.78 us
  transfers between devices with their start and end apart: 7, of which 1 were waited for; matrix products, arithmetic and copies ran while one was open for 0% of the time, Pallas kernels for 0%

profile of v6, /device:TPU:1, one launch (start us, length us, event | category | flops | bytes accessed | tf_op | source)
XLA Modules:
  0.0 96.8 jit_solution(7478358292893259300)
XLA Ops:
  0.6 1.5 %shard_map.77 = (bf16[80,128]{1,0:T(8,128)(2,1)}, bf16[8,80,128]{2,1,0:T(8,128)(2,1)}) custom-call(bf16[64,128]{1,0:T(8,128)(2,1)} %src_ref.1, bf16[64,128]{1,0:T(8,128)(2,1)} %tgt_ref.1, f32[32,128]{1,0:T(8,128)} %bitcast.8, f32[32,128]{1,0:T(8,128)} %bitcast.9, f32[8,128]{1,0:T(8,128)} %bitcast.10, f32[8,128]{1,0:T(8,128)} %bitcast.11), custom_call_target="tpu_custom_call" | custom-call | bytes 1048576 | tf_op jit(solution)/shard_map/pallas_call | solution.py:324
  2.1 3.3 %collective-permute-start.2 = (bf16[80,128]{1,0:T(8,128)(2,1)}, bf16[80,128]{1,0:T(8,128)(2,1)S(1)}, u32[]{:S(2)}, u32[]{:S(2)}) collective-permute-start(bf16[80,128]{1,0:T(8,128)(2,1)} %get-tuple-element.20.a), channel_id=1, source_target_pairs={{0,192},{64,0},{128,64},{192,128},{1,193},{65,1},{129,65},{193,129... | collective-permute-start | bytes 61448 | tf_op jit(solution)/shard_map/ppermute | solution.py:315
  5.4 0.5 collective-permute-start.1
  6.0 0.6 collective-permute-start
  6.6 8.2 %all-to-all-start = ((bf16[8,80,128]{2,1,0:T(8,128)(2,1)}), bf16[8,80,128]{2,1,0:T(8,128)(2,1)S(1)}, u32[]{:S(2)}, u32[]{:S(2)}) async-start(bf16[8,80,128]{2,1,0:T(8,128)(2,1)} %get-tuple-element.21), calls=%async_computation | async-start | bytes 327680 | tf_op jit(solution)/shard_map/all_to_all | solution.py:311
  14.7 0.0 collective-permute-done.2.d
  14.8 0.0 collective-permute-done.1.c
  14.8 0.0 collective-permute-done.b
  14.8 0.0 copy-start.2
  14.8 0.7 copy-done.2
  15.5 2.7 %collective-permute-start.5 = (bf16[4,80,128]{2,1,0:T(8,128)(2,1)S(1)}, bf16[4,80,128]{2,1,0:T(8,128)(2,1)S(1)}, u32[]{:S(2)}, u32[]{:S(2)}) collective-permute-start(bf16[4,80,128]{2,1,0:T(8,128)(2,1)S(1)} %shard_map.78.g0), channel_id=1, source_target_pairs={{0,24},{8,0},{16,8},{24,16},{1,25},{9,1},{17,9},{25,17},{2,26},{10... | collective-permute-start | bytes 245768 | tf_op jit(solution)/shard_map/ppermute | solution.py:315
  18.2 0.3 collective-permute-start.4
  18.6 0.7 collective-permute-start.3
  19.3 3.8 %all-to-all-done = bf16[8,80,128]{2,1,0:T(8,128)(2,1)S(1)} async-done(((bf16[8,80,128]{2,1,0:T(8,128)(2,1)}), bf16[8,80,128]{2,1,0:T(8,128)(2,1)S(1)}, u32[]{:S(2)}, u32[]{:S(2)}) %all-to-all-start) | async-done | bytes 163872 | tf_op jit(solution)/shard_map/all_to_all | solution.py:311
  23.1 4.6 %all-gather.yg = bf16[16,80,128]{2,1,0:T(8,128)(2,1)S(1)} all-gather(bf16[8,80,128]{2,1,0:T(8,128)(2,1)S(1)} %all-to-all-done), channel_id=2, replica_groups=mesh['x'=4,'c'=2,'y'=4,'z'=8] {'c'}, dimensions={0}, use_global_device_ids=true | all-gather | bytes 491520 | tf_op jit(solution)/shard_map/all_gather | solution.py:319
  27.6 0.0 collective-permute-done.5.g3
  27.6 0.0 collective-permute-done.4.g2
  27.6 0.0 collective-permute-done.3.g1
  27.6 4.8 %shard_map.79 = (bf16[2048,2048]{1,0:T(8,128)(2,1)S(1)}, bf16[16,80,128]{2,1,0:T(8,128)(2,1)S(1)}, f32[32,128]{1,0:T(8,128)S(1)}, f32[16,128]{1,0:T(8,128)S(1)}, f32[24,128]{1,0:T(8,128)S(1)}) custom-call(bf16[4,80,128]{2,1,0:T(8,128)(2,1)S(1)} %shard_map.78.g0, bf16[4,80,128]{2,1,0:T(8,128)(2,1)S(1)} %collective-permute-done.3.g1, ...), custom_call_target="tpu_custom_call" | custom-call | flops 3355443200 | bytes 1048576 | tf_op jit(solution)/shard_map/pallas_call | solution.py:339
  32.5 0.0 copy-start
  32.5 0.0 copy-start.1
  32.5 1.8 %all-gather.1 = f32[48,128]{1,0:T(8,128)S(1)} all-gather(f32[24,128]{1,0:T(8,128)S(1)} %get-tuple-element.26), channel_id=3, replica_groups=mesh['x'=4,'c'=2,'y'=4,'z'=8] {'c'}, dimensions={0}, use_global_device_ids=true | all-gather | bytes 36864 | tf_op jit(solution)/shard_map/all_gather | solution.py:319
  34.4 12.9 %all_to_all.25.got.wu_in = f32[16,24,128]{2,1,0:T(8,128)S(1)} all-to-all(f32[16,24,128]{2,1,0:T(8,128)S(1)} %get-tuple-element.27), channel_id=1, replica_groups=mesh['x'=4,'c'=2,'y'=4,'z'=8] {'x','y'}, dimensions={0} | all-to-all | bytes 393216 | tf_op jit(solution)/shard_map/all_to_all | solution.py:311
  47.3 11.5 %all_to_all.26.wv_in = f32[8,24,128]{2,1,0:T(8,128)S(1)} all-to-all(f32[8,24,128]{2,1,0:T(8,128)S(1)} %shard_map.81), channel_id=1, replica_groups=mesh['x'=4,'c'=2,'y'=4,'z'=8] {'z'}, dimensions={0} | all-to-all | bytes 196608 | tf_op jit(solution)/shard_map/all_to_all | solution.py:311
  58.8 4.7 %shard_map.82 = (bf16[16,144,128]{2,1,0:T(8,128)(2,1)S(1)}, bf16[8,144,128]{2,1,0:T(8,128)(2,1)S(1)}, bf16[8,144,128]{2,1,0:T(8,128)(2,1)S(1)}, f32[32,128]{1,0:T(8,128)S(1)}, f32[8,128]{1,0:T(8,128)S(1)}) custom-call(bf16[2048,2048]{1,0:T(8,128)(2,1)S(1)} %get-tuple-element.22.plan, bf16[16,80,128]{2,1,0:T(8,128)(2,1)S(1)} %get-tuple-element.23.xs, ...), custom_call_target="tpu_custom_call" | custom-call | flops 2147483648 | bytes 1048576 | tf_op jit(solution)/shard_map/pallas_call | solution.py:382
  63.5 5.0 %all-gather.2 = bf16[16,144,128]{2,1,0:T(8,128)(2,1)S(1)} all-gather(bf16[8,144,128]{2,1,0:T(8,128)(2,1)S(1)} %get-tuple-element.30), channel_id=4, replica_groups=mesh['x'=4,'c'=2,'y'=4,'z'=8] {'c'}, dimensions={0}, use_global_device_ids=true | all-gather | bytes 884736 | tf_op jit(solution)/shard_map/all_gather | solution.py:319
  68.5 0.1 shard_map.83
  68.6 14.6 %all_to_all.27.got = bf16[16,144,128]{2,1,0:T(8,128)(2,1)S(1)} all-to-all(bf16[16,144,128]{2,1,0:T(8,128)(2,1)S(1)} %get-tuple-element.32), channel_id=1, replica_groups=mesh['x'=4,'c'=2,'y'=4,'z'=8] {'x','y'}, dimensions={0} | all-to-all | bytes 1179648 | tf_op jit(solution)/shard_map/all_to_all | solution.py:311
  83.2 0.1 shard_map.84
  83.3 12.8 %all_to_all.28.got = bf16[8,144,128]{2,1,0:T(8,128)(2,1)S(1)} all-to-all(bf16[8,144,128]{2,1,0:T(8,128)(2,1)S(1)} %get-tuple-element.35), channel_id=1, replica_groups=mesh['x'=4,'c'=2,'y'=4,'z'=8] {'z'}, dimensions={0} | all-to-all | bytes 589824 | tf_op jit(solution)/shard_map/all_to_all | solution.py:311
  96.1 0.0 copy-done
  96.1 0.0 copy-done.1
  96.1 0.7 shard_map.85
  (3 shorter events, 0.0 us)
Async XLA Ops:
  2.1 12.6 %collective-permute-start.2 = (bf16[80,128]{1,0:T(8,128)(2,1)}, bf16[80,128]{1,0:T(8,128)(2,1)S(1)}, u32[]{:S(2)}, u32[]{:S(2)}) collective-permute-start(bf16[80,128]{1,0:T(8,128)(2,1)} %get-tuple-element.20.a), channel_id=1, source_target_pairs={{0,192},{64,0},{128,64},{192,128},{1,193},{65,1},{129,65},{193,129... | collective-permute-start | bytes 61448 | tf_op jit(solution)/shard_map/ppermute | solution.py:315
  5.4 9.3 %collective-permute-start.1 = (bf16[80,128]{1,0:T(8,128)(2,1)}, bf16[80,128]{1,0:T(8,128)(2,1)S(1)}, u32[]{:S(2)}, u32[]{:S(2)}) collective-permute-start(bf16[80,128]{1,0:T(8,128)(2,1)} %get-tuple-element.20.a), channel_id=1, source_target_pairs={{0,128},{64,192},{128,0},{192,64},{1,129},{65,193},{129,1},{193,65... | collective-permute-start | bytes 61448 | tf_op jit(solution)/shard_map/ppermute | solution.py:315
  6.0 8.8 %collective-permute-start = (bf16[80,128]{1,0:T(8,128)(2,1)}, bf16[80,128]{1,0:T(8,128)(2,1)S(1)}, u32[]{:S(2)}, u32[]{:S(2)}) collective-permute-start(bf16[80,128]{1,0:T(8,128)(2,1)} %get-tuple-element.20.a), channel_id=1, source_target_pairs={{0,64},{64,128},{128,192},{192,0},{1,65},{65,129},{129,193},{193,1... | collective-permute-start | bytes 61448 | tf_op jit(solution)/shard_map/ppermute | solution.py:315
  6.6 16.5 %all-to-all-start = ((bf16[8,80,128]{2,1,0:T(8,128)(2,1)}), bf16[8,80,128]{2,1,0:T(8,128)(2,1)S(1)}, u32[]{:S(2)}, u32[]{:S(2)}) async-start(bf16[8,80,128]{2,1,0:T(8,128)(2,1)} %get-tuple-element.21), calls=%async_computation | async-start | bytes 327680 | tf_op jit(solution)/shard_map/all_to_all | solution.py:311
  14.8 0.7 copy-start.2
  15.5 12.1 %collective-permute-start.5 = (bf16[4,80,128]{2,1,0:T(8,128)(2,1)S(1)}, bf16[4,80,128]{2,1,0:T(8,128)(2,1)S(1)}, u32[]{:S(2)}, u32[]{:S(2)}) collective-permute-start(bf16[4,80,128]{2,1,0:T(8,128)(2,1)S(1)} %shard_map.78.g0), channel_id=1, source_target_pairs={{0,24},{8,0},{16,8},{24,16},{1,25},{9,1},{17,9},{25,17},{2,26},{10... | collective-permute-start | bytes 245768 | tf_op jit(solution)/shard_map/ppermute | solution.py:315
  18.2 9.4 %collective-permute-start.4 = (bf16[4,80,128]{2,1,0:T(8,128)(2,1)S(1)}, bf16[4,80,128]{2,1,0:T(8,128)(2,1)S(1)}, u32[]{:S(2)}, u32[]{:S(2)}) collective-permute-start(bf16[4,80,128]{2,1,0:T(8,128)(2,1)S(1)} %shard_map.78.g0), channel_id=1, source_target_pairs={{0,16},{8,24},{16,0},{24,8},{1,17},{9,25},{17,1},{25,9},{2,18},{10... | collective-permute-start | bytes 245768 | tf_op jit(solution)/shard_map/ppermute | solution.py:315
  18.6 9.0 %collective-permute-start.3 = (bf16[4,80,128]{2,1,0:T(8,128)(2,1)S(1)}, bf16[4,80,128]{2,1,0:T(8,128)(2,1)S(1)}, u32[]{:S(2)}, u32[]{:S(2)}) collective-permute-start(bf16[4,80,128]{2,1,0:T(8,128)(2,1)S(1)} %shard_map.78.g0), channel_id=1, source_target_pairs={{0,8},{8,16},{16,24},{24,0},{1,9},{9,17},{17,25},{25,1},{2,10},{10... | collective-permute-start | bytes 245768 | tf_op jit(solution)/shard_map/ppermute | solution.py:315
  32.5 63.6 %copy-start = (bf16[64,128]{1,0:T(8,128)(2,1)S(1)}, bf16[64,128]{1,0:T(8,128)(2,1)}, u32[]{:S(2)}) copy-start(bf16[64,128]{1,0:T(8,128)(2,1)} %src_ref.1) | copy-start | bytes 49156
  32.5 63.6 %copy-start.1 = (bf16[64,128]{1,0:T(8,128)(2,1)S(1)}, bf16[64,128]{1,0:T(8,128)(2,1)}, u32[]{:S(2)}) copy-start(bf16[64,128]{1,0:T(8,128)(2,1)} %tgt_ref.1) | copy-start | bytes 49156

commit v7 on v6

--- a/solution.py
+++ b/solution.py
@@ -179,7 +179,7 @@
     out[0:D, sl] = pts
     out[D : 2 * D, sl] = (wide * c).astype(bf16)
     out[2 * D : 3 * D, sl] = (wide * r).astype(bf16)
-    out[3 * D : MA, sl] = rows16([jnp.ones((1, L), f32)] + parts(r)).astype(bf16)
+    out[3 * D : MA, sl] = rows16([jnp.ones((1, L), f32)] + parts(r) + parts(r * r)).astype(bf16)
 
 
 def finish_side(piece, c, r):
@@ -188,10 +188,10 @@
     pushed = piece[3 * D + 1 : 3 * D + 2] + piece[3 * D + 2 : 3 * D + 3] + piece[3 * D + 3 : 3 * D + 4]
     t_b = c * base + piece[D : 2 * D]
     t_r = r * base + piece[2 * D : 3 * D]
-    return t_b, t_r, r * mass + pushed, pushed, mass
-
-
-def step_kernel(plan, xs, yg, cots, wu_in, wv_in, pay, mine, other, sums, scal, ax, ay):
+    return t_b, t_r, r * mass + pushed, pushed
+
+
+def left_kernel(plan, xs, cots, wu_in, wv_in, mine, other, sums, scal, ax):
     wu = wu_in[0, 0:NA]
     for k in range(1, NA):
         wu = wu + wu_in[k, 0:NA]
@@ -213,8 +213,6 @@
     rr = jnp.full((1, L), jnp.sum(ru * ru) / NA + jnp.sum(rv * rv) / NB, f32)
     for k in range(NA):
         stack_side(ax, slice(k * L, (k + 1) * L), xs[k], bu[k : k + 1], ru[k : k + 1])
-    for k in range(NB):
-        stack_side(ay, slice(k * L, (k + 1) * L), yg[tgt_slot(k)], bv[k : k + 1], rv[k : k + 1])
     flip = lax.axis_index("c") == 0
     quad = jnp.zeros((1, L), f32)
     tails = []
@@ -225,8 +223,10 @@
         for m in range(2):
             at = 2 * n + m
             r = rv[at : at + 1]
-            t_b, t_r, s_r, pushed, _ = finish_side(part[:, m * L : (m + 1) * L], bv[at : at + 1], r)
+            piece = part[:, m * L : (m + 1) * L]
+            t_b, t_r, s_r, pushed = finish_side(piece, bv[at : at + 1], r)
             quad = quad + r * (s_r + pushed)
+            quad = quad + piece[3 * D + 4 : 3 * D + 5] + piece[3 * D + 5 : 3 * D + 6] + piece[3 * D + 6 : 3 * D + 7]
             blocks.append((t_b, t_r))
             tails.append(s_r)
         (b0, r0), (b1, r1) = blocks
@@ -234,28 +234,35 @@
         mine[n, D : 2 * D] = jnp.where(flip, r0, r1).astype(bf16)
         other[n, 0:D] = jnp.where(flip, b1, b0).astype(bf16)
         other[n, D : 2 * D] = jnp.where(flip, r1, r0).astype(bf16)
+    quad = jnp.full((1, L), jnp.sum(quad), f32)
+    extra = parts(quad) + parts(rr)
+    for n in range(NZ):
+        s0, s1 = tails[2 * n], tails[2 * n + 1]
+        mine[n, 2 * D : PR] = rows16(parts(jnp.where(flip, s0, s1)) + extra).astype(bf16)
+        other[n, 2 * D : PR] = rows16(parts(jnp.where(flip, s1, s0)) + extra).astype(bf16)
+
+
+def right_kernel(plan, yg, cots, sums, scal, pay, ay):
+    alpha = scal[0:1, :]
+    bu, bv = cots[0:NA], cots[NA : NA + NB]
+    ru = bu - alpha * (sums[0:NA] + ridge_shift * bu)
+    rv = bv - alpha * (sums[NA : NA + NB] + ridge_shift * bv)
+    for k in range(NB):
+        stack_side(ay, slice(k * L, (k + 1) * L), yg[tgt_slot(k)], bv[k : k + 1], rv[k : k + 1])
+    wide = 256
     for n in range(ROWS // wide):
         part = lax.dot_general(
             ay[...], plan[n * wide : (n + 1) * wide, :], (((1,), (1,)), ((), ())), preferred_element_type=f32
         )
         for m in range(2):
             at = 2 * n + m
-            r = ru[at : at + 1]
-            t_b, t_r, s_r, _, mass = finish_side(part[:, m * L : (m + 1) * L], bu[at : at + 1], r)
-            quad = quad + r * r * mass
+            t_b, t_r, s_r, _ = finish_side(part[:, m * L : (m + 1) * L], bu[at : at + 1], ru[at : at + 1])
             pay[at, 0:D] = t_b.astype(bf16)
             pay[at, D : 2 * D] = t_r.astype(bf16)
             pay[at, 2 * D : PR] = rows16(parts(s_r)).astype(bf16)
-    quad = jnp.full((1, L), jnp.sum(quad), f32)
-    extra = parts(quad) + parts(rr)
-    for n in range(NZ):
-        s0, s1 = tails[2 * n], tails[2 * n + 1]
-        mine[n, 2 * D : PR] = rows16(parts(jnp.where(flip, s0, s1)) + extra).astype(bf16)
-        other[n, 2 * D : PR] = rows16(parts(jnp.where(flip, s1, s0)) + extra).astype(bf16)
-
-
-def join_kernel(mine, both, pay_in, pay, send):
-    got = both.at[1 - lax.axis_index("c")]
+
+
+def join_kernel(mine, got, pay_in, pay, send):
     a = mine[0, 2 * D :].astype(f32)
     b = got[0, 2 * D :].astype(f32)
     quad = join3(a, 3) + join3(b, 3)
@@ -379,20 +386,26 @@
     )(wu, wv)
     wv = exchange(send, "z")
     half = sds((NZ, PR, L), bf16)
-    pay, mine, other, sums, scal = call(
-        step_kernel,
-        (sds((NA, PR, L), bf16), half, half, sds((NA + NB, L), f32), sds((8, L), f32)),
+    mine, other, sums, scal = call(
+        left_kernel,
+        (half, half, sds((NA + NB, L), f32), sds((8, L), f32)),
         flops=unit * 256,
-        scratch_shapes=[vm((MA, ROWS), bf16), vm((MA, COLS), bf16)],
-    )(plan, xs, yg, cots, wu, wv)
+        scratch_shapes=[vm((MA, ROWS), bf16)],
+    )(plan, xs, cots, wu, wv)
+    pay = call(
+        right_kernel,
+        sds((NA, PR, L), bf16),
+        flops=unit * 256,
+        scratch_shapes=[vm((MA, COLS), bf16)],
+    )(plan, yg, cots, sums, scal)
     pay, send = call(
         join_kernel,
         (sds((NA, PR, L), bf16), half),
         grid=(1,),
-        in_specs=[full(NZ, PR, L), full(2, NZ, PR, L), tail(NA, 16, 8)],
+        in_specs=[full(NZ, PR, L), full(NZ, PR, L), tail(NA, 16, 8)],
         out_specs=(tail(NA, 16, 8), full(NZ, PR, L)),
         input_output_aliases={2: 0},
-    )(mine, pair(other), pay)
+    )(mine, shift(other, "c", 2, 1), pay)
     got_s = exchange(pay, SA)
     tot_s, send = call(
         pass_kernel,

time: 97.9 us -> 96.6 us (0.987)
  blocking collectives: 63.2 us -> 58.6 us
  starting transfers between devices: 16.4 us -> 19.8 us
    all_gather x3 -> x2, blocking collectives: 11.4 us -> 6.46 us  [pair(): return lax.all_gather(v, 'c', axis=0, tiled=False)]
    ppermute x6 -> x7, starting transfers between devices: 8.21 us -> 11.6 us  [shift(): return lax.ppermute(v, axis, [(i, (i + k) % n) for i in range(n)])]
    pallas_call x1 -> x2, Pallas kernels: 4.71 us -> 4.91 us  [the longest x1 2.79 us: body(): call(right_kernel, sds((NA, PR, L), bf16), flops=unit * 256, scratch_shap...]
  transfers between devices with their start and end apart: 7 -> 8, of which waited for: 1 -> 1; matrix products, arithmetic and copies ran while one was open for 0% -> 0% of each run, Pallas kernels for 0% -> 3%
where the time goes in v7:
time: 96.6 us; the launch traced here: 95.9 us
  blocking collectives  58.6 us (61%)
  starting transfers between devices  19.8 us (20%)
  Pallas kernels  12.2 us (13%)
  waiting for transfers between devices  3.8 us (4%)
    all_to_all x4, blocking collectives, exchange(): return lax.all_to_all(v, axes, 0, 0, tiled=True)  52.2 us
    ppermute x7, starting transfers between devices, shift(): return lax.ppermute(v, axis, [(i, (i + k) % n) for i in range(n)])  11.6 us
    all_to_all x1, starting transfers between devices, exchange(): return lax.all_to_all(v, axes, 0, 0, tiled=True)  8.19 us
    all_gather x2, blocking collectives, pair(): return lax.all_gather(v, 'c', axis=0, tiled=False)  6.46 us
    pallas_call x1, Pallas kernels, body(): call(sweep_kernel, (sds((ROWS, COLS), bf16), sds((NA, KP, L), bf16), sds(...  4.81 us
    all_to_all x1, waiting for transfers between devices, exchange(): return lax.all_to_all(v, axes, 0, 0, tiled=True)  3.78 us
    pallas_call x1, Pallas kernels, body(): call(right_kernel, sds((NA, PR, L), bf16), flops=unit * 256, scratch_shap...  2.79 us
    pallas_call x1, Pallas kernels, body(): call(left_kernel, (half, half, sds((NA + NB, L), f32), sds((8, L), f32)),...  2.12 us
  transfers between devices with their start and end apart: 8, of which 1 were waited for; matrix products, arithmetic and copies ran while one was open for 0% of the time, Pallas kernels for 3%

profile of v7, /device:TPU:1, one launch (start us, length us, event | category | flops | bytes accessed | tf_op | source)
XLA Modules:
  0.0 95.9 jit_solution(14060601551461924556)
XLA Ops:
  0.6 1.5 %shard_map.77 = (bf16[80,128]{1,0:T(8,128)(2,1)}, bf16[8,80,128]{2,1,0:T(8,128)(2,1)}) custom-call(bf16[64,128]{1,0:T(8,128)(2,1)} %src_ref.1, bf16[64,128]{1,0:T(8,128)(2,1)} %tgt_ref.1, f32[32,128]{1,0:T(8,128)} %bitcast.6, f32[32,128]{1,0:T(8,128)} %bitcast.7, f32[8,128]{1,0:T(8,128)} %bitcast.8, f32[8,128]{1,0:T(8,128)} %bitcast.9), custom_call_target="tpu_custom_call" | custom-call | bytes 1048576 | tf_op jit(solution)/shard_map/pallas_call | solution.py:331
  2.1 3.3 %collective-permute-start.2 = (bf16[80,128]{1,0:T(8,128)(2,1)}, bf16[80,128]{1,0:T(8,128)(2,1)S(1)}, u32[]{:S(2)}, u32[]{:S(2)}) collective-permute-start(bf16[80,128]{1,0:T(8,128)(2,1)} %get-tuple-element.19.a), channel_id=1, source_target_pairs={{0,192},{64,0},{128,64},{192,128},{1,193},{65,1},{129,65},{193,129... | collective-permute-start | bytes 61448 | tf_op jit(solution)/shard_map/ppermute | solution.py:322
  5.4 0.5 collective-permute-start.1
  5.9 0.6 collective-permute-start
  6.6 8.2 %all-to-all-start = ((bf16[8,80,128]{2,1,0:T(8,128)(2,1)}), bf16[8,80,128]{2,1,0:T(8,128)(2,1)S(1)}, u32[]{:S(2)}, u32[]{:S(2)}) async-start(bf16[8,80,128]{2,1,0:T(8,128)(2,1)} %get-tuple-element.20), calls=%async_computation | async-start | bytes 327680 | tf_op jit(solution)/shard_map/all_to_all | solution.py:318
  14.7 0.0 collective-permute-done.2.d
  14.7 0.0 collective-permute-done.1.c
  14.8 0.0 collective-permute-done.b
  14.8 0.0 copy-start.2
  14.8 0.7 copy-done.2
  15.5 2.7 %collective-permute-start.5 = (bf16[4,80,128]{2,1,0:T(8,128)(2,1)S(1)}, bf16[4,80,128]{2,1,0:T(8,128)(2,1)S(1)}, u32[]{:S(2)}, u32[]{:S(2)}) collective-permute-start(bf16[4,80,128]{2,1,0:T(8,128)(2,1)S(1)} %shard_map.78.g0), channel_id=1, source_target_pairs={{0,24},{8,0},{16,8},{24,16},{1,25},{9,1},{17,9},{25,17},{2,26},{10... | collective-permute-start | bytes 245768 | tf_op jit(solution)/shard_map/ppermute | solution.py:322
  18.2 0.3 collective-permute-start.4
  18.6 0.7 collective-permute-start.3
  19.3 3.8 %all-to-all-done = bf16[8,80,128]{2,1,0:T(8,128)(2,1)S(1)} async-done(((bf16[8,80,128]{2,1,0:T(8,128)(2,1)}), bf16[8,80,128]{2,1,0:T(8,128)(2,1)S(1)}, u32[]{:S(2)}, u32[]{:S(2)}) %all-to-all-start) | async-done | bytes 163872 | tf_op jit(solution)/shard_map/all_to_all | solution.py:318
  23.1 4.6 %all-gather.yg = bf16[16,80,128]{2,1,0:T(8,128)(2,1)S(1)} all-gather(bf16[8,80,128]{2,1,0:T(8,128)(2,1)S(1)} %all-to-all-done), channel_id=2, replica_groups=mesh['x'=4,'c'=2,'y'=4,'z'=8] {'c'}, dimensions={0}, use_global_device_ids=true | all-gather | bytes 491520 | tf_op jit(solution)/shard_map/all_gather | solution.py:326
  27.6 0.0 collective-permute-done.5.g3
  27.6 0.0 collective-permute-done.4.g2
  27.6 0.0 collective-permute-done.3.g1
  27.6 4.8 %shard_map.79 = (bf16[2048,2048]{1,0:T(8,128)(2,1)S(1)}, bf16[16,80,128]{2,1,0:T(8,128)(2,1)S(1)}, f32[32,128]{1,0:T(8,128)S(1)}, f32[16,128]{1,0:T(8,128)S(1)}, f32[24,128]{1,0:T(8,128)S(1)}) custom-call(bf16[4,80,128]{2,1,0:T(8,128)(2,1)S(1)} %shard_map.78.g0, bf16[4,80,128]{2,1,0:T(8,128)(2,1)S(1)} %collective-permute-done.3.g1, ...), custom_call_target="tpu_custom_call" | custom-call | flops 3355443200 | bytes 1048576 | tf_op jit(solution)/shard_map/pallas_call | solution.py:346
  32.5 1.9 %all-gather.1 = f32[48,128]{1,0:T(8,128)S(1)} all-gather(f32[24,128]{1,0:T(8,128)S(1)} %get-tuple-element.25), channel_id=3, replica_groups=mesh['x'=4,'c'=2,'y'=4,'z'=8] {'c'}, dimensions={0}, use_global_device_ids=true | all-gather | bytes 36864 | tf_op jit(solution)/shard_map/all_gather | solution.py:326
  34.4 12.9 %all_to_all.25.got.wu_in = f32[16,24,128]{2,1,0:T(8,128)S(1)} all-to-all(f32[16,24,128]{2,1,0:T(8,128)S(1)} %get-tuple-element.26), channel_id=1, replica_groups=mesh['x'=4,'c'=2,'y'=4,'z'=8] {'x','y'}, dimensions={0} | all-to-all | bytes 393216 | tf_op jit(solution)/shard_map/all_to_all | solution.py:318
  47.3 11.5 %all_to_all.26.wv_in = f32[8,24,128]{2,1,0:T(8,128)S(1)} all-to-all(f32[8,24,128]{2,1,0:T(8,128)S(1)} %shard_map.81), channel_id=1, replica_groups=mesh['x'=4,'c'=2,'y'=4,'z'=8] {'z'}, dimensions={0} | all-to-all | bytes 196608 | tf_op jit(solution)/shard_map/all_to_all | solution.py:318
  58.8 2.1 %shard_map.82 = (bf16[8,144,128]{2,1,0:T(8,128)(2,1)S(1)}, bf16[8,144,128]{2,1,0:T(8,128)(2,1)S(1)}, f32[32,128]{1,0:T(8,128)S(1)}, f32[8,128]{1,0:T(8,128)S(1)}) custom-call(bf16[2048,2048]{1,0:T(8,128)(2,1)S(1)} %get-tuple-element.21.plan, bf16[16,80,128]{2,1,0:T(8,128)(2,1)S(1)} %get-tuple-element.22.xs, f32[32,128]{1,0:T(8,128)S(1)} %get-tuple-element.23.cots, ...), custom_call_target="tpu_custom_call" | custom-call | flops 2147483648 | bytes 1048576 | tf_op jit(solution)/shard_map/pallas_call | solution.py:389
  60.9 0.0 copy-start
  60.9 0.0 copy-start.1
  60.9 3.4 %collective-permute-start.6 = (bf16[8,144,128]{2,1,0:T(8,128)(2,1)S(1)}, bf16[8,144,128]{2,1,0:T(8,128)(2,1)S(1)}, u32[]{:S(2)}, u32[]{:S(2)}) collective-permute-start(bf16[8,144,128]{2,1,0:T(8,128)(2,1)S(1)} %get-tuple-element.29), channel_id=1, source_target_pairs={{0,32},{32,0},{1,33},{33,1},{2,34},{34,2},{3,35},{35,3},{4,36},{36... | collective-permute-start | bytes 884744 | tf_op jit(solution)/shard_map/ppermute | solution.py:322
  64.3 2.8 %shard_map.83.pay_in = bf16[16,144,128]{2,1,0:T(8,128)(2,1)S(1)} custom-call(bf16[2048,2048]{1,0:T(8,128)(2,1)S(1)} %get-tuple-element.21.plan, bf16[16,80,128]{2,1,0:T(8,128)(2,1)S(1)} %all-gather.yg, f32[32,128]{1,0:T(8,128)S(1)} %get-tuple-element.23.cots, f32[32,128]{1,0:T(8,128)S(1)} %get-tuple-element.30.sums, f32[8,128]{1,0:T(8,128)S(1)} %get-tuple-element.31.scal), custom_call_target="tpu_custom_call" | custom-call | flops 2147483648 | bytes 1048576 | tf_op jit(solution)/shard_map/pallas_call | solution.py:395
  67.1 0.0 collective-permute-done.6.got
  67.1 0.1 shard_map.84
  67.3 14.9 %all_to_all.27.got = bf16[16,144,128]{2,1,0:T(8,128)(2,1)S(1)} all-to-all(bf16[16,144,128]{2,1,0:T(8,128)(2,1)S(1)} %get-tuple-element.32), channel_id=1, replica_groups=mesh['x'=4,'c'=2,'y'=4,'z'=8] {'x','y'}, dimensions={0} | all-to-all | bytes 1179648 | tf_op jit(solution)/shard_map/all_to_all | solution.py:318
  82.2 0.1 shard_map.85
  82.3 12.9 %all_to_all.28.got = bf16[8,144,128]{2,1,0:T(8,128)(2,1)S(1)} all-to-all(bf16[8,144,128]{2,1,0:T(8,128)(2,1)S(1)} %get-tuple-element.35), channel_id=1, replica_groups=mesh['x'=4,'c'=2,'y'=4,'z'=8] {'z'}, dimensions={0} | all-to-all | bytes 589824 | tf_op jit(solution)/shard_map/all_to_all | solution.py:318
  95.2 0.0 copy-done
  95.2 0.0 copy-done.1
  95.2 0.7 shard_map.86
  (3 shorter events, 0.0 us)
Async XLA Ops:
  2.1 12.6 %collective-permute-start.2 = (bf16[80,128]{1,0:T(8,128)(2,1)}, bf16[80,128]{1,0:T(8,128)(2,1)S(1)}, u32[]{:S(2)}, u32[]{:S(2)}) collective-permute-start(bf16[80,128]{1,0:T(8,128)(2,1)} %get-tuple-element.19.a), channel_id=1, source_target_pairs={{0,192},{64,0},{128,64},{192,128},{1,193},{65,1},{129,65},{193,129... | collective-permute-start | bytes 61448 | tf_op jit(solution)/shard_map/ppermute | solution.py:322
  5.4 9.3 %collective-permute-start.1 = (bf16[80,128]{1,0:T(8,128)(2,1)}, bf16[80,128]{1,0:T(8,128)(2,1)S(1)}, u32[]{:S(2)}, u32[]{:S(2)}) collective-permute-start(bf16[80,128]{1,0:T(8,128)(2,1)} %get-tuple-element.19.a), channel_id=1, source_target_pairs={{0,128},{64,192},{128,0},{192,64},{1,129},{65,193},{129,1},{193,65... | collective-permute-start | bytes 61448 | tf_op jit(solution)/shard_map/ppermute | solution.py:322
  5.9 8.8 %collective-permute-start = (bf16[80,128]{1,0:T(8,128)(2,1)}, bf16[80,128]{1,0:T(8,128)(2,1)S(1)}, u32[]{:S(2)}, u32[]{:S(2)}) collective-permute-start(bf16[80,128]{1,0:T(8,128)(2,1)} %get-tuple-element.19.a), channel_id=1, source_target_pairs={{0,64},{64,128},{128,192},{192,0},{1,65},{65,129},{129,193},{193,1... | collective-permute-start | bytes 61448 | tf_op jit(solution)/shard_map/ppermute | solution.py:322
  6.6 16.5 %all-to-all-start = ((bf16[8,80,128]{2,1,0:T(8,128)(2,1)}), bf16[8,80,128]{2,1,0:T(8,128)(2,1)S(1)}, u32[]{:S(2)}, u32[]{:S(2)}) async-start(bf16[8,80,128]{2,1,0:T(8,128)(2,1)} %get-tuple-element.20), calls=%async_computation | async-start | bytes 327680 | tf_op jit(solution)/shard_map/all_to_all | solution.py:318
  14.8 0.7 copy-start.2
  15.5 12.1 %collective-permute-start.5 = (bf16[4,80,128]{2,1,0:T(8,128)(2,1)S(1)}, bf16[4,80,128]{2,1,0:T(8,128)(2,1)S(1)}, u32[]{:S(2)}, u32[]{:S(2)}) collective-permute-start(bf16[4,80,128]{2,1,0:T(8,128)(2,1)S(1)} %shard_map.78.g0), channel_id=1, source_target_pairs={{0,24},{8,0},{16,8},{24,16},{1,25},{9,1},{17,9},{25,17},{2,26},{10... | collective-permute-start | bytes 245768 | tf_op jit(solution)/shard_map/ppermute | solution.py:322
  18.2 9.4 %collective-permute-start.4 = (bf16[4,80,128]{2,1,0:T(8,128)(2,1)S(1)}, bf16[4,80,128]{2,1,0:T(8,128)(2,1)S(1)}, u32[]{:S(2)}, u32[]{:S(2)}) collective-permute-start(bf16[4,80,128]{2,1,0:T(8,128)(2,1)S(1)} %shard_map.78.g0), channel_id=1, source_target_pairs={{0,16},{8,24},{16,0},{24,8},{1,17},{9,25},{17,1},{25,9},{2,18},{10... | collective-permute-start | bytes 245768 | tf_op jit(solution)/shard_map/ppermute | solution.py:322
  18.6 9.0 %collective-permute-start.3 = (bf16[4,80,128]{2,1,0:T(8,128)(2,1)S(1)}, bf16[4,80,128]{2,1,0:T(8,128)(2,1)S(1)}, u32[]{:S(2)}, u32[]{:S(2)}) collective-permute-start(bf16[4,80,128]{2,1,0:T(8,128)(2,1)S(1)} %shard_map.78.g0), channel_id=1, source_target_pairs={{0,8},{8,16},{16,24},{24,0},{1,9},{9,17},{17,25},{25,1},{2,10},{10... | collective-permute-start | bytes 245768 | tf_op jit(solution)/shard_map/ppermute | solution.py:322
  60.9 34.3 %copy-start = (bf16[64,128]{1,0:T(8,128)(2,1)S(1)}, bf16[64,128]{1,0:T(8,128)(2,1)}, u32[]{:S(2)}) copy-start(bf16[64,128]{1,0:T(8,128)(2,1)} %src_ref.1) | copy-start | bytes 49156
  60.9 34.3 %copy-start.1 = (bf16[64,128]{1,0:T(8,128)(2,1)S(1)}, bf16[64,128]{1,0:T(8,128)(2,1)}, u32[]{:S(2)}) copy-start(bf16[64,128]{1,0:T(8,128)(2,1)} %tgt_ref.1) | copy-start | bytes 49156
  60.9 6.2 %collective-permute-start.6 = (bf16[8,144,128]{2,1,0:T(8,128)(2,1)S(1)}, bf16[8,144,128]{2,1,0:T(8,128)(2,1)S(1)}, u32[]{:S(2)}, u32[]{:S(2)}) collective-permute-start(bf16[8,144,128]{2,1,0:T(8,128)(2,1)S(1)} %get-tuple-element.29), channel_id=1, source_target_pairs={{0,32},{32,0},{1,33},{33,1},{2,34},{34,2},{3,35},{35,3},{4,36},{36... | collective-permute-start | bytes 884744 | tf_op jit(solution)/shard_map/ppermute | solution.py:322

commit v8 on v7

--- a/solution.py
+++ b/solution.py
@@ -105,7 +105,7 @@
         out[k] = part[...]
 
 
-def sweep_kernel(g0, g1, g2, g3, yg, plan, xs, cots, wu_out, part_out, xt, ya, bub, bvb, row, col):
+def sweep_kernel(g0, g1, g2, g3, yg, plan, xs, cots, row, part_out, xt, ya, bub, bvb, col):
     mx = lax.axis_index("x")
     my = lax.axis_index("y")
     for m, g in enumerate((g0, g1, g2, g3)):
@@ -143,23 +143,24 @@
                 down = jnp.sum(mixed, axis=0)
                 col[:, sl] = down if r == 0 else col[:, sl] + down
             row[rows, :] = acc.reshape(rb, L)
-    wu = jnp.concatenate(
-        [jnp.sum(row[k * L : (k + 1) * L, :].T, axis=0, keepdims=True) for k in range(NA)], axis=0
-    )
     wv = jnp.concatenate(
         [jnp.sum(col[:, k * L : (k + 1) * L], axis=0, keepdims=True) for k in range(NB)], axis=0
     )
     bu = cots[0:NA]
     bv = cots[NA : NA + NB]
-    bw = jnp.sum(wu * bu + wv * bv)
+    bw = jnp.sum(wv * bv) + jnp.sum(row[...] * bub[...])
     bb = jnp.sum(bu * bu) / NA + jnp.sum(bv * bv) / NB
     mark = lax.broadcasted_iota(jnp.int32, (8, L), 0)
-    wu_out[...] = wu
     part_out[...] = jnp.concatenate([wv, jnp.where(mark == 0, bw, bb)], axis=0)
 
 
-def mix_kernel(wu, parts, send, own):
-    total = parts[0] + parts[1]
+def turn_kernel(row, wu):
+    for k in range(NA):
+        wu[k : k + 1, :] = jnp.sum(row[k * L : (k + 1) * L, :].T, axis=0, keepdims=True)
+
+
+def mix_kernel(wu, part, sib, send, own):
+    total = part[...] + sib[...]
     own[...] = total[0:NB]
     whole = jnp.concatenate([wu[...], total[NB:]], axis=0)
     send[...] = jnp.broadcast_to(whole[None], send.shape)
@@ -343,13 +344,13 @@
     g1, g2, g3 = [shift(g0, "y", 4, k) for k in (1, 2, 3)]
     unit = ROWS * COLS * 2
     vm = pltpu.VMEM
-    plan, xs, cots, wu, part = call(
+    plan, xs, cots, row, part = call(
         sweep_kernel,
         (
             sds((ROWS, COLS), bf16),
             sds((NA, KP, L), bf16),
             sds((NA + NB, L), f32),
-            sds((NA, L), f32),
+            sds((ROWS, L), f32),
             sds((NB + 8, L), f32),
         ),
         flops=unit * 400,
@@ -358,10 +359,10 @@
             vm((L, COLS), bf16),
             vm((ROWS, L), f32),
             vm((8, COLS), f32),
-            vm((ROWS, L), f32),
             vm((8, COLS), f32),
         ],
     )(g0, g1, g2, g3, yg)
+    wu = call(turn_kernel, sds((NA, L), f32), flops=unit * 200)(row)
 
     def tail(n, rows, at):
         return pl.BlockSpec((n, rows, L), lambda i: (0, at, 0))
@@ -373,9 +374,9 @@
         mix_kernel,
         (sds((NA, 24, L), f32), sds((NB, L), f32)),
         grid=(1,),
-        in_specs=[full(NA, L), full(2, NB + 8, L)],
+        in_specs=[full(NA, L), full(NB + 8, L), full(NB + 8, L)],
         out_specs=(full(NA, 24, L), full(NB, L)),
-    )(wu, pair(part))
+    )(wu, part, shift(part, "c", 2, 1))
     wu = exchange(send, SA)
     send = call(
         relay_kernel,

time: 96.6 us -> 96 us (level)
  blocking collectives: 58.6 us -> 56.8 us
    all_gather x2 -> x1, blocking collectives: 6.46 us -> 4.57 us  [pair(): return lax.all_gather(v, 'c', axis=0, tiled=False)]
    ppermute x7 -> x8, starting transfers between devices: 11.6 us -> 12 us  [shift(): return lax.ppermute(v, axis, [(i, (i + k) % n) for i in range(n)])]
  transfers between devices with their start and end apart: 8 -> 9, of which waited for: 1 -> 2; matrix products, arithmetic and copies ran while one was open for 0% -> 0% of each run, Pallas kernels for 3% -> 3%
where the time goes in v8:
time: 96 us; the launch traced here: 95.3 us
  blocking collectives  56.8 us (59%)
  starting transfers between devices  20.2 us (21%)
  Pallas kernels  12.5 us (13%)
  waiting for transfers between devices  4.28 us (4%)
    all_to_all x4, blocking collectives, exchange(): return lax.all_to_all(v, axes, 0, 0, tiled=True)  52.2 us
    ppermute x8, starting transfers between devices, shift(): return lax.ppermute(v, axis, [(i, (i + k) % n) for i in range(n)])  12 us
    all_to_all x1, starting transfers between devices, exchange(): return lax.all_to_all(v, axes, 0, 0, tiled=True)  8.19 us
    pallas_call x1, Pallas kernels, body(): call(sweep_kernel, (sds((ROWS, COLS), bf16), sds((NA, KP, L), bf16), sds(...  4.81 us
    all_gather x1, blocking collectives, pair(): return lax.all_gather(v, 'c', axis=0, tiled=False)  4.57 us
    all_to_all x1, waiting for transfers between devices, exchange(): return lax.all_to_all(v, axes, 0, 0, tiled=True)  3.78 us
    pallas_call x1, Pallas kernels, body(): call(right_kernel, sds((NA, PR, L), bf16), flops=unit * 256, scratch_shap...  2.79 us
    pallas_call x1, Pallas kernels, body(): call(left_kernel, (half, half, sds((NA + NB, L), f32), sds((8, L), f32)),...  2.12 us
  transfers between devices with their start and end apart: 9, of which 2 were waited for; matrix products, arithmetic and copies ran while one was open for 0% of the time, Pallas kernels for 3%

profile of v8, /device:TPU:1, one launch (start us, length us, event | category | flops | bytes accessed | tf_op | source)
XLA Modules:
  0.0 95.3 jit_solution(16310679314251364179)
XLA Ops:
  0.6 1.5 %shard_map.77 = (bf16[80,128]{1,0:T(8,128)(2,1)}, bf16[8,80,128]{2,1,0:T(8,128)(2,1)}) custom-call(bf16[64,128]{1,0:T(8,128)(2,1)} %src_ref.1, bf16[64,128]{1,0:T(8,128)(2,1)} %tgt_ref.1, f32[32,128]{1,0:T(8,128)} %bitcast.4, f32[32,128]{1,0:T(8,128)} %bitcast.5, f32[8,128]{1,0:T(8,128)} %bitcast.6, f32[8,128]{1,0:T(8,128)} %bitcast.7), custom_call_target="tpu_custom_call" | custom-call | bytes 1048576 | tf_op jit(solution)/shard_map/pallas_call | solution.py:332
  2.1 3.3 %collective-permute-start.2 = (bf16[80,128]{1,0:T(8,128)(2,1)}, bf16[80,128]{1,0:T(8,128)(2,1)S(1)}, u32[]{:S(2)}, u32[]{:S(2)}) collective-permute-start(bf16[80,128]{1,0:T(8,128)(2,1)} %get-tuple-element.19.a), channel_id=1, source_target_pairs={{0,192},{64,0},{128,64},{192,128},{1,193},{65,1},{129,65},{193,129... | collective-permute-start | bytes 61448 | tf_op jit(solution)/shard_map/ppermute | solution.py:323
  5.4 0.5 collective-permute-start.1
  5.9 0.6 collective-permute-start
  6.6 8.2 %all-to-all-start = ((bf16[8,80,128]{2,1,0:T(8,128)(2,1)}), bf16[8,80,128]{2,1,0:T(8,128)(2,1)S(1)}, u32[]{:S(2)}, u32[]{:S(2)}) async-start(bf16[8,80,128]{2,1,0:T(8,128)(2,1)} %get-tuple-element.20), calls=%async_computation | async-start | bytes 327680 | tf_op jit(solution)/shard_map/all_to_all | solution.py:319
  14.7 0.0 collective-permute-done.2.d
  14.7 0.0 collective-permute-done.1.c
  14.8 0.0 collective-permute-done.b
  14.8 0.0 copy-start.2
  14.8 0.7 copy-done.2
  15.5 2.7 %collective-permute-start.5 = (bf16[4,80,128]{2,1,0:T(8,128)(2,1)S(1)}, bf16[4,80,128]{2,1,0:T(8,128)(2,1)S(1)}, u32[]{:S(2)}, u32[]{:S(2)}) collective-permute-start(bf16[4,80,128]{2,1,0:T(8,128)(2,1)S(1)} %shard_map.78.g0), channel_id=1, source_target_pairs={{0,24},{8,0},{16,8},{24,16},{1,25},{9,1},{17,9},{25,17},{2,26},{10... | collective-permute-start | bytes 245768 | tf_op jit(solution)/shard_map/ppermute | solution.py:323
  18.2 0.3 collective-permute-start.4
  18.6 0.7 collective-permute-start.3
  19.3 3.8 %all-to-all-done = bf16[8,80,128]{2,1,0:T(8,128)(2,1)S(1)} async-done(((bf16[8,80,128]{2,1,0:T(8,128)(2,1)}), bf16[8,80,128]{2,1,0:T(8,128)(2,1)S(1)}, u32[]{:S(2)}, u32[]{:S(2)}) %all-to-all-start) | async-done | bytes 163872 | tf_op jit(solution)/shard_map/all_to_all | solution.py:319
  23.1 4.6 %all-gather.yg = bf16[16,80,128]{2,1,0:T(8,128)(2,1)S(1)} all-gather(bf16[8,80,128]{2,1,0:T(8,128)(2,1)S(1)} %all-to-all-done), channel_id=2, replica_groups=mesh['x'=4,'c'=2,'y'=4,'z'=8] {'c'}, dimensions={0}, use_global_device_ids=true | all-gather | bytes 491520 | tf_op jit(solution)/shard_map/all_gather | solution.py:327
  27.6 0.0 collective-permute-done.5.g3
  27.6 0.0 collective-permute-done.4.g2
  27.6 0.0 collective-permute-done.3.g1
  27.6 4.8 %shard_map.79 = (bf16[2048,2048]{1,0:T(8,128)(2,1)S(1)}, bf16[16,80,128]{2,1,0:T(8,128)(2,1)S(1)}, f32[32,128]{1,0:T(8,128)S(1)}, f32[2048,128]{1,0:T(8,128)S(1)}, f32[24,128]{1,0:T(8,128)S(1)}) custom-call(bf16[4,80,128]{2,1,0:T(8,128)(2,1)S(1)} %shard_map.78.g0, bf16[4,80,128]{2,1,0:T(8,128)(2,1)S(1)} %collective-permute-done.3.g1, ...), custom_call_target="tpu_custom_call" | custom-call | flops 3355443200 | bytes 1048576 | tf_op jit(solution)/shard_map/pallas_call | solution.py:347
  32.5 0.4 collective-permute-start.6
  32.9 0.3 shard_map.80.wu
  33.2 0.5 collective-permute-done.6.sib
  33.7 12.9 %all_to_all.25.got.wu_in = f32[16,24,128]{2,1,0:T(8,128)S(1)} all-to-all(f32[16,24,128]{2,1,0:T(8,128)S(1)} %get-tuple-element.26), channel_id=1, replica_groups=mesh['x'=4,'c'=2,'y'=4,'z'=8] {'x','y'}, dimensions={0} | all-to-all | bytes 393216 | tf_op jit(solution)/shard_map/all_to_all | solution.py:319
  46.7 11.5 %all_to_all.26.wv_in = f32[8,24,128]{2,1,0:T(8,128)S(1)} all-to-all(f32[8,24,128]{2,1,0:T(8,128)S(1)} %shard_map.82), channel_id=1, replica_groups=mesh['x'=4,'c'=2,'y'=4,'z'=8] {'z'}, dimensions={0} | all-to-all | bytes 196608 | tf_op jit(solution)/shard_map/all_to_all | solution.py:319
  58.2 2.1 %shard_map.83 = (bf16[8,144,128]{2,1,0:T(8,128)(2,1)S(1)}, bf16[8,144,128]{2,1,0:T(8,128)(2,1)S(1)}, f32[32,128]{1,0:T(8,128)S(1)}, f32[8,128]{1,0:T(8,128)S(1)}) custom-call(bf16[2048,2048]{1,0:T(8,128)(2,1)S(1)} %get-tuple-element.21.plan, bf16[16,80,128]{2,1,0:T(8,128)(2,1)S(1)} %get-tuple-element.22.xs, f32[32,128]{1,0:T(8,128)S(1)} %get-tuple-element.23.cots, ...), custom_call_target="tpu_custom_call" | custom-call | flops 2147483648 | bytes 1048576 | tf_op jit(solution)/shard_map/pallas_call | solution.py:390
  60.3 0.0 copy-start
  60.3 0.0 copy-start.1
  60.3 3.4 %collective-permute-start.7 = (bf16[8,144,128]{2,1,0:T(8,128)(2,1)S(1)}, bf16[8,144,128]{2,1,0:T(8,128)(2,1)S(1)}, u32[]{:S(2)}, u32[]{:S(2)}) collective-permute-start(bf16[8,144,128]{2,1,0:T(8,128)(2,1)S(1)} %get-tuple-element.29), channel_id=1, source_target_pairs={{0,32},{32,0},{1,33},{33,1},{2,34},{34,2},{3,35},{35,3},{4,36},{36... | collective-permute-start | bytes 884744 | tf_op jit(solution)/shard_map/ppermute | solution.py:323
  63.7 2.8 %shard_map.84.pay_in = bf16[16,144,128]{2,1,0:T(8,128)(2,1)S(1)} custom-call(bf16[2048,2048]{1,0:T(8,128)(2,1)S(1)} %get-tuple-element.21.plan, bf16[16,80,128]{2,1,0:T(8,128)(2,1)S(1)} %all-gather.yg, f32[32,128]{1,0:T(8,128)S(1)} %get-tuple-element.23.cots, f32[32,128]{1,0:T(8,128)S(1)} %get-tuple-element.30.sums, f32[8,128]{1,0:T(8,128)S(1)} %get-tuple-element.31.scal), custom_call_target="tpu_custom_call" | custom-call | flops 2147483648 | bytes 1048576 | tf_op jit(solution)/shard_map/pallas_call | solution.py:396
  66.5 0.0 collective-permute-done.7.got
  66.5 0.1 shard_map.85
  66.6 14.9 %all_to_all.27.got = bf16[16,144,128]{2,1,0:T(8,128)(2,1)S(1)} all-to-all(bf16[16,144,128]{2,1,0:T(8,128)(2,1)S(1)} %get-tuple-element.32), channel_id=1, replica_groups=mesh['x'=4,'c'=2,'y'=4,'z'=8] {'x','y'}, dimensions={0} | all-to-all | bytes 1179648 | tf_op jit(solution)/shard_map/all_to_all | solution.py:319
  81.6 0.1 shard_map.86
  81.7 12.9 %all_to_all.28.got = bf16[8,144,128]{2,1,0:T(8,128)(2,1)S(1)} all-to-all(bf16[8,144,128]{2,1,0:T(8,128)(2,1)S(1)} %get-tuple-element.35), channel_id=1, replica_groups=mesh['x'=4,'c'=2,'y'=4,'z'=8] {'z'}, dimensions={0} | all-to-all | bytes 589824 | tf_op jit(solution)/shard_map/all_to_all | solution.py:319
  94.6 0.0 copy-done
  94.6 0.0 copy-done.1
  94.6 0.7 shard_map.87
  (3 shorter events, 0.0 us)
Async XLA Ops:
  2.1 12.6 %collective-permute-start.2 = (bf16[80,128]{1,0:T(8,128)(2,1)}, bf16[80,128]{1,0:T(8,128)(2,1)S(1)}, u32[]{:S(2)}, u32[]{:S(2)}) collective-permute-start(bf16[80,128]{1,0:T(8,128)(2,1)} %get-tuple-element.19.a), channel_id=1, source_target_pairs={{0,192},{64,0},{128,64},{192,128},{1,193},{65,1},{129,65},{193,129... | collective-permute-start | bytes 61448 | tf_op jit(solution)/shard_map/ppermute | solution.py:323
  5.4 9.3 %collective-permute-start.1 = (bf16[80,128]{1,0:T(8,128)(2,1)}, bf16[80,128]{1,0:T(8,128)(2,1)S(1)}, u32[]{:S(2)}, u32[]{:S(2)}) collective-permute-start(bf16[80,128]{1,0:T(8,128)(2,1)} %get-tuple-element.19.a), channel_id=1, source_target_pairs={{0,128},{64,192},{128,0},{192,64},{1,129},{65,193},{129,1},{193,65... | collective-permute-start | bytes 61448 | tf_op jit(solution)/shard_map/ppermute | solution.py:323
  5.9 8.8 %collective-permute-start = (bf16[80,128]{1,0:T(8,128)(2,1)}, bf16[80,128]{1,0:T(8,128)(2,1)S(1)}, u32[]{:S(2)}, u32[]{:S(2)}) collective-permute-start(bf16[80,128]{1,0:T(8,128)(2,1)} %get-tuple-element.19.a), channel_id=1, source_target_pairs={{0,64},{64,128},{128,192},{192,0},{1,65},{65,129},{129,193},{193,1... | collective-permute-start | bytes 61448 | tf_op jit(solution)/shard_map/ppermute | solution.py:323
  6.6 16.5 %all-to-all-start = ((bf16[8,80,128]{2,1,0:T(8,128)(2,1)}), bf16[8,80,128]{2,1,0:T(8,128)(2,1)S(1)}, u32[]{:S(2)}, u32[]{:S(2)}) async-start(bf16[8,80,128]{2,1,0:T(8,128)(2,1)} %get-tuple-element.20), calls=%async_computation | async-start | bytes 327680 | tf_op jit(solution)/shard_map/all_to_all | solution.py:319
  14.8 0.7 copy-start.2
  15.5 12.1 %collective-permute-start.5 = (bf16[4,80,128]{2,1,0:T(8,128)(2,1)S(1)}, bf16[4,80,128]{2,1,0:T(8,128)(2,1)S(1)}, u32[]{:S(2)}, u32[]{:S(2)}) collective-permute-start(bf16[4,80,128]{2,1,0:T(8,128)(2,1)S(1)} %shard_map.78.g0), channel_id=1, source_target_pairs={{0,24},{8,0},{16,8},{24,16},{1,25},{9,1},{17,9},{25,17},{2,26},{10... | collective-permute-start | bytes 245768 | tf_op jit(solution)/shard_map/ppermute | solution.py:323
  18.2 9.4 %collective-permute-start.4 = (bf16[4,80,128]{2,1,0:T(8,128)(2,1)S(1)}, bf16[4,80,128]{2,1,0:T(8,128)(2,1)S(1)}, u32[]{:S(2)}, u32[]{:S(2)}) collective-permute-start(bf16[4,80,128]{2,1,0:T(8,128)(2,1)S(1)} %shard_map.78.g0), channel_id=1, source_target_pairs={{0,16},{8,24},{16,0},{24,8},{1,17},{9,25},{17,1},{25,9},{2,18},{10... | collective-permute-start | bytes 245768 | tf_op jit(solution)/shard_map/ppermute | solution.py:323
  18.6 9.0 %collective-permute-start.3 = (bf16[4,80,128]{2,1,0:T(8,128)(2,1)S(1)}, bf16[4,80,128]{2,1,0:T(8,128)(2,1)S(1)}, u32[]{:S(2)}, u32[]{:S(2)}) collective-permute-start(bf16[4,80,128]{2,1,0:T(8,128)(2,1)S(1)} %shard_map.78.g0), channel_id=1, source_target_pairs={{0,8},{8,16},{16,24},{24,0},{1,9},{9,17},{17,25},{25,1},{2,10},{10... | collective-permute-start | bytes 245768 | tf_op jit(solution)/shard_map/ppermute | solution.py:323
  32.5 1.3 %collective-permute-start.6 = (f32[24,128]{1,0:T(8,128)S(1)}, f32[24,128]{1,0:T(8,128)S(1)}, u32[]{:S(2)}, u32[]{:S(2)}) collective-permute-start(f32[24,128]{1,0:T(8,128)S(1)} %get-tuple-element.25.part), channel_id=1, source_target_pairs={{0,32},{32,0},{1,33},{33,1},{2,34},{34,2},{3,35},{35,3},{4,36},{36... | collective-permute-start | bytes 36872 | tf_op jit(solution)/shard_map/ppermute | solution.py:323
  60.3 34.3 %copy-start = (bf16[64,128]{1,0:T(8,128)(2,1)S(1)}, bf16[64,128]{1,0:T(8,128)(2,1)}, u32[]{:S(2)}) copy-start(bf16[64,128]{1,0:T(8,128)(2,1)} %src_ref.1) | copy-start | bytes 49156
  60.3 34.3 %copy-start.1 = (bf16[64,128]{1,0:T(8,128)(2,1)S(1)}, bf16[64,128]{1,0:T(8,128)(2,1)}, u32[]{:S(2)}) copy-start(bf16[64,128]{1,0:T(8,128)(2,1)} %tgt_ref.1) | copy-start | bytes 49156
  60.3 6.2 %collective-permute-start.7 = (bf16[8,144,128]{2,1,0:T(8,128)(2,1)S(1)}, bf16[8,144,128]{2,1,0:T(8,128)(2,1)S(1)}, u32[]{:S(2)}, u32[]{:S(2)}) collective-permute-start(bf16[8,144,128]{2,1,0:T(8,128)(2,1)S(1)} %get-tuple-element.29), channel_id=1, source_target_pairs={{0,32},{32,0},{1,33},{33,1},{2,34},{34,2},{3,35},{35,3},{4,36},{36... | collective-permute-start | bytes 884744 | tf_op jit(solution)/shard_map/ppermute | solution.py:323

commit v9 on v8

--- a/solution.py
+++ b/solution.py
@@ -154,8 +154,15 @@
     part_out[...] = jnp.concatenate([wv, jnp.where(mark == 0, bw, bb)], axis=0)
 
 
-def turn_kernel(row, wu):
+def turn_kernel(row, xs, yg, cots, wu, xb, yb):
     for k in range(NA):
+        sl = slice(k * L, (k + 1) * L)
+        for out, block, c in (
+            (xb, xs[k], cots[k : k + 1, :]),
+            (yb, yg[tgt_slot(k)], cots[NA + k : NA + k + 1, :]),
+        ):
+            out[0:D, sl] = block[0:D]
+            out[D : 2 * D, sl] = (block[0:D].astype(f32) * c).astype(bf16)
         wu[k : k + 1, :] = jnp.sum(row[k * L : (k + 1) * L, :].T, axis=0, keepdims=True)
 
 
@@ -174,11 +181,9 @@
     send[...] = jnp.broadcast_to(whole[None], send.shape)
 
 
-def stack_side(out, sl, block, c, r):
+def stack_side(out, sl, block, r):
     pts = block[0:D]
     wide = pts.astype(f32)
-    out[0:D, sl] = pts
-    out[D : 2 * D, sl] = (wide * c).astype(bf16)
     out[2 * D : 3 * D, sl] = (wide * r).astype(bf16)
     out[3 * D : MA, sl] = rows16([jnp.ones((1, L), f32)] + parts(r) + parts(r * r)).astype(bf16)
 
@@ -192,7 +197,8 @@
     return t_b, t_r, r * mass + pushed, pushed
 
 
-def left_kernel(plan, xs, cots, wu_in, wv_in, mine, other, sums, scal, ax):
+def left_kernel(plan, xs, xb, cots, wu_in, wv_in, mine, other, sums, scal, ax):
+    ax[0 : 2 * D, :] = xb[...]
     wu = wu_in[0, 0:NA]
     for k in range(1, NA):
         wu = wu + wu_in[k, 0:NA]
@@ -213,7 +219,7 @@
     rv = bv - alpha * (wv + ridge_shift * bv)
     rr = jnp.full((1, L), jnp.sum(ru * ru) / NA + jnp.sum(rv * rv) / NB, f32)
     for k in range(NA):
-        stack_side(ax, slice(k * L, (k + 1) * L), xs[k], bu[k : k + 1], ru[k : k + 1])
+        stack_side(ax, slice(k * L, (k + 1) * L), xs[k], ru[k : k + 1])
     flip = lax.axis_index("c") == 0
     quad = jnp.zeros((1, L), f32)
     tails = []
@@ -243,13 +249,14 @@
         other[n, 2 * D : PR] = rows16(parts(jnp.where(flip, s1, s0)) + extra).astype(bf16)
 
 
-def right_kernel(plan, yg, cots, sums, scal, pay, ay):
+def right_kernel(plan, yg, yb, cots, sums, scal, pay, ay):
+    ay[0 : 2 * D, :] = yb[...]
     alpha = scal[0:1, :]
     bu, bv = cots[0:NA], cots[NA : NA + NB]
     ru = bu - alpha * (sums[0:NA] + ridge_shift * bu)
     rv = bv - alpha * (sums[NA : NA + NB] + ridge_shift * bv)
     for k in range(NB):
-        stack_side(ay, slice(k * L, (k + 1) * L), yg[tgt_slot(k)], bv[k : k + 1], rv[k : k + 1])
+        stack_side(ay, slice(k * L, (k + 1) * L), yg[tgt_slot(k)], rv[k : k + 1])
     wide = 256
     for n in range(ROWS // wide):
         part = lax.dot_general(
@@ -362,7 +369,11 @@
             vm((8, COLS), f32),
         ],
     )(g0, g1, g2, g3, yg)
-    wu = call(turn_kernel, sds((NA, L), f32), flops=unit * 200)(row)
+    wu, xb, yb = call(
+        turn_kernel,
+        (sds((NA, L), f32), sds((2 * D, ROWS), bf16), sds((2 * D, COLS), bf16)),
+        flops=unit * 200,
+    )(row, xs, yg, cots)
 
     def tail(n, rows, at):
         return pl.BlockSpec((n, rows, L), lambda i: (0, at, 0))
@@ -392,13 +403,13 @@
         (half, half, sds((NA + NB, L), f32), sds((8, L), f32)),
         flops=unit * 256,
         scratch_shapes=[vm((MA, ROWS), bf16)],
-    )(plan, xs, cots, wu, wv)
+    )(plan, xs, xb, cots, wu, wv)
     pay = call(
         right_kernel,
         sds((NA, PR, L), bf16),
         flops=unit * 256,
         scratch_shapes=[vm((MA, COLS), bf16)],
-    )(plan, yg, cots, sums, scal)
+    )(plan, yg, yb, cots, sums, scal)
     pay, send = call(
         join_kernel,
         (sds((NA, PR, L), bf16), half),

time: 96 us -> 95.9 us (level)
  no operation moved by 1% of the time
where the time goes in v9:
time: 95.9 us; the launch traced here: 95.2 us
  blocking collectives  56.8 us (59%)
  starting transfers between devices  20.2 us (21%)
  Pallas kernels  12.5 us (13%)
  waiting for transfers between devices  4.15 us (4%)
    all_to_all x4, blocking collectives, exchange(): return lax.all_to_all(v, axes, 0, 0, tiled=True)  52.2 us
    ppermute x8, starting transfers between devices, shift(): return lax.ppermute(v, axis, [(i, (i + k) % n) for i in range(n)])  12 us
    all_to_all x1, starting transfers between devices, exchange(): return lax.all_to_all(v, axes, 0, 0, tiled=True)  8.19 us
    pallas_call x1, Pallas kernels, body(): call(sweep_kernel, (sds((ROWS, COLS), bf16), sds((NA, KP, L), bf16), sds(...  4.76 us
    all_gather x1, blocking collectives, pair(): return lax.all_gather(v, 'c', axis=0, tiled=False)  4.57 us
    all_to_all x1, waiting for transfers between devices, exchange(): return lax.all_to_all(v, axes, 0, 0, tiled=True)  3.78 us
    pallas_call x1, Pallas kernels, body(): call(right_kernel, sds((NA, PR, L), bf16), flops=unit * 256, scratch_shap...  2.78 us
    pallas_call x1, Pallas kernels, body(): call(left_kernel, (half, half, sds((NA + NB, L), f32), sds((8, L), f32)),...  2.12 us
  transfers between devices with their start and end apart: 9, of which 2 were waited for; matrix products, arithmetic and copies ran while one was open for 0% of the time, Pallas kernels for 3%

profile of v9, /device:TPU:1, one launch (start us, length us, event | category | flops | bytes accessed | tf_op | source)
XLA Modules:
  0.0 95.2 jit_solution(1600114710725709032)
XLA Ops:
  0.6 1.5 %shard_map.77 = (bf16[80,128]{1,0:T(8,128)(2,1)}, bf16[8,80,128]{2,1,0:T(8,128)(2,1)}) custom-call(bf16[64,128]{1,0:T(8,128)(2,1)} %src_ref.1, bf16[64,128]{1,0:T(8,128)(2,1)} %tgt_ref.1, f32[32,128]{1,0:T(8,128)} %bitcast.4, f32[32,128]{1,0:T(8,128)} %bitcast.5, f32[8,128]{1,0:T(8,128)} %bitcast.6, f32[8,128]{1,0:T(8,128)} %bitcast.7), custom_call_target="tpu_custom_call" | custom-call | bytes 1048576 | tf_op jit(solution)/shard_map/pallas_call | solution.py:339
  2.1 3.3 %collective-permute-start.2 = (bf16[80,128]{1,0:T(8,128)(2,1)}, bf16[80,128]{1,0:T(8,128)(2,1)S(1)}, u32[]{:S(2)}, u32[]{:S(2)}) collective-permute-start(bf16[80,128]{1,0:T(8,128)(2,1)} %get-tuple-element.22.a), channel_id=1, source_target_pairs={{0,192},{64,0},{128,64},{192,128},{1,193},{65,1},{129,65},{193,129... | collective-permute-start | bytes 61448 | tf_op jit(solution)/shard_map/ppermute | solution.py:330
  5.4 0.5 collective-permute-start.1
  5.9 0.6 collective-permute-start
  6.5 8.2 %all-to-all-start = ((bf16[8,80,128]{2,1,0:T(8,128)(2,1)}), bf16[8,80,128]{2,1,0:T(8,128)(2,1)S(1)}, u32[]{:S(2)}, u32[]{:S(2)}) async-start(bf16[8,80,128]{2,1,0:T(8,128)(2,1)} %get-tuple-element.23), calls=%async_computation | async-start | bytes 327680 | tf_op jit(solution)/shard_map/all_to_all | solution.py:326
  14.7 0.0 collective-permute-done.2.d
  14.7 0.0 collective-permute-done.1.c
  14.7 0.0 collective-permute-done.b
  14.7 0.0 copy-start.2
  14.8 0.7 copy-done.2
  15.5 2.7 %collective-permute-start.5 = (bf16[4,80,128]{2,1,0:T(8,128)(2,1)S(1)}, bf16[4,80,128]{2,1,0:T(8,128)(2,1)S(1)}, u32[]{:S(2)}, u32[]{:S(2)}) collective-permute-start(bf16[4,80,128]{2,1,0:T(8,128)(2,1)S(1)} %shard_map.78.g0), channel_id=1, source_target_pairs={{0,24},{8,0},{16,8},{24,16},{1,25},{9,1},{17,9},{25,17},{2,26},{10... | collective-permute-start | bytes 245768 | tf_op jit(solution)/shard_map/ppermute | solution.py:330
  18.2 0.3 collective-permute-start.4
  18.6 0.7 collective-permute-start.3
  19.3 3.8 %all-to-all-done = bf16[8,80,128]{2,1,0:T(8,128)(2,1)S(1)} async-done(((bf16[8,80,128]{2,1,0:T(8,128)(2,1)}), bf16[8,80,128]{2,1,0:T(8,128)(2,1)S(1)}, u32[]{:S(2)}, u32[]{:S(2)}) %all-to-all-start) | async-done | bytes 163872 | tf_op jit(solution)/shard_map/all_to_all | solution.py:326
  23.0 4.6 %all-gather.yg = bf16[16,80,128]{2,1,0:T(8,128)(2,1)S(1)} all-gather(bf16[8,80,128]{2,1,0:T(8,128)(2,1)S(1)} %all-to-all-done), channel_id=2, replica_groups=mesh['x'=4,'c'=2,'y'=4,'z'=8] {'c'}, dimensions={0}, use_global_device_ids=true | all-gather | bytes 491520 | tf_op jit(solution)/shard_map/all_gather | solution.py:334
  27.6 0.0 collective-permute-done.5.g3
  27.6 0.0 collective-permute-done.4.g2
  27.6 0.0 collective-permute-done.3.g1
  27.6 4.8 %shard_map.79 = (bf16[2048,2048]{1,0:T(8,128)(2,1)S(1)}, bf16[16,80,128]{2,1,0:T(8,128)(2,1)S(1)}, f32[32,128]{1,0:T(8,128)S(1)}, f32[2048,128]{1,0:T(8,128)S(1)}, f32[24,128]{1,0:T(8,128)S(1)}) custom-call(bf16[4,80,128]{2,1,0:T(8,128)(2,1)S(1)} %shard_map.78.g0, bf16[4,80,128]{2,1,0:T(8,128)(2,1)S(1)} %collective-permute-done.3.g1, ...), custom_call_target="tpu_custom_call" | custom-call | flops 3355443200 | bytes 1048576 | tf_op jit(solution)/shard_map/pallas_call | solution.py:354
  32.4 0.4 collective-permute-start.6
  32.8 0.5 shard_map.80
  33.3 0.4 collective-permute-done.6.sib
  33.7 12.9 %all_to_all.25.got.wu_in = f32[16,24,128]{2,1,0:T(8,128)S(1)} all-to-all(f32[16,24,128]{2,1,0:T(8,128)S(1)} %get-tuple-element.31), channel_id=1, replica_groups=mesh['x'=4,'c'=2,'y'=4,'z'=8] {'x','y'}, dimensions={0} | all-to-all | bytes 393216 | tf_op jit(solution)/shard_map/all_to_all | solution.py:326
  46.6 11.5 %all_to_all.26.wv_in = f32[8,24,128]{2,1,0:T(8,128)S(1)} all-to-all(f32[8,24,128]{2,1,0:T(8,128)S(1)} %shard_map.82), channel_id=1, replica_groups=mesh['x'=4,'c'=2,'y'=4,'z'=8] {'z'}, dimensions={0} | all-to-all | bytes 196608 | tf_op jit(solution)/shard_map/all_to_all | solution.py:326
  58.1 2.1 %shard_map.83 = (bf16[8,144,128]{2,1,0:T(8,128)(2,1)S(1)}, bf16[8,144,128]{2,1,0:T(8,128)(2,1)S(1)}, f32[32,128]{1,0:T(8,128)S(1)}, f32[8,128]{1,0:T(8,128)S(1)}) custom-call(bf16[2048,2048]{1,0:T(8,128)(2,1)S(1)} %get-tuple-element.24.plan, bf16[16,80,128]{2,1,0:T(8,128)(2,1)S(1)} %get-tuple-element.25.xs, bf16[128,2048]{1,0:T(8,128)(2,1)S(1)} %get-tuple-element.28.xb, ...), custom_call_target="tpu_custom_call" | custom-call | flops 2147483648 | bytes 1048576 | tf_op jit(solution)/shard_map/pallas_call | solution.py:401
  60.2 0.0 copy-start
  60.3 0.0 copy-start.1
  60.3 3.4 %collective-permute-start.7 = (bf16[8,144,128]{2,1,0:T(8,128)(2,1)S(1)}, bf16[8,144,128]{2,1,0:T(8,128)(2,1)S(1)}, u32[]{:S(2)}, u32[]{:S(2)}) collective-permute-start(bf16[8,144,128]{2,1,0:T(8,128)(2,1)S(1)} %get-tuple-element.34), channel_id=1, source_target_pairs={{0,32},{32,0},{1,33},{33,1},{2,34},{34,2},{3,35},{35,3},{4,36},{36... | collective-permute-start | bytes 884744 | tf_op jit(solution)/shard_map/ppermute | solution.py:330
  63.7 2.8 %shard_map.84.pay_in = bf16[16,144,128]{2,1,0:T(8,128)(2,1)S(1)} custom-call(bf16[2048,2048]{1,0:T(8,128)(2,1)S(1)} %get-tuple-element.24.plan, bf16[16,80,128]{2,1,0:T(8,128)(2,1)S(1)} %all-gather.yg, bf16[128,2048]{1,0:T(8,128)(2,1)S(1)} %get-tuple-element.35.yb, f32[32,128]{1,0:T(8,128)S(1)} %get-tuple-element.27.cots, ...), custom_call_target="tpu_custom_call" | custom-call | flops 2147483648 | bytes 1048576 | tf_op jit(solution)/shard_map/pallas_call | solution.py:407
  66.5 0.0 collective-permute-done.7.got
  66.5 0.1 shard_map.85
  66.6 14.9 %all_to_all.27.got = bf16[16,144,128]{2,1,0:T(8,128)(2,1)S(1)} all-to-all(bf16[16,144,128]{2,1,0:T(8,128)(2,1)S(1)} %get-tuple-element.38), channel_id=1, replica_groups=mesh['x'=4,'c'=2,'y'=4,'z'=8] {'x','y'}, dimensions={0} | all-to-all | bytes 1179648 | tf_op jit(solution)/shard_map/all_to_all | solution.py:326
  81.5 0.1 shard_map.86
  81.6 12.9 %all_to_all.28.got = bf16[8,144,128]{2,1,0:T(8,128)(2,1)S(1)} all-to-all(bf16[8,144,128]{2,1,0:T(8,128)(2,1)S(1)} %get-tuple-element.41), channel_id=1, replica_groups=mesh['x'=4,'c'=2,'y'=4,'z'=8] {'z'}, dimensions={0} | all-to-all | bytes 589824 | tf_op jit(solution)/shard_map/all_to_all | solution.py:326
  94.5 0.0 copy-done
  94.5 0.0 copy-done.1
  94.5 0.7 shard_map.87
  (3 shorter events, 0.0 us)
Async XLA Ops:
  2.1 12.6 %collective-permute-start.2 = (bf16[80,128]{1,0:T(8,128)(2,1)}, bf16[80,128]{1,0:T(8,128)(2,1)S(1)}, u32[]{:S(2)}, u32[]{:S(2)}) collective-permute-start(bf16[80,128]{1,0:T(8,128)(2,1)} %get-tuple-element.22.a), channel_id=1, source_target_pairs={{0,192},{64,0},{128,64},{192,128},{1,193},{65,1},{129,65},{193,129... | collective-permute-start | bytes 61448 | tf_op jit(solution)/shard_map/ppermute | solution.py:330
  5.4 9.3 %collective-permute-start.1 = (bf16[80,128]{1,0:T(8,128)(2,1)}, bf16[80,128]{1,0:T(8,128)(2,1)S(1)}, u32[]{:S(2)}, u32[]{:S(2)}) collective-permute-start(bf16[80,128]{1,0:T(8,128)(2,1)} %get-tuple-element.22.a), channel_id=1, source_target_pairs={{0,128},{64,192},{128,0},{192,64},{1,129},{65,193},{129,1},{193,65... | collective-permute-start | bytes 61448 | tf_op jit(solution)/shard_map/ppermute | solution.py:330
  5.9 8.8 %collective-permute-start = (bf16[80,128]{1,0:T(8,128)(2,1)}, bf16[80,128]{1,0:T(8,128)(2,1)S(1)}, u32[]{:S(2)}, u32[]{:S(2)}) collective-permute-start(bf16[80,128]{1,0:T(8,128)(2,1)} %get-tuple-element.22.a), channel_id=1, source_target_pairs={{0,64},{64,128},{128,192},{192,0},{1,65},{65,129},{129,193},{193,1... | collective-permute-start | bytes 61448 | tf_op jit(solution)/shard_map/ppermute | solution.py:330
  6.5 16.5 %all-to-all-start = ((bf16[8,80,128]{2,1,0:T(8,128)(2,1)}), bf16[8,80,128]{2,1,0:T(8,128)(2,1)S(1)}, u32[]{:S(2)}, u32[]{:S(2)}) async-start(bf16[8,80,128]{2,1,0:T(8,128)(2,1)} %get-tuple-element.23), calls=%async_computation | async-start | bytes 327680 | tf_op jit(solution)/shard_map/all_to_all | solution.py:326
  14.7 0.7 copy-start.2
  15.5 12.1 %collective-permute-start.5 = (bf16[4,80,128]{2,1,0:T(8,128)(2,1)S(1)}, bf16[4,80,128]{2,1,0:T(8,128)(2,1)S(1)}, u32[]{:S(2)}, u32[]{:S(2)}) collective-permute-start(bf16[4,80,128]{2,1,0:T(8,128)(2,1)S(1)} %shard_map.78.g0), channel_id=1, source_target_pairs={{0,24},{8,0},{16,8},{24,16},{1,25},{9,1},{17,9},{25,17},{2,26},{10... | collective-permute-start | bytes 245768 | tf_op jit(solution)/shard_map/ppermute | solution.py:330
  18.2 9.4 %collective-permute-start.4 = (bf16[4,80,128]{2,1,0:T(8,128)(2,1)S(1)}, bf16[4,80,128]{2,1,0:T(8,128)(2,1)S(1)}, u32[]{:S(2)}, u32[]{:S(2)}) collective-permute-start(bf16[4,80,128]{2,1,0:T(8,128)(2,1)S(1)} %shard_map.78.g0), channel_id=1, source_target_pairs={{0,16},{8,24},{16,0},{24,8},{1,17},{9,25},{17,1},{25,9},{2,18},{10... | collective-permute-start | bytes 245768 | tf_op jit(solution)/shard_map/ppermute | solution.py:330
  18.6 9.0 %collective-permute-start.3 = (bf16[4,80,128]{2,1,0:T(8,128)(2,1)S(1)}, bf16[4,80,128]{2,1,0:T(8,128)(2,1)S(1)}, u32[]{:S(2)}, u32[]{:S(2)}) collective-permute-start(bf16[4,80,128]{2,1,0:T(8,128)(2,1)S(1)} %shard_map.78.g0), channel_id=1, source_target_pairs={{0,8},{8,16},{16,24},{24,0},{1,9},{9,17},{17,25},{25,1},{2,10},{10... | collective-permute-start | bytes 245768 | tf_op jit(solution)/shard_map/ppermute | solution.py:330
  32.4 1.3 %collective-permute-start.6 = (f32[24,128]{1,0:T(8,128)S(1)}, f32[24,128]{1,0:T(8,128)S(1)}, u32[]{:S(2)}, u32[]{:S(2)}) collective-permute-start(f32[24,128]{1,0:T(8,128)S(1)} %get-tuple-element.30.part), channel_id=1, source_target_pairs={{0,32},{32,0},{1,33},{33,1},{2,34},{34,2},{3,35},{35,3},{4,36},{36... | collective-permute-start | bytes 36872 | tf_op jit(solution)/shard_map/ppermute | solution.py:330
  60.2 34.3 %copy-start = (bf16[64,128]{1,0:T(8,128)(2,1)S(1)}, bf16[64,128]{1,0:T(8,128)(2,1)}, u32[]{:S(2)}) copy-start(bf16[64,128]{1,0:T(8,128)(2,1)} %src_ref.1) | copy-start | bytes 49156
  60.3 34.3 %copy-start.1 = (bf16[64,128]{1,0:T(8,128)(2,1)S(1)}, bf16[64,128]{1,0:T(8,128)(2,1)}, u32[]{:S(2)}) copy-start(bf16[64,128]{1,0:T(8,128)(2,1)} %tgt_ref.1) | copy-start | bytes 49156
  60.3 6.2 %collective-permute-start.7 = (bf16[8,144,128]{2,1,0:T(8,128)(2,1)S(1)}, bf16[8,144,128]{2,1,0:T(8,128)(2,1)S(1)}, u32[]{:S(2)}, u32[]{:S(2)}) collective-permute-start(bf16[8,144,128]{2,1,0:T(8,128)(2,1)S(1)} %get-tuple-element.34), channel_id=1, source_target_pairs={{0,32},{32,0},{1,33},{33,1},{2,34},{34,2},{3,35},{35,3},{4,36},{36... | collective-permute-start | bytes 884744 | tf_op jit(solution)/shard_map/ppermute | solution.py:330
